TPU v7x, 32 devices: a whole 2x2x4 slice. The times are simulated.
32 devices in a mesh: fsdp: 32 (over z, y, x, core).
Axes of the slice: x: 2, y: 2, z: 4, core: 2. Of those that a mesh axis runs over, the one named last changes fastest.
Arguments:
- tokens: bfloat16 [4096, 2048], P('fsdp'), may hold values from -6 to 6
- segments: int32 [4096], P('fsdp'), may hold values from 0 to 3, as said below
- positions: int32 [4096], P('fsdp'), may hold values from 0 to 2047
- gain_attn: bfloat16 [2048], P('fsdp'), may hold values from 0.5 to 1.5
- w_query: bfloat16 [2048, 2048], P('fsdp'), may hold values from -0.125 to 0.125
- w_key: bfloat16 [2048, 2048], P('fsdp'), may hold values from -0.125 to 0.125
- w_value: bfloat16 [2048, 2048], P('fsdp'), may hold values from -0.125 to 0.125
- w_out: bfloat16 [2048, 2048], P('fsdp'), may hold values from -0.75 to 0.75
- gain_mlp: bfloat16 [2048], P('fsdp'), may hold values from 0.5 to 1.5
- w_gate: bfloat16 [2048, 8192], P('fsdp'), may hold values from -0.125 to 0.125
- w_up: bfloat16 [2048, 8192], P('fsdp'), may hold values from -0.125 to 0.125
- w_down: bfloat16 [8192, 2048], P('fsdp'), may hold values from -0.0625 to 0.0625
- cotangent: bfloat16 [4096, 2048], P('fsdp'), may hold values from -6 to 6
Outputs:
- result: bfloat16 [4096, 2048], P('fsdp')
- grad_tokens: float32 [4096, 2048], P('fsdp')
- grad_gain_attn: float32 [2048], P('fsdp')
- grad_w_query: float32 [2048, 2048], P('fsdp')
- grad_w_key: float32 [2048, 2048], P('fsdp')
- grad_w_value: float32 [2048, 2048], P('fsdp')
- grad_w_out: float32 [2048, 2048], P('fsdp')
- grad_gain_mlp: float32 [2048], P('fsdp')
- grad_w_gate: float32 [2048, 8192], P('fsdp')
- grad_w_up: float32 [2048, 8192], P('fsdp')
- grad_w_down: float32 [8192, 2048], P('fsdp')
Inputs may be any that keep to these rules, and one draw needn't show every extreme that they name: `segments`: segment numbers never fall along the token rows and never continue across a sequence boundary; each document has 1 to 1984 tokens and one has exactly 1984.
All inputs are finite; a program needn't handle non-finite values.
Results may differ from a plain program's by a relative error of at most 0.014.
Values may be sent and summed in bfloat16 or wider, within the bound.
No kernel may reach another device: no remote copies, remote signals or barrier semaphores. Data moves between devices by JAX's collectives and lax.ppermute only.
A program may use at most 704 MiB of HBM per device.

v0:
```python
import jax
import jax.numpy as jnp
from jax import lax
from jax.sharding import PartitionSpec as P

HEADS = 32
HEAD_DIM = 64
SEQ = 2048


EPS = 1e-05
THETA = 130000.0
NEG = -1e30


def passed_along(value, axis, steps):
    count = lax.axis_size(axis)
    initial, last = (max(0, -steps), min(count, count - steps))
    return lax.ppermute(value, axis, [(source, source + steps) for source in range(initial, last)])


def norm_rows(v, gain):
    scale = lax.rsqrt(jnp.mean(v * v, axis=-1, keepdims=True) + EPS)
    return v * scale * gain


def swiglu(gate, up):
    return jax.nn.silu(gate) * up


def rotate(v, positions, sign):
    half = v.shape[-1] // 2
    freqs = THETA ** (-jnp.arange(half, dtype=jnp.float32) * 2.0 / v.shape[-1])
    angles = positions.astype(jnp.float32)[:, None] * freqs[None, :]
    cosine = jnp.cos(angles)[:, None, :]
    sine = sign * jnp.sin(angles)[:, None, :]
    first = v[..., :half]
    second = v[..., half:]
    return jnp.concatenate(
        [first * cosine - second * sine, second * cosine + first * sine], axis=-1
    )


def matmul(left, right):
    return jnp.dot(left, right, preferred_element_type=jnp.float32)


def times_t(left, right):
    return lax.dot_general(
        left, right, (((1,), (1,)), ((), ())), preferred_element_type=jnp.float32
    )


def t_times(left, right):
    return lax.dot_general(
        left, right, (((0,), (0,)), ((), ())), preferred_element_type=jnp.float32
    )


def split_heads(v, count):
    rows = v.shape[0]
    return v.reshape(rows, count, -1, HEAD_DIM).transpose(1, 0, 2, 3)


def join_heads(v):
    count, rows, group, size = v.shape
    return v.transpose(1, 0, 2, 3).reshape(rows, count * group * size)


def scores_of(query, keys, valid):
    scale = query.shape[-1] ** (-0.5)
    scores = jnp.einsum("qhd,khd->hqk", query, keys, preferred_element_type=jnp.float32) * scale
    return jnp.where(valid[None], scores, NEG)


def attend_forward(query, keys, values, valid):
    scores = scores_of(query, keys, valid)
    top = jnp.max(scores, axis=-1, keepdims=True)
    expd = jnp.where(valid[None], jnp.exp(scores - top), 0.0)
    total = jnp.sum(expd, axis=-1, keepdims=True)
    probs = (expd / total).astype(jnp.bfloat16)
    out = jnp.einsum("hqk,khd->qhd", probs, values, preferred_element_type=jnp.float32)
    return (out, top + jnp.log(total))


def attend_backward(query, keys, values, grad_out, logsum, valid):
    scale = query.shape[-1] ** (-0.5)
    scores = scores_of(query, keys, valid)
    probs = jnp.where(valid[None], jnp.exp(scores - logsum), 0.0)
    dprob = jnp.einsum("qhd,khd->hqk", grad_out, values, preferred_element_type=jnp.float32)
    delta = jnp.sum(probs * dprob, axis=-1, keepdims=True)
    dscore = (probs * (dprob - delta)).astype(jnp.bfloat16)
    dquery = jnp.einsum("hqk,khd->qhd", dscore, keys, preferred_element_type=jnp.float32) * scale
    dkeys = jnp.einsum("hqk,qhd->khd", dscore, query, preferred_element_type=jnp.float32) * scale
    dvalues = jnp.einsum(
        "hqk,qhd->khd", probs.astype(jnp.bfloat16), grad_out, preferred_element_type=jnp.float32
    )
    return (dquery, dkeys, dvalues)


def local(
    tokens,
    segments,
    positions,
    gain_attn,
    w_query,
    w_key,
    w_value,
    w_out,
    gain_mlp,
    w_gate,
    w_up,
    w_down,
    cotangent,
):
    rows = tokens.shape[0]
    reach = SEQ // rows
    index = lax.axis_index("fsdp")
    count = HEADS // min(8, HEADS)
    full_query, full_key, full_value, full_out, full_gain = (
        lax.all_gather(w_query, "fsdp", axis=0, tiled=True),
        lax.all_gather(w_key, "fsdp", axis=0, tiled=True),
        lax.all_gather(w_value, "fsdp", axis=0, tiled=True),
        lax.all_gather(w_out, "fsdp", axis=0, tiled=True),
        lax.all_gather(gain_attn, "fsdp", axis=0, tiled=True),
    )
    x = tokens.astype(jnp.float32)
    h1, norm_one_back = jax.vjp(norm_rows, x, full_gain.astype(jnp.float32))
    h1_b = h1.astype(jnp.bfloat16)
    query_b = rotate(
        matmul(h1_b, full_query).reshape(rows, HEADS, HEAD_DIM), positions, 1.0
    ).astype(jnp.bfloat16)
    key_b = rotate(matmul(h1_b, full_key).reshape(rows, HEADS, HEAD_DIM), positions, 1.0).astype(
        jnp.bfloat16
    )
    query_b = query_b.reshape(rows, -1)
    key_b = key_b.reshape(rows, -1)
    value_b = matmul(h1_b, full_value).astype(jnp.bfloat16)
    stacked = jnp.stack([key_b, value_b])
    remote = [passed_along(stacked, "fsdp", dist) for dist in range(1, reach)]
    remote_docs = [passed_along(segments, "fsdp", dist) for dist in range(1, reach)]
    earlier = [remote[dist - 1] for dist in range(reach - 1, 0, -1)] + [stacked]
    keys_all = jnp.concatenate([item[0] for item in earlier], axis=0)
    values_all = jnp.concatenate([item[1] for item in earlier], axis=0)
    key_docs = jnp.concatenate(
        [remote_docs[dist - 1] for dist in range(reach - 1, 0, -1)] + [segments], axis=0
    )
    query_rows = index * rows + jnp.arange(rows, dtype=jnp.int32)
    key_rows = (index - reach + 1) * rows + jnp.arange(reach * rows, dtype=jnp.int32)
    seq_start = index // reach * reach * rows
    valid = (
        (key_rows[None, :] >= seq_start)
        & (key_rows[None, :] >= 0)
        & (key_rows[None, :] <= query_rows[:, None])
        & (key_docs[None, :] == segments[:, None])
    )
    query_g = split_heads(query_b, count)
    keys_g = split_heads(keys_all, count)
    values_g = split_heads(values_all, count)
    out_g, logsum = lax.map(
        lambda item: attend_forward(item[0], item[1], item[2], valid), (query_g, keys_g, values_g)
    )
    out_b = join_heads(out_g).astype(jnp.bfloat16)
    x2 = x + matmul(out_b, full_out)
    full_gate, full_up, full_down, full_gain2 = (
        lax.all_gather(w_gate, "fsdp", axis=0, tiled=True),
        lax.all_gather(w_up, "fsdp", axis=0, tiled=True),
        lax.all_gather(w_down, "fsdp", axis=0, tiled=True),
        lax.all_gather(gain_mlp, "fsdp", axis=0, tiled=True),
    )
    h2, norm_two_back = jax.vjp(norm_rows, x2, full_gain2.astype(jnp.float32))
    h2_b = h2.astype(jnp.bfloat16)
    gate = matmul(h2_b, full_gate)
    up = matmul(h2_b, full_up)
    mixed, swiglu_back = jax.vjp(swiglu, gate, up)
    mixed_b = mixed.astype(jnp.bfloat16)
    result = (x2 + matmul(mixed_b, full_down)).astype(jnp.bfloat16)
    back_gate, back_up, back_down = (
        lax.all_gather(w_gate, "fsdp", axis=0, tiled=True),
        lax.all_gather(w_up, "fsdp", axis=0, tiled=True),
        lax.all_gather(w_down, "fsdp", axis=0, tiled=True),
    )
    grad_mixed = times_t(cotangent, back_down)
    grad_gate, grad_up = swiglu_back(grad_mixed)
    gate_b = grad_gate.astype(jnp.bfloat16)
    up_b = grad_up.astype(jnp.bfloat16)
    grad_h2 = times_t(gate_b, back_gate) + times_t(up_b, back_up)
    normed_two, gain_two_part = norm_two_back(grad_h2)
    grad_x2 = cotangent.astype(jnp.float32) + normed_two
    picked = h2_b
    gate_up = lax.psum_scatter(
        jnp.concatenate([t_times(picked, gate_b), t_times(picked, up_b)], axis=1),
        "fsdp",
        scatter_dimension=0,
        tiled=True,
    )
    hidden_width = w_gate.shape[1]
    picked = mixed_b
    grad_down = lax.psum_scatter(
        t_times(picked, cotangent), "fsdp", scatter_dimension=0, tiled=True
    )
    back_query, back_key, back_value, back_out = (
        lax.all_gather(w_query, "fsdp", axis=0, tiled=True),
        lax.all_gather(w_key, "fsdp", axis=0, tiled=True),
        lax.all_gather(w_value, "fsdp", axis=0, tiled=True),
        lax.all_gather(w_out, "fsdp", axis=0, tiled=True),
    )
    attn_grad_b = grad_x2.astype(jnp.bfloat16)
    grad_out_b = times_t(attn_grad_b, back_out).astype(jnp.bfloat16)
    grad_out_g = split_heads(grad_out_b, count)
    dquery_g, dkeys_g, dvalues_g = lax.map(
        lambda item: attend_backward(item[0], item[1], item[2], item[3], item[4], valid),
        (query_g, keys_g, values_g, grad_out_g, logsum),
    )
    grad_query = join_heads(dquery_g)
    grad_keys = join_heads(dkeys_g)
    grad_values = join_heads(dvalues_g)
    own_row = (reach - 1) * rows
    key_total = grad_keys[own_row:]
    value_total = grad_values[own_row:]
    for dist in range(1, reach):
        low_row = (reach - 1 - dist) * rows
        returned = passed_along(
            jnp.stack(
                [grad_keys[low_row : low_row + rows], grad_values[low_row : low_row + rows]]
            ).astype(jnp.bfloat16),
            "fsdp",
            -dist,
        ).astype(jnp.float32)
        key_total = key_total + returned[0]
        value_total = value_total + returned[1]
    dquery_b = (
        rotate(grad_query.reshape(rows, HEADS, HEAD_DIM), positions, -1.0)
        .reshape(rows, -1)
        .astype(jnp.bfloat16)
    )
    dkey_b = (
        rotate(key_total.reshape(rows, HEADS, HEAD_DIM), positions, -1.0)
        .reshape(rows, -1)
        .astype(jnp.bfloat16)
    )
    dvalue_b = value_total.astype(jnp.bfloat16)
    grad_h1 = (
        times_t(dquery_b, back_query) + times_t(dkey_b, back_key) + times_t(dvalue_b, back_value)
    )
    normed_one, gain_one_part = norm_one_back(grad_h1)
    grad_tokens = grad_x2 + normed_one
    picked = h1_b
    attn_all = lax.psum_scatter(
        jnp.concatenate(
            [
                t_times(picked, dquery_b),
                t_times(picked, dkey_b),
                t_times(picked, dvalue_b),
                t_times(out_b, attn_grad_b),
            ],
            axis=1,
        ),
        "fsdp",
        scatter_dimension=0,
        tiled=True,
    )
    width = w_query.shape[1]
    gain_one_grad, gain_two_grad = (
        lax.psum_scatter(gain_one_part, "fsdp", scatter_dimension=0, tiled=True),
        lax.psum_scatter(gain_two_part, "fsdp", scatter_dimension=0, tiled=True),
    )
    return (
        result,
        grad_tokens,
        gain_one_grad,
        attn_all[:, :width],
        attn_all[:, width : 2 * width],
        attn_all[:, 2 * width : 3 * width],
        attn_all[:, 3 * width :],
        gain_two_grad,
        gate_up[:, :hidden_width],
        gate_up[:, hidden_width:],
        grad_down,
    )


def solution(mesh):
    placed = (
        P("fsdp", None),
        P("fsdp"),
        P("fsdp"),
        P("fsdp"),
        P("fsdp", None),
        P("fsdp", None),
        P("fsdp", None),
        P("fsdp", None),
        P("fsdp"),
        P("fsdp", None),
        P("fsdp", None),
        P("fsdp", None),
        P("fsdp", None),
    )
    return jax.shard_map(
        local,
        mesh=mesh,
        in_specs=placed,
        out_specs=(
            P("fsdp", None),
            P("fsdp", None),
            P("fsdp"),
            P("fsdp", None),
            P("fsdp", None),
            P("fsdp", None),
            P("fsdp", None),
            P("fsdp"),
            P("fsdp", None),
            P("fsdp", None),
            P("fsdp", None),
        ),
        check_vma=False,
    )
```

profile of v0, /device:TPU:0, one launch (start us, length us, event | category | flops | bytes accessed | tf_op | source)
XLA Modules:
  0.0 5193.9 jit_solution(8642749775443017705)
XLA Ops:
  32.2 39.5 all-reduce.6
  107.6 63.5 %all-gather.10.cloned.1.call-done = bf16[2048,2048]{1,0:T(8,128)(2,1)} async-done(((bf16[64,2048]{1,0:T(8,128)(2,1)}), bf16[2048,2048]{1,0:T(8,128)(2,1)}) %all-gather.10.cloned.1.call-update) | async-done | bytes 8388624 | tf_op jit(solution)/shard_map/all_gather | solution.py:123
  193.8 170.6 %all-gather.12.cloned.1.call-done = bf16[2048,2048]{1,0:T(8,128)(2,1)} async-done(((bf16[64,2048]{1,0:T(8,128)(2,1)}), bf16[2048,2048]{1,0:T(8,128)(2,1)}) %all-gather.12.cloned.1.call-update) | async-done | bytes 8388624 | tf_op jit(solution)/shard_map/all_gather | solution.py:121
  397.2 60.6 %collective-permute-start.8 = (bf16[2,128,2048]{2,1,0:T(8,128)(2,1)}, bf16[2,128,2048]{2,1,0:T(8,128)(2,1)S(1)}, u32[]{:S(2)}, u32[]{:S(2)}) collective-permute-start(bf16[2,128,2048]{2,1,0:T(8,128)(2,1)} %pad_maximum_fusion.2), channel_id=1, source_target_pairs={{0,7},{1,8},{2,9},{3,10},{4,11},{5,12},{6,13},{7,14},{8,15},{9,16}... | collective-permute-start | bytes 3145736 | tf_op jit(solution)/shard_map/ppermute | solution.py:19
  468.8 38.4 collective-permute-start.11
  513.9 22.9 collective-permute-start.13
  632.9 56.0 %while.30 = (s32[]{:T(128)}, bf16[4,128,8,64]{1,3,2,0:T(8,128)(2,1)S(1)}, f32[4,8,128,1]{2,1,3,0:T(8,128)}, bf16[4,2048,8,64]{1,3,2,0:T(8,128)(2,1)}, bf16[4,128...) while((s32[]{:T(128)}, ...), condition=%wide.region_4.5_spmd.clone.clone, body=%wide.region_1.4_spmd.clone.sunk.clone | while | flops 567278592 | bytes 30856312 | solution.py:160
  695.2 134.2 %all-gather.16.cloned.1.call-done = bf16[2048,8192]{1,0:T(8,128)(2,1)} async-done(((bf16[64,8192]{1,0:T(8,128)(2,1)}), bf16[2048,8192]{1,0:T(8,128)(2,1)}) %all-gather.16.cloned.1.call-update) | async-done | bytes 33554448 | tf_op jit(solution)/shard_map/all_gather | solution.py:166
  829.4 17.1 fusion.137
  846.5 225.6 %all-gather.18.cloned.1.call-done = bf16[2048,8192]{1,0:T(8,128)(2,1)} async-done(((bf16[64,8192]{1,0:T(8,128)(2,1)}), bf16[2048,8192]{1,0:T(8,128)(2,1)}) %all-gather.18.cloned.1.call-update) | async-done | bytes 33554448 | tf_op jit(solution)/shard_map/all_gather | solution.py:167
  1072.1 17.8 fusion.138
  1089.9 178.1 %all-gather.20.cloned.1.call-done = bf16[8192,2048]{1,0:T(8,128)(2,1)} async-done(((bf16[256,2048]{1,0:T(8,128)(2,1)}), bf16[8192,2048]{1,0:T(8,128)(2,1)}) %all-gather.20.cloned.1.call-update) | async-done | bytes 33554448 | tf_op jit(solution)/shard_map/all_gather | solution.py:168
  1268.0 20.2 multiply_convert_fusion.1
  1288.1 24.7 fusion.142
  1312.9 23.3 fusion.141
  1336.2 86.9 %pad_maximum_fusion = f32[2048,16384]{1,0:T(8,128)} fusion(f32[2048,8192]{1,0:T(8,128)} %fusion.142, f32[2048,8192]{1,0:T(8,128)} %fusion.141), kind=kLoop, calls=%fused_computation.57 | loop fusion | flops 33554432 | bytes 268435456 | tf_op jit(solution)/shard_map/concatenate | solution.py:192
  1440.4 17.6 multiply_reduce_fusion.1
  1466.1 128.9 %while.31 = (s32[]{:T(128)}, f32[4,128,8,64]{1,3,2,0:T(8,128)}, f32[4,2048,8,64]{1,3,2,0:T(8,128)}, f32[4,2048,8,64]{1,3,2,0:T(8,128)}, bf16[4,2048,8,64]{1,3,2,...) while((s32[]{:T(128)}, f32[4,128,8,64]{1,3,2,0:T(8,128)}, ...), condition=%wide.region_9.10_spmd.clone.clone, body=%wide.region_7.9_spmd.clone.sunk.clone | while | flops 1365310464 | bytes 146059456 | solution.py:211
  1618.6 54.8 %collective-permute-done.44 = bf16[2,128,2048]{1,2,0:T(8,128)(2,1)S(1)} collective-permute-done((bf16[2,128,2048]{1,2,0:T(8,128)(2,1)S(1)}, bf16[2,128,2048]{1,2,0:T(8,128)(2,1)S(1)}, u32[]{:S(2)}, u32[]{:S(2)}) %collective-permute-start.44) | collective-permute-done | bytes 1048608 | tf_op jit(solution)/shard_map/ppermute | solution.py:19
  1692.3 38.9 collective-permute-done.38
  1732.5 70.4 %collective-permute-done.37 = bf16[2,128,2048]{1,2,0:T(8,128)(2,1)S(1)} collective-permute-done((bf16[2,128,2048]{1,2,0:T(8,128)(2,1)S(1)}, bf16[2,128,2048]{1,2,0:T(8,128)(2,1)S(1)}, u32[]{:S(2)}, u32[]{:S(2)}) %collective-permute-start.37) | collective-permute-done | bytes 1048608 | tf_op jit(solution)/shard_map/ppermute | solution.py:19
  1804.1 86.2 %collective-permute-done.36 = bf16[2,128,2048]{1,2,0:T(8,128)(2,1)S(1)} collective-permute-done((bf16[2,128,2048]{1,2,0:T(8,128)(2,1)S(1)}, bf16[2,128,2048]{1,2,0:T(8,128)(2,1)S(1)}, u32[]{:S(2)}, u32[]{:S(2)}) %collective-permute-start.36) | collective-permute-done | bytes 1048608 | tf_op jit(solution)/shard_map/ppermute | solution.py:19
  1892.7 59.9 %collective-permute-done.35 = bf16[2,128,2048]{1,2,0:T(8,128)(2,1)S(1)} collective-permute-done((bf16[2,128,2048]{1,2,0:T(8,128)(2,1)S(1)}, bf16[2,128,2048]{1,2,0:T(8,128)(2,1)S(1)}, u32[]{:S(2)}, u32[]{:S(2)}) %collective-permute-start.35) | collective-permute-done | bytes 1048608 | tf_op jit(solution)/shard_map/ppermute | solution.py:19
  1986.8 33.4 collective-permute-done.32
  2022.7 19.9 collective-permute-done.31
  2081.2 40.7 pad_maximum_fusion.1
  2122.0 62.5 %copy.161 = f32[2048,8192]{1,0:T(8,128)} copy(f32[2048,8192]{0,1:T(8,128)} %pad_maximum_fusion.1) | data formatting | bytes 134217728
  2186.2 23.6 fusion.143
  2241.7 329.9 %all-reduce.5 = (f32[2048]{0:T(1024)S(1)}, f32[2048]{0:T(1024)S(1)}) all-reduce(f32[2048]{0:T(1024)S(1)} %get-tuple-element.207, f32[2048]{0:T(1024)S(1)} %copy-done.71), channel_id=2, replica_groups=mesh['fsdp'=32] {'fsdp'}, use_global_device_ids=true, to_apply=%region_12.13.clone | all-reduce | flops 4096 | bytes 32768
  2574.1 1195.5 %all-reduce.9.cloned.1.call-done = f32[2048,16384]{1,0:T(8,128)} async-done(((f32[2048,16384]{1,0:T(8,128)}), f32[2048,16384]{1,0:T(8,128)}) %all-reduce.9.cloned.1.call-update) | async-done | bytes 134217744
  3774.5 699.4 %reduce-scatter.7.cloned.1.call-done = f32[64,8192]{1,0:T(8,128)} async-done(((f32[2048,8192]{1,0:T(8,128)}), f32[64,8192]{1,0:T(8,128)}) %reduce-scatter.7.cloned.1.call-update) | async-done | bytes 2097168
  4476.7 710.1 %reduce-scatter.5.cloned.1.call-done = f32[256,2048]{1,0:T(8,128)} async-done(((f32[8192,2048]{1,0:T(8,128)}), f32[256,2048]{1,0:T(8,128)}) %reduce-scatter.5.cloned.1.call-update) | async-done | bytes 2097168 | tf_op jit(solution)/shard_map/reduce_scatter | solution.py:199
  (527 shorter events, 599.3 us)
Async XLA Ops:
  7.2 92.6 %all-gather.8.cloned.1.call-start = ((), (), s32[]{:S(2)}) async-start(), calls=%async_computation.2 | async-start | bytes 8650752 | tf_op jit(solution)/shard_map/all_gather | solution.py:122
  7.9 163.2 %all-gather.10.cloned.1.call-start = ((), (), s32[]{:S(2)}) async-start(), calls=%async_computation.3 | async-start | bytes 8650752 | tf_op jit(solution)/shard_map/all_gather | solution.py:123
  8.7 355.8 %all-gather.12.cloned.1.call-start = ((), (), s32[]{:S(2)}) async-start(), calls=%async_computation.4 | async-start | bytes 8650752 | tf_op jit(solution)/shard_map/all_gather | solution.py:121
  9.4 679.5 %all-gather.14.cloned.1.call-start = ((), (), s32[]{:S(2)}) async-start(), calls=%async_computation.5 | async-start | bytes 8650752 | tf_op jit(solution)/shard_map/all_gather | solution.py:124
  10.0 819.4 %all-gather.16.cloned.1.call-start = ((), (), s32[]{:S(2)}) async-start(), calls=%async_computation.6 | async-start | bytes 34603008 | tf_op jit(solution)/shard_map/all_gather | solution.py:166
  10.6 1061.6 %all-gather.18.cloned.1.call-start = ((), (), s32[]{:S(2)}) async-start(), calls=%async_computation.7 | async-start | bytes 34603008 | tf_op jit(solution)/shard_map/all_gather | solution.py:167
  11.1 1256.8 %all-gather.20.cloned.1.call-start = ((), (), s32[]{:S(2)}) async-start(), calls=%async_computation.8 | async-start | bytes 34603008 | tf_op jit(solution)/shard_map/all_gather | solution.py:168
  11.9 3757.7 %all-reduce.9.cloned.1.call-start = ((), (), s32[]{:S(2)}) async-start(), calls=%async_computation.11 | async-start | bytes 268435456
  98.4 83.6 %collective-permute-start.29 = (s32[128]{0:T(128)}, s32[128]{0:T(128)S(1)}, u32[]{:S(2)}, u32[]{:S(2)}) collective-permute-start(s32[128]{0:T(128)} %param.18), channel_id=1, source_target_pairs={{0,1},{1,2},{2,3},{3,4},{4,5},{5,6},{6,7},{7,8},{8,9},{9,10},{10,1... | collective-permute-start | bytes 1544 | tf_op jit(solution)/shard_map/ppermute | solution.py:19
  176.9 195.6 %collective-permute-start = (bf16[2,128,2048]{2,1,0:T(8,128)(2,1)}, bf16[2,128,2048]{2,1,0:T(8,128)(2,1)}, u32[]{:S(2)}, u32[]{:S(2)}) collective-permute-start(bf16[2,128,2048]{2,1,0:T(8,128)(2,1)} %pad_maximum_fusion.2), channel_id=1, source_target_pairs={{0,15},{1,16},{2,17},{3,18},{4,19},{5,20},{6,21},{7,22},{8,23},{9,... | collective-permute-start | bytes 3145736 | tf_op jit(solution)/shard_map/ppermute | solution.py:19
  182.0 202.6 %collective-permute-start.1 = (bf16[2,128,2048]{2,1,0:T(8,128)(2,1)}, bf16[2,128,2048]{2,1,0:T(8,128)(2,1)}, u32[]{:S(2)}, u32[]{:S(2)}) collective-permute-start(bf16[2,128,2048]{2,1,0:T(8,128)(2,1)} %pad_maximum_fusion.2), channel_id=1, source_target_pairs={{0,14},{1,15},{2,16},{3,17},{4,18},{5,19},{6,20},{7,21},{8,22},{9,... | collective-permute-start | bytes 3145736 | tf_op jit(solution)/shard_map/ppermute | solution.py:19
  186.8 202.4 %collective-permute-start.2 = (bf16[2,128,2048]{2,1,0:T(8,128)(2,1)}, bf16[2,128,2048]{2,1,0:T(8,128)(2,1)}, u32[]{:S(2)}, u32[]{:S(2)}) collective-permute-start(bf16[2,128,2048]{2,1,0:T(8,128)(2,1)} %pad_maximum_fusion.2), channel_id=1, source_target_pairs={{0,13},{1,14},{2,15},{3,16},{4,17},{5,18},{6,19},{7,20},{8,21},{9,... | collective-permute-start | bytes 3145736 | tf_op jit(solution)/shard_map/ppermute | solution.py:19
  189.1 208.1 %collective-permute-start.3 = (bf16[2,128,2048]{2,1,0:T(8,128)(2,1)}, bf16[2,128,2048]{2,1,0:T(8,128)(2,1)}, u32[]{:S(2)}, u32[]{:S(2)}) collective-permute-start(bf16[2,128,2048]{2,1,0:T(8,128)(2,1)} %pad_maximum_fusion.2), channel_id=1, source_target_pairs={{0,12},{1,13},{2,14},{3,15},{4,16},{5,17},{6,18},{7,19},{8,20},{9,... | collective-permute-start | bytes 3145736 | tf_op jit(solution)/shard_map/ppermute | solution.py:19
  191.4 268.7 %collective-permute-start.4 = (bf16[2,128,2048]{2,1,0:T(8,128)(2,1)}, bf16[2,128,2048]{2,1,0:T(8,128)(2,1)}, u32[]{:S(2)}, u32[]{:S(2)}) collective-permute-start(bf16[2,128,2048]{2,1,0:T(8,128)(2,1)} %pad_maximum_fusion.2), channel_id=1, source_target_pairs={{0,11},{1,12},{2,13},{3,14},{4,15},{5,16},{6,17},{7,18},{8,19},{9,... | collective-permute-start | bytes 3145736 | tf_op jit(solution)/shard_map/ppermute | solution.py:19
  372.5 93.9 %collective-permute-start.5 = (bf16[2,128,2048]{2,1,0:T(8,128)(2,1)}, bf16[2,128,2048]{2,1,0:T(8,128)(2,1)S(1)}, u32[]{:S(2)}, u32[]{:S(2)}) collective-permute-start(bf16[2,128,2048]{2,1,0:T(8,128)(2,1)} %pad_maximum_fusion.2), channel_id=1, source_target_pairs={{0,10},{1,11},{2,12},{3,13},{4,14},{5,15},{6,16},{7,17},{8,18},{9,... | collective-permute-start | bytes 3145736 | tf_op jit(solution)/shard_map/ppermute | solution.py:19
  384.6 84.1 %collective-permute-start.6 = (bf16[2,128,2048]{2,1,0:T(8,128)(2,1)}, bf16[2,128,2048]{2,1,0:T(8,128)(2,1)S(1)}, u32[]{:S(2)}, u32[]{:S(2)}) collective-permute-start(bf16[2,128,2048]{2,1,0:T(8,128)(2,1)} %pad_maximum_fusion.2), channel_id=1, source_target_pairs={{0,9},{1,10},{2,11},{3,12},{4,13},{5,14},{6,15},{7,16},{8,17},{9,1... | collective-permute-start | bytes 3145736 | tf_op jit(solution)/shard_map/ppermute | solution.py:19
  389.2 118.9 %collective-permute-start.7 = (bf16[2,128,2048]{2,1,0:T(8,128)(2,1)}, bf16[2,128,2048]{2,1,0:T(8,128)(2,1)S(1)}, u32[]{:S(2)}, u32[]{:S(2)}) collective-permute-start(bf16[2,128,2048]{2,1,0:T(8,128)(2,1)} %pad_maximum_fusion.2), channel_id=1, source_target_pairs={{0,8},{1,9},{2,10},{3,11},{4,12},{5,13},{6,14},{7,15},{8,16},{9,17... | collective-permute-start | bytes 3145736 | tf_op jit(solution)/shard_map/ppermute | solution.py:19
  397.2 116.7 %collective-permute-start.8 = (bf16[2,128,2048]{2,1,0:T(8,128)(2,1)}, bf16[2,128,2048]{2,1,0:T(8,128)(2,1)S(1)}, u32[]{:S(2)}, u32[]{:S(2)}) collective-permute-start(bf16[2,128,2048]{2,1,0:T(8,128)(2,1)} %pad_maximum_fusion.2), channel_id=1, source_target_pairs={{0,7},{1,8},{2,9},{3,10},{4,11},{5,12},{6,13},{7,14},{8,15},{9,16}... | collective-permute-start | bytes 3145736 | tf_op jit(solution)/shard_map/ppermute | solution.py:19
  460.1 77.7 %collective-permute-start.9 = (bf16[2,128,2048]{2,1,0:T(8,128)(2,1)}, bf16[2,128,2048]{2,1,0:T(8,128)(2,1)S(1)}, u32[]{:S(2)}, u32[]{:S(2)}) collective-permute-start(bf16[2,128,2048]{2,1,0:T(8,128)(2,1)} %pad_maximum_fusion.2), channel_id=1, source_target_pairs={{0,6},{1,7},{2,8},{3,9},{4,10},{5,11},{6,12},{7,13},{8,14},{9,15},... | collective-permute-start | bytes 3145736 | tf_op jit(solution)/shard_map/ppermute | solution.py:19
  466.4 75.0 %collective-permute-start.10 = (bf16[2,128,2048]{2,1,0:T(8,128)(2,1)}, bf16[2,128,2048]{2,1,0:T(8,128)(2,1)S(1)}, u32[]{:S(2)}, u32[]{:S(2)}) collective-permute-start(bf16[2,128,2048]{2,1,0:T(8,128)(2,1)} %pad_maximum_fusion.2), channel_id=1, source_target_pairs={{0,5},{1,6},{2,7},{3,8},{4,9},{5,10},{6,11},{7,12},{8,13},{9,14},{... | collective-permute-start | bytes 3145736 | tf_op jit(solution)/shard_map/ppermute | solution.py:19
  468.8 73.7 %collective-permute-start.11 = (bf16[2,128,2048]{2,1,0:T(8,128)(2,1)}, bf16[2,128,2048]{2,1,0:T(8,128)(2,1)S(1)}, u32[]{:S(2)}, u32[]{:S(2)}) collective-permute-start(bf16[2,128,2048]{2,1,0:T(8,128)(2,1)} %pad_maximum_fusion.2), channel_id=1, source_target_pairs={{0,4},{1,5},{2,6},{3,7},{4,8},{5,9},{6,10},{7,11},{8,12},{9,13},{1... | collective-permute-start | bytes 3145736 | tf_op jit(solution)/shard_map/ppermute | solution.py:19
  1423.1 3050.7 %reduce-scatter.7.cloned.1.call-start = ((), (), s32[]{:S(2)}) async-start(), calls=%async_computation.10 | async-start | bytes 69206016
  1612.7 63.6 %collective-permute-start.43 = (bf16[2,128,2048]{1,2,0:T(8,128)(2,1)S(1)}, bf16[2,128,2048]{1,2,0:T(8,128)(2,1)S(1)}, u32[]{:S(2)}, u32[]{:S(2)}) collective-permute-start(bf16[2,128,2048]{1,2,0:T(8,128)(2,1)S(1)} %pad_maximum_fusion.16), channel_id=1, source_target_pairs={{14,0},{15,1},{16,2},{17,3},{18,4},{19,5},{20,6},{21,7},{22,8},{23... | collective-permute-start | bytes 3145736 | tf_op jit(solution)/shard_map/ppermute | solution.py:19
  1677.6 125.3 %collective-permute-start.37 = (bf16[2,128,2048]{1,2,0:T(8,128)(2,1)S(1)}, bf16[2,128,2048]{1,2,0:T(8,128)(2,1)S(1)}, u32[]{:S(2)}, u32[]{:S(2)}) collective-permute-start(bf16[2,128,2048]{1,2,0:T(8,128)(2,1)S(1)} %pad_maximum_fusion.10), channel_id=1, source_target_pairs={{8,0},{9,1},{10,2},{11,3},{12,4},{13,5},{14,6},{15,7},{16,8},{17,9... | collective-permute-start | bytes 3145736 | tf_op jit(solution)/shard_map/ppermute | solution.py:19
  1678.9 211.5 %collective-permute-start.36 = (bf16[2,128,2048]{1,2,0:T(8,128)(2,1)S(1)}, bf16[2,128,2048]{1,2,0:T(8,128)(2,1)S(1)}, u32[]{:S(2)}, u32[]{:S(2)}) collective-permute-start(bf16[2,128,2048]{1,2,0:T(8,128)(2,1)S(1)} %pad_maximum_fusion.9), channel_id=1, source_target_pairs={{7,0},{8,1},{9,2},{10,3},{11,4},{12,5},{13,6},{14,7},{15,8},{16,9}... | collective-permute-start | bytes 3145736 | tf_op jit(solution)/shard_map/ppermute | solution.py:19
  1680.3 272.3 %collective-permute-start.35 = (bf16[2,128,2048]{1,2,0:T(8,128)(2,1)S(1)}, bf16[2,128,2048]{1,2,0:T(8,128)(2,1)S(1)}, u32[]{:S(2)}, u32[]{:S(2)}) collective-permute-start(bf16[2,128,2048]{1,2,0:T(8,128)(2,1)S(1)} %pad_maximum_fusion.8), channel_id=1, source_target_pairs={{6,0},{7,1},{8,2},{9,3},{10,4},{11,5},{12,6},{13,7},{14,8},{15,9},... | collective-permute-start | bytes 3145736 | tf_op jit(solution)/shard_map/ppermute | solution.py:19
  1691.0 290.7 %collective-permute-start.34 = (bf16[2,128,2048]{1,2,0:T(8,128)(2,1)}, bf16[2,128,2048]{1,2,0:T(8,128)(2,1)S(1)}, u32[]{:S(2)}, u32[]{:S(2)}) collective-permute-start(bf16[2,128,2048]{1,2,0:T(8,128)(2,1)} %pad_maximum_fusion.7), channel_id=1, source_target_pairs={{5,0},{6,1},{7,2},{8,3},{9,4},{10,5},{11,6},{12,7},{13,8},{14,9},{... | collective-permute-start | bytes 3145736 | tf_op jit(solution)/shard_map/ppermute | solution.py:19
  1731.2 253.1 %collective-permute-start.33 = (bf16[2,128,2048]{1,2,0:T(8,128)(2,1)}, bf16[2,128,2048]{1,2,0:T(8,128)(2,1)S(1)}, u32[]{:S(2)}, u32[]{:S(2)}) collective-permute-start(bf16[2,128,2048]{1,2,0:T(8,128)(2,1)} %pad_maximum_fusion.6), channel_id=1, source_target_pairs={{4,0},{5,1},{6,2},{7,3},{8,4},{9,5},{10,6},{11,7},{12,8},{13,9},{1... | collective-permute-start | bytes 3145736 | tf_op jit(solution)/shard_map/ppermute | solution.py:19
  1802.8 217.4 %collective-permute-start.32 = (bf16[2,128,2048]{1,2,0:T(8,128)(2,1)}, bf16[2,128,2048]{1,2,0:T(8,128)(2,1)S(1)}, u32[]{:S(2)}, u32[]{:S(2)}) collective-permute-start(bf16[2,128,2048]{1,2,0:T(8,128)(2,1)} %pad_maximum_fusion.5), channel_id=1, source_target_pairs={{3,0},{4,1},{5,2},{6,3},{7,4},{8,5},{9,6},{10,7},{11,8},{12,9},{13... | collective-permute-start | bytes 3145736 | tf_op jit(solution)/shard_map/ppermute | solution.py:19
  1890.3 152.3 %collective-permute-start.31 = (bf16[2,128,2048]{1,2,0:T(8,128)(2,1)S(1)}, bf16[2,128,2048]{1,2,0:T(8,128)(2,1)S(1)}, u32[]{:S(2)}, u32[]{:S(2)}) collective-permute-start(bf16[2,128,2048]{1,2,0:T(8,128)(2,1)S(1)} %pad_maximum_fusion.4), channel_id=1, source_target_pairs={{2,0},{3,1},{4,2},{5,3},{6,4},{7,5},{8,6},{9,7},{10,8},{11,9},{12,... | collective-permute-start | bytes 3145736 | tf_op jit(solution)/shard_map/ppermute | solution.py:19
  1952.6 92.7 %collective-permute-start.30 = (bf16[2,128,2048]{1,2,0:T(8,128)(2,1)}, bf16[2,128,2048]{1,2,0:T(8,128)(2,1)S(1)}, u32[]{:S(2)}, u32[]{:S(2)}) collective-permute-start(bf16[2,128,2048]{1,2,0:T(8,128)(2,1)} %pad_maximum_fusion.3), channel_id=1, source_target_pairs={{1,0},{2,1},{3,2},{4,3},{5,4},{6,5},{7,6},{8,7},{9,8},{10,9},{11,1... | collective-permute-start | bytes 3145736 | tf_op jit(solution)/shard_map/ppermute | solution.py:19
  2184.5 3002.4 %reduce-scatter.5.cloned.1.call-start = ((), (), s32[]{:S(2)}) async-start(), calls=%async_computation.9 | async-start | bytes 69206016 | tf_op jit(solution)/shard_map/reduce_scatter | solution.py:199
  (109 other events, 5344.8 us)
Sparse Core Ops, SparseCore 0:
  10.9 81.1 all-gather.7
  94.9 76.1 all-gather.9
  174.0 190.4 all-gather.11
  367.2 210.6 all-gather.13
  580.6 248.7 all-gather.15
  832.1 239.9 all-gather.17
  1075.0 192.9 all-gather.19
  1423.3 2346.2 all-reduce.8
  3771.9 701.8 reduce-scatter.6
  4476.6 710.1 reduce-scatter.4
where the time goes:
time: 5210 us; the launch traced here: 5190 us
  waiting for transfers between devices  3760 us (72%)
  matrix products  377 us (7%)
  blocking collectives  369 us (7%)
  starting transfers between devices  233 us (4%)
  other arithmetic  220 us (4%)
  local copies, waits for them, and re-layouts  208 us (4%)
    unnamed x12, waiting for transfers between devices  1900 us
    reduce_scatter x1, waiting for transfers between devices, local(): lax.psum_scatter(t_times(picked, cotangent), 'fsdp', scatter_dimension=0,...  710 us
    ppermute x45, waiting for transfers between devices, passed_along(): lax.ppermute(value, axis, [(source, source + steps) for source in range(i...  378 us
    unnamed x2, blocking collectives  369 us
    ppermute x45, starting transfers between devices, passed_along(): lax.ppermute(value, axis, [(source, source + steps) for source in range(i...  232 us
    all_gather x1, waiting for transfers between devices, local(): lax.all_gather(w_up, 'fsdp', axis=0, tiled=True)  226 us
    all_gather x1, waiting for transfers between devices, local(): lax.all_gather(w_down, 'fsdp', axis=0, tiled=True)  178 us
    all_gather x1, waiting for transfers between devices, local(): lax.all_gather(w_query, 'fsdp', axis=0, tiled=True)  171 us
  transfers between devices with their start and end apart: 55, of which 18 were waited for; matrix products, arithmetic and copies ran while one was open for 12% of the time, Pallas kernels for 0%

commit v1 on v0

v1 whole, which is shorter than its diff:
```python
import jax
import jax.numpy as jnp
from jax import lax
from jax.sharding import PartitionSpec as P

HEADS = 32
HEAD_DIM = 64
SEQ = 2048


EPS = 1e-05
THETA = 130000.0
NEG = -1e30
BF = jnp.bfloat16


def norm_rows(v, gain):
    scale = lax.rsqrt(jnp.mean(v * v, axis=-1, keepdims=True) + EPS)
    return v * scale * gain


def norm_back(v, gain, grad):
    scale = lax.rsqrt(jnp.mean(v * v, axis=-1, keepdims=True) + EPS)
    hat = v * scale
    weighted = gain * grad
    back = scale * (weighted - hat * jnp.mean(hat * weighted, axis=-1, keepdims=True))
    return back, jnp.sum(grad * hat, axis=0)


def matmul(left, right):
    return jnp.dot(left, right, preferred_element_type=jnp.float32)


def times_t(left, right):
    return lax.dot_general(
        left, right, (((1,), (1,)), ((), ())), preferred_element_type=jnp.float32
    )


def t_times(left, right):
    return lax.dot_general(
        left, right, (((0,), (0,)), ((), ())), preferred_element_type=jnp.float32
    )


def rotate(v, cosine, sine):
    rows, width = v.shape
    v = v.reshape(rows, width // HEAD_DIM, 2, HEAD_DIM // 2)
    first, second = v[:, :, 0], v[:, :, 1]
    cosine, sine = cosine[:, None], sine[:, None]
    turned = jnp.stack([first * cosine - second * sine, second * cosine + first * sine], axis=2)
    return turned.reshape(rows, width)


def heads_first(v):
    return v.reshape(v.shape[0], -1, HEAD_DIM).transpose(1, 0, 2)


def heads_last(v):
    return v.transpose(1, 0, 2).reshape(v.shape[1], -1)


def attend_forward(query, keys, values, valid):
    query, keys, values = heads_first(query), heads_first(keys), heads_first(values)
    scores = jnp.einsum("hqd,hkd->hqk", query, keys, preferred_element_type=jnp.float32)
    scores = jnp.where(valid[None], scores * HEAD_DIM**-0.5, NEG)
    top = jnp.max(scores, axis=-1, keepdims=True)
    expd = jnp.exp(scores - top)
    total = jnp.sum(expd, axis=-1, keepdims=True)
    probs = (expd / total).astype(BF)
    out = jnp.einsum("hqk,hkd->hqd", probs, values, preferred_element_type=jnp.float32)
    return heads_last(out), top + jnp.log(total)


def attend_backward(query, keys, values, grad_out, logsum, valid):
    query, keys, values, grad_out = (heads_first(v) for v in (query, keys, values, grad_out))
    scale = HEAD_DIM**-0.5
    scores = jnp.einsum("hqd,hkd->hqk", query, keys, preferred_element_type=jnp.float32)
    probs = jnp.where(valid[None], jnp.exp(scores * scale - logsum), 0.0)
    dprob = jnp.einsum("hqd,hkd->hqk", grad_out, values, preferred_element_type=jnp.float32)
    delta = jnp.sum(probs * dprob, axis=-1, keepdims=True)
    dscore = (probs * (dprob - delta)).astype(BF)
    dquery = jnp.einsum("hqk,hkd->hqd", dscore, keys, preferred_element_type=jnp.float32) * scale
    dkeys = jnp.einsum("hqk,hqd->hkd", dscore, query, preferred_element_type=jnp.float32) * scale
    dvalues = jnp.einsum(
        "hqk,hqd->hkd", probs.astype(BF), grad_out, preferred_element_type=jnp.float32
    )
    return heads_last(dquery), heads_last(dkeys), heads_last(dvalues)


def local(
    tokens,
    segments,
    positions,
    gain_attn,
    w_query,
    w_key,
    w_value,
    w_out,
    gain_mlp,
    w_gate,
    w_up,
    w_down,
    cotangent,
):
    rows, width = tokens.shape
    team = SEQ // rows
    count = lax.axis_size("fsdp")
    teams = count // team
    index = lax.axis_index("fsdp")
    mine = index // team
    place = index % team
    groups = [[t * team + p for p in range(team)] for t in range(teams)]
    own = w_query.shape[0]
    head_cuts = teams if own % HEAD_DIM == 0 else 1
    ff_own = w_down.shape[0]

    def gather(v):
        return lax.all_gather(v, "fsdp", axis=0, tiled=True, axis_index_groups=groups)

    def scatter(v):
        return lax.psum_scatter(
            v, "fsdp", scatter_dimension=0, tiled=True, axis_index_groups=groups
        )

    def exchange(v):
        return lax.all_to_all(v, "fsdp", 0, 0, tiled=True, axis_index_groups=groups)

    def to_team(v, ahead):
        return lax.ppermute(
            v, "fsdp", [(i, (i + ahead * team) % count) for i in range(count)]
        )

    def across(v):
        held = jnp.zeros((teams,) + v.shape, v.dtype)
        held = lax.dynamic_update_index_in_dim(held, v, mine, 0)
        for ahead in range(1, teams):
            held = lax.dynamic_update_index_in_dim(
                held, to_team(v, ahead), (mine - ahead) % teams, 0
            )
        return held

    def sum_across(v):
        total = lax.dynamic_index_in_dim(v, mine, 0, keepdims=False)
        for ahead in range(1, teams):
            sent = lax.dynamic_index_in_dim(v, (mine + ahead) % teams, 0, keepdims=False)
            total = total + to_team(sent.astype(BF), ahead).astype(jnp.float32)
        return total

    def cut_columns(w, cuts):
        r, c = w.shape
        return w.reshape(r, cuts, team, -1).transpose(2, 0, 1, 3).reshape(team, r, c // team)

    def join_columns(v, cuts):
        _, r, c = v.shape
        return v.reshape(team, r, cuts, -1).transpose(1, 2, 0, 3).reshape(r, c * team)

    def columns_of(weights, cuts):
        cut = jnp.concatenate([cut_columns(w, cuts) for w in weights], axis=2)
        block = exchange(cut)
        full = across(block.reshape(-1, block.shape[2]))
        return full.reshape(-1, block.shape[2])

    def rows_of(grad, parts, cuts):
        grad = sum_across(grad.reshape(teams, -1, grad.shape[1])).astype(BF)
        got = exchange(grad.reshape(team, -1, grad.shape[1]))
        each = got.shape[2] // parts
        return [
            join_columns(got[:, :, i * each : (i + 1) * each], cuts).astype(jnp.float32)
            for i in range(parts)
        ]

    small = jnp.concatenate(
        [v.astype(jnp.float32) for v in (gain_attn, gain_mlp, segments, positions)]
    )
    small = lax.all_gather(small, "fsdp", axis=0)
    gain_one = small[:, :own].reshape(1, -1)
    gain_two = small[:, own : 2 * own].reshape(1, -1)
    small = lax.dynamic_slice_in_dim(small, mine * team, team, 0)
    docs = small[:, 2 * own : 2 * own + rows].reshape(-1)
    places = small[:, 2 * own + rows :].reshape(-1)

    x_all = gather(tokens)
    w_qkv = columns_of([w_query, w_key, w_value], head_cuts)
    dy_all = gather(cotangent)
    w_gu = columns_of([w_gate, w_up], teams)
    if head_cuts == teams:
        out_rows = across(w_out).reshape(-1, width)
    else:
        out_rows = lax.dynamic_slice_in_dim(
            lax.all_gather(w_out, "fsdp", axis=0, tiled=True), place * (width // team), width // team
        )
    down_rows = across(w_down).reshape(-1, width)

    freqs = THETA ** (-jnp.arange(HEAD_DIM // 2, dtype=jnp.float32) * 2.0 / HEAD_DIM)
    angles = places[:, None] * freqs[None, :]
    cosine, sine = jnp.cos(angles), jnp.sin(angles)
    order = jnp.arange(SEQ, dtype=jnp.int32)
    valid = (docs[:, None] == docs[None, :]) & (order[:, None] >= order[None, :])

    h1 = norm_rows(x_all.astype(jnp.float32), gain_one).astype(BF)
    qkv = matmul(h1, w_qkv)
    each = qkv.shape[1] // 3
    query = rotate(qkv[:, :each], cosine, sine).astype(BF)
    keys = rotate(qkv[:, each : 2 * each], cosine, sine).astype(BF)
    values = qkv[:, 2 * each :].astype(BF)
    out, logsum = attend_forward(query, keys, values, valid)
    out = out.astype(BF)
    x = tokens.astype(jnp.float32)
    x2 = x + scatter(matmul(out, out_rows).astype(BF)).astype(jnp.float32)
    h2 = gather(norm_rows(x2, gain_two).astype(BF))
    gu = matmul(h2, w_gu)
    hidden = gu.shape[1] // 2
    gate, up = gu[:, :hidden], gu[:, hidden:]
    sig = jax.nn.sigmoid(gate)
    silu = gate * sig
    mixed = (silu * up).astype(BF)
    dm = times_t(dy_all, down_rows)
    dgate = (dm * up * (sig + silu * (1.0 - sig))).astype(BF)
    dup = (dm * silu).astype(BF)
    dgu = jnp.concatenate([dgate, dup], axis=1)
    dh2 = scatter(times_t(dgu, w_gu).astype(BF)).astype(jnp.float32)
    result = (x2 + scatter(matmul(mixed, down_rows).astype(BF)).astype(jnp.float32)).astype(BF)
    grad_down = sum_across(t_times(mixed, dy_all).reshape(teams, ff_own, width))
    grad_gate, grad_up = rows_of(t_times(h2, dgu), 2, teams)

    back, gain_two_part = norm_back(x2, gain_two, dh2)
    dx2 = cotangent.astype(jnp.float32) + back
    da = gather(dx2.astype(BF))
    dout = times_t(da, out_rows).astype(BF)
    grad_out = t_times(out, da)
    if head_cuts == teams:
        grad_out = sum_across(grad_out.reshape(teams, own, width))
    else:
        grad_out = lax.psum(grad_out, "fsdp", axis_index_groups=[list(t) for t in zip(*groups)])
        grad_out = lax.dynamic_slice_in_dim(gather(grad_out), index * own, own)
    dquery, dkeys, dvalues = attend_backward(query, keys, values, dout, logsum, valid)
    dqkv = jnp.concatenate(
        [
            rotate(dquery, cosine, -sine).astype(BF),
            rotate(dkeys, cosine, -sine).astype(BF),
            dvalues.astype(BF),
        ],
        axis=1,
    )
    dh1 = scatter(times_t(dqkv, w_qkv).astype(BF)).astype(jnp.float32)
    grad_query, grad_key, grad_value = rows_of(t_times(h1, dqkv), 3, head_cuts)
    back, gain_one_part = norm_back(x, gain_one, dh1)
    grad_tokens = dx2 + back
    gains = jnp.stack([gain_one_part, gain_two_part]).reshape(2, count, own).transpose(1, 0, 2)
    gains = jnp.sum(lax.all_to_all(gains, "fsdp", 0, 0, tiled=True), axis=0)
    return (
        result,
        grad_tokens,
        gains[0],
        grad_query,
        grad_key,
        grad_value,
        grad_out,
        gains[1],
        grad_gate,
        grad_up,
        grad_down,
    )


def solution(mesh):
    flat = P("fsdp")
    wide = P("fsdp", None)
    return jax.shard_map(
        local,
        mesh=mesh,
        in_specs=(wide, flat, flat, flat, wide, wide, wide, wide, flat, wide, wide, wide, wide),
        out_specs=(wide, wide, flat, wide, wide, wide, wide, flat, wide, wide, wide),
        check_vma=False,
    )
```

time: 5210 us -> 1050 us (0.20)
  waiting for transfers between devices: 3760 us -> 569 us
  blocking collectives: 369 us -> 99 us
  starting transfers between devices: 233 us -> 33.3 us
  matrix products: 377 us -> 188 us
  local copies, waits for them, and re-layouts: 208 us -> 59.1 us
  other arithmetic: 220 us -> 82.9 us
    unnamed x12 -> x8, waiting for transfers between devices: 1900 us -> 1.3 us
    all_gather x7 -> x4, waiting for transfers between devices: 772 us -> 53.3 us  [gather(): lax.all_gather(v, 'fsdp', axis=0, tiled=True, axis_index_groups=groups)]
    reduce_scatter x1 -> x4, waiting for transfers between devices: 710 us -> 182 us  [scatter(): lax.psum_scatter(v, 'fsdp', scatter_dimension=0, tiled=True, axis_index_g...]
    unnamed x2 -> x0, blocking collectives: 369 us -> none
    ppermute x45 -> x8, starting transfers between devices: 232 us -> 16.1 us  [to_team(): lax.ppermute(v, 'fsdp', [(i, (i + ahead * team) % count) for i in range(c...]
    concatenate x4 -> x3, other arithmetic: 128 us -> 2.66 us  [the longest x2 2.59 us: columns_of(): cut = jnp.concatenate([cut_columns(w, cuts) for w in weights], axis=2)]
    slice x66 -> x3, local copies, waits for them, and re-layouts: 115 us -> 0.35 us  [the longest x1 0.22 us: local(): keys = rotate(qkv[:, each:2 * each], cosine, sine).astype(BF)]
    unnamed x208 -> x117, local copies, waits for them, and re-layouts: 88.7 us -> 16.3 us
  transfers between devices with their start and end apart: 55 -> 20, of which waited for: 18 -> 9; matrix products, arithmetic and copies ran while one was open for 12% -> 12% of each run, Pallas kernels for 0% -> 0%
where the time goes in v1:
time: 1050 us
  waiting for transfers between devices  569 us (54%)
  matrix products  188 us (18%)
  blocking collectives  99 us (9%)
  other arithmetic  82.9 us (8%)
  local copies, waits for them, and re-layouts  59.1 us (6%)
  starting transfers between devices  33.3 us (3%)
  between operations  15.6 us (1%)
    ppermute x8, waiting for transfers between devices, to_team(): lax.ppermute(v, 'fsdp', [(i, (i + ahead * team) % count) for i in range(c...  329 us
    reduce_scatter x4, waiting for transfers between devices, scatter(): lax.psum_scatter(v, 'fsdp', scatter_dimension=0, tiled=True, axis_index_g...  182 us
    all_gather x4, waiting for transfers between devices, gather(): lax.all_gather(v, 'fsdp', axis=0, tiled=True, axis_index_groups=groups)  53.3 us
    all_gather x1, blocking collectives, local(): small = lax.all_gather(small, 'fsdp', axis=0)  51.3 us
    all_to_all x1, blocking collectives, exchange(): return lax.all_to_all(v, 'fsdp', 0, 0, tiled=True, axis_index_groups=groups)  47.7 us
    dot_general x4, matrix products, times_t(): lax.dot_general(left, right, (((1,), (1,)), ((), ())), preferred_element_...  38.8 us
    dot_general x4, matrix products, t_times(): lax.dot_general(left, right, (((0,), (0,)), ((), ())), preferred_element_...  33.2 us
    dot_general x4, matrix products, matmul(): return jnp.dot(left, right, preferred_element_type=jnp.float32)  32.8 us
  transfers between devices with their start and end apart: 20, of which 9 were waited for; matrix products, arithmetic and copies ran while one was open for 12% of the time, Pallas kernels for 0%

profile of v1, /device:TPU:0, one launch (start us, length us, event | category | flops | bytes accessed | tf_op | source)
XLA Modules:
  0.0 1046.9 jit_solution(15451732365698274430)
XLA Ops:
  18.9 4.8 all-to-all-start
  23.9 51.3 %all-gather.1 = f32[32,1,384]{2,1,0:T(1,128)S(1)} all-gather(f32[1,1,384]{2,1,0:T(1,128)S(1)} %reshape.372), channel_id=2, replica_groups=mesh['fsdp'=32] {'fsdp'}, dimensions={0}, use_global_device_ids=true | all-gather | bytes 50688 | tf_op jit(solution)/shard_map/all_gather | solution.py:176
  77.1 5.4 fusion.7
  83.2 33.1 %collective-permute-done = bf16[1024,384]{1,0:T(8,128)(2,1)} collective-permute-done((bf16[1024,384]{1,0:T(8,128)(2,1)S(1)}, bf16[1024,384]{1,0:T(8,128)(2,1)}, u32[]{:S(2)}, u32[]{:S(2)}) %collective-permute-start) | collective-permute-done | bytes 786464 | tf_op jit(solution)/shard_map/ppermute | solution.py:130
  117.7 5.7 fusion.2
  130.7 14.6 %select_reduce_fusion = (f32[2,2048]{1,0:T(2,128)S(1)}, f32[2,2048,2048]{1,2,0:T(8,128)}) fusion(pred[2048,2048]{0,1:T(8,128)(4,1)S(1)} %copy-done, bf16[2,2048,64]{1,2,0:T(8,128)(2,1)S(1)} %bitcast.212, bf16[2,2048,64]{1,2,0:T(8,128)(2,1)S(1)} %bitcast.186), kind=kOutput, calls=%fused_computation.5 | convolution fusion | flops 1098903552 | bytes 38813696 | tf_op jit(solution)/shard_map/hqd,hkd->hqk/dot_general | solution.py:65
  145.3 14.6 %fusion = f32[2,2048]{1,0:T(2,128)S(1)} fusion(f32[2,2048,2048]{1,2,0:T(8,128)} %get-tuple-element.50, f32[2,2048]{1,0:T(2,128)S(1)} %get-tuple-element.49, pred[2048,2048]{0,1:T(8,128)(4,1)S(1)} %copy-done), kind=kLoop, calls=%fused_computation.6 | loop fusion | flops 33550336 | bytes 37781504 | tf_op jit(solution)/shard_map/reduce_sum | solution.py:69
  159.9 15.9 %fusion.24 = bf16[2,2048,64]{1,2,0:T(8,128)(2,1)S(1)} fusion(bf16[2,2048,64]{1,2,0:T(8,128)(2,1)S(1)} %bitcast.205, f32[2,2048,2048]{1,2,0:T(8,128)} %get-tuple-element.50, f32[2,2048]{1,0:T(2,128)S(1)} %fusion, f32[2,2048]{1,0:T(2,128)S(1)} %get-tuple-element.49, pred[2048,2048]{0,1:T(8,128)(4,1)} %fusion.7), kind=kOutput, calls=%fused_computation.43 | convolution fusion | flops 1115947008 | bytes 38830080 | tf_op jit(solution)/shard_map/hqk,hkd->hqd/dot_general | solution.py:71
  175.9 5.6 bitcast_convert_fusion
  181.7 88.5 %reduce-scatter.5.cloned.1.call-done = bf16[128,2048]{1,0:T(8,128)(2,1)} async-done(((bf16[2048,2048]{1,0:T(8,128)(2,1)}), bf16[128,2048]{1,0:T(8,128)(2,1)}) %reduce-scatter.5.cloned.1.call-update) | async-done | bytes 524304 | tf_op jit(solution)/shard_map/reduce_scatter | solution.py:122
  282.2 47.7 %all_to_all.25 = bf16[16,64,1024]{2,1,0:T(8,128)(2,1)S(1)} all-to-all(bf16[16,64,1024]{2,1,0:T(8,128)(2,1)S(1)} %pad_maximum_fusion.3), channel_id=1, replica_groups={{0,1,2,3,4,5,6,7,8,9,10,11,12,13,14,15},{16,17,18,19,20,21,22,23,24,25,..., dimensions={0} | all-to-all | bytes 4194304 | tf_op jit(solution)/shard_map/all_to_all | solution.py:127
  333.2 135.2 %collective-permute-done.3 = bf16[256,2048]{1,0:T(8,128)(2,1)S(1)} collective-permute-done((bf16[256,2048]{1,0:T(8,128)(2,1)S(1)}, bf16[256,2048]{1,0:T(8,128)(2,1)S(1)}, u32[]{:S(2)}, u32[]{:S(2)}) %collective-permute-start.3) | collective-permute-done | bytes 1048608 | tf_op jit(solution)/shard_map/ppermute | solution.py:130
  474.2 14.7 %fusion.60 = f32[2048,1024]{0,1:T(8,128)} fusion(bf16[2048,2048]{1,0:T(8,128)(2,1)} %all-gather.9.cloned.1.call-done, bf16[2048,1024]{1,0:T(8,128)(2,1)} %bitcast.26), kind=kOutput, calls=%fused_computation.146 | convolution fusion | flops 8589934592 | bytes 20971520 | tf_op jit(solution)/shard_map/dot_general | solution.py:31
  489.0 11.6 %fusion.14 = (bf16[2048,512]{0,1:T(8,128)(2,1)S(1)}, bf16[2048,512]{0,1:T(8,128)(2,1)S(1)}, bf16[2048,512]{0,1:T(8,128)(2,1)}) fusion(f32[2048,1024]{0,1:T(8,128)} %fusion.60, bf16[512,2048]{1,0:T(8,128)(2,1)S(1)} %bitcast.208, bf16[2048,2048]{1,0:T(8,128)(2,1)} %all-gather.11.cloned.1.call-done), kind=kOutput, calls=%fused_computation.30 | convolution fusion | flops 4309647360 | bytes 25165824 | tf_op jit(solution)/shard_map/dot_general | solution.py:35
  502.6 13.5 %convolution_convert_fusion.1 = bf16[2048,2048]{1,0:T(8,128)(2,1)} fusion(bf16[2048,1024]{1,0:T(8,128)(2,1)} %bitcast.26, bf16[2048,512]{0,1:T(8,128)(2,1)S(1)} %get-tuple-element.17, bf16[2048,512]{0,1:T(8,128)(2,1)S(1)} %get-tuple-element.16), kind=kOutput, calls=%fused_computation.22 | convolution fusion | flops 8602517504 | bytes 16777216 | tf_op jit(solution)/shard_map/dot_general | solution.py:35
  516.1 93.2 %reduce-scatter.9.cloned.1.call-done = bf16[128,2048]{1,0:T(8,128)(2,1)} async-done(((bf16[2048,2048]{1,0:T(8,128)(2,1)}), bf16[128,2048]{1,0:T(8,128)(2,1)}) %reduce-scatter.9.cloned.1.call-update) | async-done | bytes 524304 | tf_op jit(solution)/shard_map/reduce_scatter | solution.py:122
  613.9 53.3 %all-gather.13.cloned.1.call-done = bf16[2048,2048]{1,0:T(8,128)(2,1)} async-done(((bf16[128,2048]{1,0:T(8,128)(2,1)}), bf16[2048,2048]{1,0:T(8,128)(2,1)}) %all-gather.13.cloned.1.call-update) | async-done | bytes 8388624 | tf_op jit(solution)/shard_map/all_gather | solution.py:119
  667.2 6.4 convolution_convert_fusion.3
  673.7 14.2 %fusion.21 = bf16[2,2048,64]{1,2,0:T(8,128)(2,1)S(1)} fusion(bf16[2,2048,64]{1,2,0:T(8,128)(2,1)S(1)} %bitcast.217, f32[2,2048,2048]{1,2,0:T(8,128)} %get-tuple-element.50, f32[2,2048]{1,0:T(2,128)S(1)} %log_add_fusion, pred[2048,2048]{0,1:T(8,128)(4,1)S(1)} %copy-done.1), kind=kOutput, calls=%fused_computation.41 | convolution fusion | flops 1107558400 | bytes 38813696 | tf_op jit(solution)/shard_map/hqk,hqd->hkd/dot_general | solution.py:85
  687.9 24.4 %multiply_reduce_fusion = (f32[2,2048]{1,0:T(2,128)S(1)}, f32[2,2048,2048]{1,2,0:T(8,128)}) fusion(f32[2,2048,2048]{1,2,0:T(8,128)} %get-tuple-element.50, f32[2,2048]{1,0:T(2,128)S(1)} %log_add_fusion, pred[2048,2048]{0,1:T(8,128)(4,1)S(1)} %copy-done.1, bf16[2,2048,64]{1,2,0:T(8,128)(2,1)S(1)} %bitcast.218, bf16[2,2048,64]{1,2,0:T(8,128)(2,1)S(1)} %bitcast.206), kind=kOutput, calls=%fused_computation.1 | convolution fusion | flops 1115680768 | bytes 72384512 | tf_op jit(solution)/shard_map/hqd,hkd->hqk/dot_general | solution.py:80
  712.3 29.6 %multiply_convert_fusion = bf16[2,2048,2048]{1,2,0:T(8,128)(2,1)} fusion(f32[2,2048,2048]{1,2,0:T(8,128)} %get-tuple-element.52, f32[2,2048,2048]{1,2,0:T(8,128)} %get-tuple-element.50, f32[2,2048]{1,0:T(2,128)S(1)} %get-tuple-element.51, f32[2,2048]{1,0:T(2,128)S(1)} %log_add_fusion, pred[2048,2048]{0,1:T(8,128)(4,1)} %fusion.7), kind=kLoop, calls=%fused_computation | loop fusion | flops 50331648 | bytes 88113152 | tf_op jit(solution)/shard_map/convert_element_type | solution.py:82
  741.9 10.8 %convolution_multiply_fusion.1 = f32[2,2048,64]{1,2,0:T(8,128)S(1)} fusion(bf16[2,2048,2048]{1,2,0:T(8,128)(2,1)} %multiply_convert_fusion, bf16[2,2048,64]{1,2,0:T(8,128)(2,1)S(1)} %bitcast.213), kind=kOutput, calls=%fused_computation.38 | convolution fusion | flops 1074003968 | bytes 18350080 | tf_op jit(solution)/shard_map/hqk,hqd->hkd/dot_general | solution.py:84
  757.3 7.3 convolution_convert_fusion
  766.1 8.4 convolution_convert_fusion.2
  776.1 12.1 %fusion.16 = f32[2048,1024]{1,0:T(8,128)S(1)} fusion(bf16[2048,2048]{1,0:T(8,128)(2,1)} %all-gather.9.cloned.1.call-done, bf16[2048,512]{0,1:T(8,128)(2,1)} %copy-done.53, bf16[2048,512]{0,1:T(8,128)(2,1)S(1)} %copy-done.52), kind=kOutput, calls=%fused_computation.36 | convolution fusion | flops 8598323200 | bytes 20971520 | tf_op jit(solution)/shard_map/dot_general | solution.py:41
  791.1 91.3 %collective-permute-done.6 = bf16[1024,1024]{1,0:T(8,128)(2,1)S(1)} collective-permute-done((bf16[1024,1024]{1,0:T(8,128)(2,1)S(1)}, bf16[1024,1024]{1,0:T(8,128)(2,1)S(1)}, u32[]{:S(2)}, u32[]{:S(2)}) %collective-permute-start.6) | collective-permute-done | bytes 2097184 | tf_op jit(solution)/shard_map/ppermute | solution.py:130
  888.4 7.7 fusion.61
  898.8 8.6 fusion.17
  908.1 36.4 %collective-permute-done.7 = bf16[256,2048]{1,0:T(8,128)(2,1)S(1)} collective-permute-done((bf16[256,2048]{1,0:T(8,128)(2,1)S(1)}, bf16[256,2048]{1,0:T(8,128)(2,1)S(1)}, u32[]{:S(2)}, u32[]{:S(2)}) %collective-permute-start.7) | collective-permute-done | bytes 1048608 | tf_op jit(solution)/shard_map/ppermute | solution.py:130
  946.0 32.9 %collective-permute-done.4 = bf16[1024,384]{1,0:T(8,128)(2,1)S(1)} collective-permute-done((bf16[1024,384]{1,0:T(8,128)(2,1)S(1)}, bf16[1024,384]{1,0:T(8,128)(2,1)S(1)}, u32[]{:S(2)}, u32[]{:S(2)}) %collective-permute-start.4) | collective-permute-done | bytes 786464 | tf_op jit(solution)/shard_map/ppermute | solution.py:130
  984.0 4.8 fusion.10
  1026.7 4.1 all-to-all-start.2
  (245 shorter events, 123.3 us)
Async XLA Ops:
  7.2 110.5 %all-gather.7.cloned.1.call-start = ((), (), s32[]{:S(2)}) async-start(), calls=%async_computation.9 | async-start | bytes 8912896 | tf_op jit(solution)/shard_map/all_gather | solution.py:119
  7.9 74.9 %collective-permute-start.1 = (bf16[64,2048]{1,0:T(8,128)(2,1)}, bf16[64,2048]{1,0:T(8,128)(2,1)S(1)}, u32[]{:S(2)}, u32[]{:S(2)}) collective-permute-start(bf16[64,2048]{1,0:T(8,128)(2,1)} %param.20), channel_id=1, source_target_pairs={{0,16},{1,17},{2,18},{3,19},{4,20},{5,21},{6,22},{7,23},{8,24},{9,... | collective-permute-start | bytes 786440 | tf_op jit(solution)/shard_map/ppermute | solution.py:130
  17.9 64.7 %copy-start.32 = (bf16[64,2048]{1,0:T(8,128)(2,1)S(1)}, bf16[64,2048]{1,0:T(8,128)(2,1)}, u32[]{:S(2)}) copy-start(bf16[64,2048]{1,0:T(8,128)(2,1)} %param.20) | copy-start | bytes 786436
  18.9 63.7 %all-to-all-start = ((bf16[16,64,384]{2,1,0:T(8,128)(2,1)}), bf16[16,64,384]{2,1,0:T(8,128)(2,1)S(1)}, u32[]{:S(2)}, u32[]{:S(2)}) async-start(bf16[16,64,384]{2,1,0:T(8,128)(2,1)} %pad_maximum_fusion.5), calls=%async_computation | async-start | bytes 1572864 | tf_op jit(solution)/shard_map/all_to_all | solution.py:127
  23.7 246.5 %reduce-scatter.5.cloned.1.call-start = ((), (), s32[]{:S(2)}) async-start(), calls=%async_computation.10 | async-start | bytes 8912896 | tf_op jit(solution)/shard_map/reduce_scatter | solution.py:122
  82.6 33.7 %collective-permute-start = (bf16[1024,384]{1,0:T(8,128)(2,1)S(1)}, bf16[1024,384]{1,0:T(8,128)(2,1)}, u32[]{:S(2)}, u32[]{:S(2)}) collective-permute-start(bf16[1024,384]{1,0:T(8,128)(2,1)S(1)} %bitcast.200), channel_id=1, source_target_pairs={{0,16},{1,17},{2,18},{3,19},{4,20},{5,21},{6,22},{7,23},{8,24},{9,... | collective-permute-start | bytes 2359304 | tf_op jit(solution)/shard_map/ppermute | solution.py:130
  82.9 93.0 %copy-start.20 = (bf16[2,64,2048]{2,1,0:T(8,128)(2,1)}, bf16[2,64,2048]{2,1,0:T(8,128)(2,1)S(1)}, u32[]{:S(2)}) copy-start(bf16[2,64,2048]{2,1,0:T(8,128)(2,1)S(1)} %bitcast_dynamic-update-slice_fusion.6) | copy-start | bytes 1572868
  181.5 88.7 %copy-start.3 = (bf16[128,2048]{1,0:T(8,128)(2,1)S(1)}, bf16[128,2048]{1,0:T(8,128)(2,1)}, u32[]{:S(2)}) copy-start(bf16[128,2048]{1,0:T(8,128)(2,1)} %param.13) | copy-start | bytes 1572868
  181.5 92.7 %copy-start.30 = (bf16[64,8192]{1,0:T(8,128)(2,1)S(1)}, bf16[64,8192]{1,0:T(8,128)(2,1)}, u32[]{:S(2)}) copy-start(bf16[64,8192]{1,0:T(8,128)(2,1)} %param.22) | copy-start | bytes 3145732
  181.6 292.7 %all-gather.9.cloned.1.call-start = ((), (), s32[]{:S(2)}) async-start(), calls=%async_computation.11 | async-start | bytes 8912896 | tf_op jit(solution)/shard_map/all_gather | solution.py:119
  181.7 429.8 %copy-start.33 = (f32[2048]{0:T(1024)}, f32[2048]{0:T(1024)S(1)}, u32[]{:S(2)}) copy-start(f32[2048]{0:T(1024)S(1)} %mul.328) | copy-start | bytes 24580
  271.5 340.0 %copy-start.38 = (f32[128]{0:T(128)}, f32[128]{0:T(128)S(1)}, u32[]{:S(2)}) copy-start(f32[128]{0:T(128)S(1)} %add_rsqrt_fusion.2) | copy-start | bytes 1540
  273.6 215.4 %all-gather.11.cloned.1.call-start = ((), (), s32[]{:S(2)}) async-start(), calls=%async_computation.13 | async-start | bytes 8912896 | tf_op jit(solution)/shard_map/all_gather | solution.py:119
  274.2 335.2 %reduce-scatter.9.cloned.1.call-start = ((), (), s32[]{:S(2)}) async-start(), calls=%async_computation.14 | async-start | bytes 8912896 | tf_op jit(solution)/shard_map/reduce_scatter | solution.py:122
  329.9 142.8 %collective-permute-start.2 = (bf16[1024,1024]{1,0:T(8,128)(2,1)S(1)}, bf16[1024,1024]{1,0:T(8,128)(2,1)S(1)}, u32[]{:S(2)}, u32[]{:S(2)}) collective-permute-start(bf16[1024,1024]{1,0:T(8,128)(2,1)S(1)} %bitcast.179), channel_id=1, source_target_pairs={{0,16},{1,17},{2,18},{3,19},{4,20},{5,21},{6,22},{7,23},{8,24},{9,... | collective-permute-start | bytes 6291464 | tf_op jit(solution)/shard_map/ppermute | solution.py:130
  332.8 135.6 %collective-permute-start.3 = (bf16[256,2048]{1,0:T(8,128)(2,1)S(1)}, bf16[256,2048]{1,0:T(8,128)(2,1)S(1)}, u32[]{:S(2)}, u32[]{:S(2)}) collective-permute-start(bf16[256,2048]{1,0:T(8,128)(2,1)S(1)} %copy-done.29), channel_id=1, source_target_pairs={{0,16},{1,17},{2,18},{3,19},{4,20},{5,21},{6,22},{7,23},{8,24},{9,... | collective-permute-start | bytes 3145736 | tf_op jit(solution)/shard_map/ppermute | solution.py:130
  516.1 93.3 %copy-start.5 = (bf16[128,2048]{1,0:T(8,128)(2,1)S(1)}, bf16[128,2048]{1,0:T(8,128)(2,1)}, u32[]{:S(2)}) copy-start(bf16[128,2048]{1,0:T(8,128)(2,1)} %reduce-scatter.5.cloned.1.call-done) | copy-start | bytes 1572868
  516.1 95.5 %copy-start.12 = (bf16[128,2048]{1,0:T(8,128)(2,1)S(1)}, bf16[128,2048]{1,0:T(8,128)(2,1)}, u32[]{:S(2)}) copy-start(bf16[128,2048]{1,0:T(8,128)(2,1)} %param.25) | copy-start | bytes 1572868
  516.1 151.1 %copy-start.21 = (bf16[2,64,2048]{2,1,0:T(8,128)(2,1)S(1)}, bf16[2,64,2048]{2,1,0:T(8,128)(2,1)}, u32[]{:S(2)}) copy-start(bf16[2,64,2048]{2,1,0:T(8,128)(2,1)} %copy-done.20) | copy-start | bytes 1572868
  516.1 151.1 %all-gather.13.cloned.1.call-start = ((), (), s32[]{:S(2)}) async-start(), calls=%async_computation.15 | async-start | bytes 8912896 | tf_op jit(solution)/shard_map/all_gather | solution.py:119
  611.5 55.7 %copy-start.42 = (f32[128]{0:T(128)}, f32[128]{0:T(128)S(1)}, u32[]{:S(2)}) copy-start(f32[128]{0:T(128)S(1)} %broadcast_multiply_fusion.1) | copy-start | bytes 1540
  613.9 410.5 %reduce-scatter.11.cloned.1.call-start = ((), (), s32[]{:S(2)}) async-start(), calls=%async_computation.16 | async-start | bytes 8912896 | tf_op jit(solution)/shard_map/reduce_scatter | solution.py:122
  687.9 68.4 %copy-start.49 = (bf16[2,2048,64]{1,2,0:T(8,128)(2,1)}, bf16[2,2048,64]{1,2,0:T(8,128)(2,1)S(1)}, u32[]{:S(2)}) copy-start(bf16[2,2048,64]{1,2,0:T(8,128)(2,1)S(1)} %fusion.21) | copy-start | bytes 1572868
  764.6 266.2 %reduce-scatter.7.cloned.1.call-start = ((), (), s32[]{:S(2)}) async-start(), calls=%async_computation.12 | async-start | bytes 8912896 | tf_op jit(solution)/shard_map/reduce_scatter | solution.py:122
  788.6 93.8 %collective-permute-start.6 = (bf16[1024,1024]{1,0:T(8,128)(2,1)S(1)}, bf16[1024,1024]{1,0:T(8,128)(2,1)S(1)}, u32[]{:S(2)}, u32[]{:S(2)}) collective-permute-start(bf16[1024,1024]{1,0:T(8,128)(2,1)S(1)} %fusion.25), channel_id=1, source_target_pairs={{0,16},{1,17},{2,18},{3,19},{4,20},{5,21},{6,22},{7,23},{8,24},{9,... | collective-permute-start | bytes 6291464 | tf_op jit(solution)/shard_map/ppermute | solution.py:130
  884.5 95.5 %all-to-all-start.4 = ((bf16[16,64,1024]{2,1,0:T(8,128)(2,1)}), bf16[16,64,1024]{2,1,0:T(8,128)(2,1)S(1)}, u32[]{:S(2)}, u32[]{:S(2)}) async-start(bf16[16,64,1024]{2,1,0:T(8,128)(2,1)} %bitcast.185), calls=%async_computation.8 | async-start | bytes 4194304 | tf_op jit(solution)/shard_map/all_to_all | solution.py:127
  896.3 48.2 %collective-permute-start.7 = (bf16[256,2048]{1,0:T(8,128)(2,1)S(1)}, bf16[256,2048]{1,0:T(8,128)(2,1)S(1)}, u32[]{:S(2)}, u32[]{:S(2)}) collective-permute-start(bf16[256,2048]{1,0:T(8,128)(2,1)S(1)} %fusion.42), channel_id=1, source_target_pairs={{0,16},{1,17},{2,18},{3,19},{4,20},{5,21},{6,22},{7,23},{8,24},{9,... | collective-permute-start | bytes 3145736 | tf_op jit(solution)/shard_map/ppermute | solution.py:130
  907.5 76.5 %copy-start.15 = (bf16[2,2048,64]{1,2,0:T(8,128)(2,1)S(1)}, bf16[2,2048,64]{1,2,0:T(8,128)(2,1)}, u32[]{:S(2)}) copy-start(bf16[2,2048,64]{1,2,0:T(8,128)(2,1)} %copy-done.14) | copy-start | bytes 1572868
  907.5 71.4 %collective-permute-start.4 = (bf16[1024,384]{1,0:T(8,128)(2,1)S(1)}, bf16[1024,384]{1,0:T(8,128)(2,1)S(1)}, u32[]{:S(2)}, u32[]{:S(2)}) collective-permute-start(bf16[1024,384]{1,0:T(8,128)(2,1)S(1)} %fusion.44), channel_id=1, source_target_pairs={{0,16},{1,17},{2,18},{3,19},{4,20},{5,21},{6,22},{7,23},{8,24},{9,... | collective-permute-start | bytes 2359304 | tf_op jit(solution)/shard_map/ppermute | solution.py:130
  980.0 32.9 %all-to-all-start.3 = ((bf16[16,64,384]{2,1,0:T(8,128)(2,1)}), bf16[16,64,384]{2,1,0:T(8,128)(2,1)S(1)}, u32[]{:S(2)}, u32[]{:S(2)}) async-start(bf16[16,64,384]{2,1,0:T(8,128)(2,1)} %bitcast.202), calls=%async_computation.7 | async-start | bytes 1572864 | tf_op jit(solution)/shard_map/all_to_all | solution.py:127
  988.9 23.2 %collective-permute-start.5 = (bf16[64,2048]{1,0:T(8,128)(2,1)S(1)}, bf16[64,2048]{1,0:T(8,128)(2,1)S(1)}, u32[]{:S(2)}, u32[]{:S(2)}) collective-permute-start(bf16[64,2048]{1,0:T(8,128)(2,1)S(1)} %fusion.47), channel_id=1, source_target_pairs={{0,16},{1,17},{2,18},{3,19},{4,20},{5,21},{6,22},{7,23},{8,24},{9,... | collective-permute-start | bytes 786440 | tf_op jit(solution)/shard_map/ppermute | solution.py:130
  1026.7 11.3 %all-to-all-start.2 = ((f32[32,1,128]{2,1,0:T(1,128)}), f32[32,1,128]{2,1,0:T(1,128)S(1)}, u32[]{:S(2)}, u32[]{:S(2)}) async-start(f32[32,1,128]{2,1,0:T(1,128)} %reshape.378), calls=%async_computation.6 | async-start | bytes 32768 | tf_op jit(solution)/shard_map/all_to_all | solution.py:251
  (42 other events, 488.4 us)
Sparse Core Ops, SparseCore 0:
  9.6 64.1 all-gather.6
  181.7 88.4 reduce-scatter.4
  273.7 91.0 all-gather.8
  366.2 85.3 all-gather.10
  516.2 93.1 reduce-scatter.8
  614.0 53.1 all-gather.12
  764.7 128.0 reduce-scatter.10
  895.0 135.2 reduce-scatter.6

commit v2 on v1

v2 whole, which is shorter than its diff:
```python
import functools

import jax
import jax.numpy as jnp
from jax import lax
from jax.experimental import pallas as pl
from jax.experimental.pallas import tpu as pltpu
from jax.sharding import PartitionSpec as P

HEADS = 32
HEAD_DIM = 64
SEQ = 2048
DOCS = 16


EPS = 1e-05
THETA = 130000.0
HIDE = -1e30
BF = jnp.bfloat16
F32 = jnp.float32
LANES = 2 * HEAD_DIM
HALF = HEAD_DIM // 2
BLOCK = 512
VMEM = 56 * 2**20


def barrier(*values):
    return lax.optimization_barrier(values)


def norm_rows(v, gain):
    scale = lax.rsqrt(jnp.mean(v * v, axis=-1, keepdims=True) + EPS)
    return v * scale * gain


def norm_back(v, gain, grad):
    scale = lax.rsqrt(jnp.mean(v * v, axis=-1, keepdims=True) + EPS)
    hat = v * scale
    weighted = gain * grad
    back = scale * (weighted - hat * jnp.mean(hat * weighted, axis=-1, keepdims=True))
    return back, jnp.sum(grad * hat, axis=0)


def matmul(left, right):
    return jnp.dot(left, right, preferred_element_type=F32)


def times_t(left, right):
    return lax.dot_general(left, right, (((1,), (1,)), ((), ())), preferred_element_type=F32)


def t_times(left, right):
    return lax.dot_general(left, right, (((0,), (0,)), ((), ())), preferred_element_type=F32)


def lane_index(shape):
    return lax.broadcasted_iota(jnp.int32, shape, len(shape) - 1)


def of_head(head, shape):
    return lane_index(shape) // HALF % 2 == head


def value_of_head(head, shape):
    return lane_index(shape) // HEAD_DIM == head


def parts_of(v):
    high = v.astype(BF)
    rest = v - high.astype(F32)
    mid = rest.astype(BF)
    return high, mid, (rest - mid.astype(F32)).astype(BF)


def in_lanes(columns, first, shape):
    lane = lane_index(shape)
    out = jnp.zeros(shape, BF)
    for c, column in enumerate(columns):
        out = jnp.where(lane == first + c, column, out)
    return out


def forward_kernel(subs, offsets, qkv, cosine, sine, q_mask, k_mask, qe, ke, vs, out, out32):
    rows = sum(subs)
    blocks = SEQ // rows
    full = (SEQ, LANES)

    def place_block(b, carry):
        start = 0
        for r, sub in enumerate(subs):
            here = pl.ds(pl.multiple_of(offsets[r * blocks + b], 16), sub)
            there = pl.ds(pl.multiple_of(b * rows + start, 16), sub)
            start += sub
            c, s = cosine[there, :], sine[there, :]
            for at, ends in ((0, qe), (1, ke)):
                v = qkv[here, at * LANES : (at + 1) * LANES]
                turned = (v * c + pltpu.roll(v, HEAD_DIM, 1) * s).astype(BF)
                if at == 0:
                    turned = turned * (HEAD_DIM**-0.5)
                mask = (q_mask, k_mask)[at][there, :]
                for head in range(2):
                    ends[head, there, :] = jnp.where(of_head(head, turned.shape), turned, mask)
            vs[there, :] = qkv[here, 2 * LANES :].astype(BF)
        return carry

    lax.fori_loop(0, blocks, place_block, 0)
    diagonal = lax.broadcasted_iota(jnp.int32, (BLOCK, BLOCK), 0) >= lane_index((BLOCK, BLOCK))
    shape = (BLOCK, LANES)
    for i in range(SEQ // BLOCK):
        mine = slice(i * BLOCK, (i + 1) * BLOCK)
        outs = []
        for head in range(2):
            query = qe[head, mine, :]
            scores = []
            for j in range(i + 1):
                s = times_t(query, ke[head, j * BLOCK : (j + 1) * BLOCK, :])
                scores.append(jnp.where(diagonal, s, HIDE) if j == i else s)
            top = functools.reduce(jnp.maximum, scores)
            top = jnp.max(top, axis=1, keepdims=True)
            total = jnp.zeros(shape, F32)
            for j, s in enumerate(scores):
                probs = jnp.exp(s - top).astype(BF)
                value = vs[j * BLOCK : (j + 1) * BLOCK, :]
                value = jnp.where(value_of_head(head, shape), value, jnp.ones((), BF))
                total += matmul(probs, value)
            spare = (1 - head) * HEAD_DIM
            weight = total[:, spare : spare + 1]
            outs.append(total / weight)
            logsum = top + jnp.log(weight)
            first = HEAD_DIM + (1 - head) * HALF
            extra = in_lanes(parts_of(-logsum), first, shape)
            qe[head, mine, :] = query + extra
        out32[mine, :] = jnp.where(value_of_head(0, shape), outs[0], outs[1])

    def send_block(b, carry):
        start = 0
        for r, sub in enumerate(subs):
            here = pl.ds(pl.multiple_of(offsets[r * blocks + b], 16), sub)
            there = pl.ds(pl.multiple_of(b * rows + start, 16), sub)
            start += sub
            out[here, :] = out32[there, :].astype(BF)
        return carry

    lax.fori_loop(0, blocks, send_block, 0)


def backward_kernel(subs, offsets, qe, ke, vs, out32, dout, cosine, sine, grads, de, dq, dk, dv):
    rows = sum(subs)
    blocks = SEQ // rows

    def place_block(b, carry):
        start = 0
        for r, sub in enumerate(subs):
            here = pl.ds(pl.multiple_of(offsets[r * blocks + b], 16), sub)
            there = pl.ds(pl.multiple_of(b * rows + start, 16), sub)
            start += sub
            grad = dout[here, :]
            weighted = grad.astype(F32) * out32[there, :]
            shape = grad.shape
            for head in range(2):
                own = value_of_head(head, shape)
                delta = jnp.sum(jnp.where(own, weighted, 0.0), axis=1, keepdims=True)
                extra = in_lanes(parts_of(-delta), (1 - head) * HEAD_DIM, shape)
                de[head, there, :] = jnp.where(own, grad, extra)
        return carry

    lax.fori_loop(0, blocks, place_block, 0)
    shape = (BLOCK, LANES)
    diagonal = lax.broadcasted_iota(jnp.int32, (BLOCK, BLOCK), 0) <= lane_index((BLOCK, BLOCK))
    lane = lane_index(shape)
    for head in range(2):
        spare = (1 - head) * HEAD_DIM
        ones = jnp.where((lane >= spare) & (lane < spare + 3), jnp.ones((), BF), jnp.zeros((), BF))
        for j in range(SEQ // BLOCK):
            theirs = slice(j * BLOCK, (j + 1) * BLOCK)
            key = ke[head, theirs, :]
            value = jnp.where(value_of_head(head, shape), vs[theirs, :], ones)
            dkey = jnp.zeros(shape, F32)
            dvalue = jnp.zeros(shape, F32)
            for i in range(j, SEQ // BLOCK):
                mine = slice(i * BLOCK, (i + 1) * BLOCK)
                query = qe[head, mine, :]
                grad = de[head, mine, :]
                probs = jnp.exp(times_t(key, query))
                if i == j:
                    probs = jnp.where(diagonal, probs, 0.0)
                dscore = (probs * times_t(value, grad)).astype(BF)
                dvalue += matmul(probs.astype(BF), grad)
                dkey += matmul(dscore, query)
                dquery = t_times(dscore, key)
                if j > 0:
                    dquery += dq[head, mine, :]
                dq[head, mine, :] = dquery
            dk[head, theirs, :] = dkey
            dv[head, theirs, :] = dvalue

    def send_block(b, carry):
        start = 0
        for r, sub in enumerate(subs):
            here = pl.ds(pl.multiple_of(offsets[r * blocks + b], 16), sub)
            there = pl.ds(pl.multiple_of(b * rows + start, 16), sub)
            start += sub
            c, s = cosine[there, :], sine[there, :]
            first = of_head(0, (sub, LANES))
            query = jnp.where(first, dq[0, there, :], dq[1, there, :]) * (HEAD_DIM**-0.5)
            key = jnp.where(first, dk[0, there, :], dk[1, there, :])
            for at, v in ((0, query), (1, key)):
                turned = v * c - pltpu.roll(v, HEAD_DIM, 1) * s
                grads[here, at * LANES : (at + 1) * LANES] = turned.astype(BF)
            value = jnp.where(value_of_head(0, (sub, LANES)), dv[0, there, :], dv[1, there, :])
            grads[here, 2 * LANES :] = value.astype(BF)
        return carry

    lax.fori_loop(0, blocks, send_block, 0)


def attend_forward(subs, offsets, qkv, cosine, sine, q_mask, k_mask):
    like = jax.ShapeDtypeStruct
    smem = pl.BlockSpec(memory_space=pltpu.SMEM)
    vmem = pl.BlockSpec(memory_space=pltpu.VMEM)
    return pl.pallas_call(
        functools.partial(forward_kernel, subs),
        out_shape=[
            like((2, SEQ, LANES), BF),
            like((2, SEQ, LANES), BF),
            like((SEQ, LANES), BF),
            like((SEQ, LANES), BF),
            like((SEQ, LANES), F32),
        ],
        in_specs=[smem] + [vmem] * 5,
        out_specs=[vmem] * 5,
        compiler_params=pltpu.CompilerParams(vmem_limit_bytes=VMEM),
        cost_estimate=pl.CostEstimate(
            flops=8 * SEQ * SEQ * LANES, bytes_accessed=12 * 2**20, transcendentals=SEQ * SEQ
        ),
    )(offsets, qkv, cosine, sine, q_mask, k_mask)


def attend_backward(subs, offsets, qe, ke, vs, out32, dout, cosine, sine):
    smem = pl.BlockSpec(memory_space=pltpu.SMEM)
    vmem = pl.BlockSpec(memory_space=pltpu.VMEM)
    return pl.pallas_call(
        functools.partial(backward_kernel, subs),
        out_shape=jax.ShapeDtypeStruct((SEQ, 3 * LANES), BF),
        in_specs=[smem] + [vmem] * 7,
        out_specs=vmem,
        scratch_shapes=[
            pltpu.VMEM((2, SEQ, LANES), BF),
            pltpu.VMEM((2, SEQ, LANES), F32),
            pltpu.VMEM((2, SEQ, LANES), F32),
            pltpu.VMEM((2, SEQ, LANES), F32),
        ],
        compiler_params=pltpu.CompilerParams(vmem_limit_bytes=VMEM),
        cost_estimate=pl.CostEstimate(
            flops=20 * SEQ * SEQ * LANES, bytes_accessed=12 * 2**20, transcendentals=SEQ * SEQ
        ),
    )(offsets, qe, ke, vs, out32, dout, cosine, sine)


class Team:
    def __init__(self, rows, count):
        self.rows, self.count = rows, count
        self.size = SEQ // rows
        self.teams = count // self.size
        axes = [2 << k for k in range(self.size.bit_length() - 2)]
        self.rails = [tuple(axes[r:] + axes[:r]) for r in range(len(axes))]
        share = rows // (8 * 16) * 16
        self.subs = [2 * share] + [3 * share] * (len(axes) - 1)
        self.subs[-1] += rows - sum(self.subs)

    def flip(self, v, mask):
        return lax.ppermute(v, "fsdp", [(i, i ^ mask) for i in range(self.count)])

    def ahead(self, v, teams):
        step = teams * self.size
        return lax.ppermute(v, "fsdp", [(i, (i + step) % self.count) for i in range(self.count)])

    def cut(self, v, times=1):
        out, start = [], 0
        for sub in self.subs:
            out.append(v[start : start + times * sub])
            start += times * sub
        return out

    def offsets(self, place):
        away = jnp.arange(self.size, dtype=jnp.int32) ^ place
        out, start = [], 0
        for rail, sub in zip(self.rails, self.subs):
            at = (away & 1) * (SEQ // 2) + start * (self.size // 2)
            for k, mask in enumerate(rail):
                at = at + jnp.where(away & mask != 0, sub << k, 0)
            out.append(at)
            start += sub
        return jnp.concatenate(out).astype(jnp.int32)

    def gather(self, v):
        held = self.cut(v)
        steps = len(self.rails[0])
        for s in range(steps - 1):
            got = barrier(*[self.flip(h, rail[s]) for h, rail in zip(held, self.rails)])
            held = barrier(*[jnp.concatenate([h, g]) for h, g in zip(held, got)])
        last = [self.flip(h, rail[-1]) for h, rail in zip(held, self.rails)]
        low = [self.flip(h, 1) for h in held]
        got = barrier(*last, *low)
        last, low = got[: len(last)], got[len(last) :]
        high = [self.flip(h, 1) for h in last]
        out = []
        for pair in zip(held, last):
            out.extend(pair)
        for pair in zip(low, high):
            out.extend(pair)
        return out

    def scatter(self, left, times):
        half = SEQ // 2
        chips = self.size // 2
        sent = [self.flip(times(c).astype(BF), 1) for c in self.cut(left[half:], chips)]
        kept = [times(c) for c in self.cut(left[:half], chips)]
        held = [k + s.astype(F32) for k, s in zip(kept, sent)]
        for step in reversed(range(len(self.rails[0]))):
            upper = barrier(*[h[h.shape[0] // 2 :].astype(BF) for h in held])
            got = barrier(*[self.flip(u, rail[step]) for u, rail in zip(upper, self.rails)])
            held = [h[: h.shape[0] // 2] + g.astype(F32) for h, g in zip(held, got)]
        return jnp.concatenate(held)


def local(
    tokens,
    segments,
    positions,
    gain_attn,
    w_query,
    w_key,
    w_value,
    w_out,
    gain_mlp,
    w_gate,
    w_up,
    w_down,
    cotangent,
):
    rows, width = tokens.shape
    count = lax.axis_size("fsdp")
    team = Team(rows, count)
    size, teams = team.size, team.teams
    index = lax.axis_index("fsdp")
    mine = index // size
    place = index % size
    groups = [[t * size + p for p in range(size)] for t in range(teams)]
    own = w_query.shape[0]
    whole_heads = own % HEAD_DIM == 0
    ff_own = w_down.shape[0]

    def exchange(v):
        return lax.all_to_all(v, "fsdp", 0, 0, tiled=True, axis_index_groups=groups)

    def across(v):
        held = jnp.zeros((teams,) + v.shape, v.dtype)
        held = lax.dynamic_update_index_in_dim(held, v, mine, 0)
        for step in range(1, teams):
            held = lax.dynamic_update_index_in_dim(
                held, team.ahead(v, step), (mine - step) % teams, 0
            )
        return held

    def sum_across(v):
        total = lax.dynamic_index_in_dim(v, mine, 0, keepdims=False)
        for step in range(1, teams):
            sent = lax.dynamic_index_in_dim(v, (mine + step) % teams, 0, keepdims=False)
            total = total + team.ahead(sent.astype(BF), step).astype(F32)
        return total

    def cut_ff(w):
        r, c = w.shape
        return w.reshape(r, teams, size, -1).transpose(2, 0, 1, 3).reshape(size, r, c // size)

    def join_ff(v):
        _, r, c = v.shape
        return v.reshape(size, r, teams, -1).transpose(1, 2, 0, 3).reshape(r, c * size)

    def cut_values(w):
        r, c = w.shape
        w = w.reshape((r, 2, size, -1) if whole_heads else (r, size, 2, -1))
        return w.transpose((2, 0, 1, 3) if whole_heads else (1, 0, 2, 3)).reshape(size, r, -1)

    def join_values(v):
        _, r, c = v.shape
        v = v.reshape(size, r, 2, -1)
        return v.transpose((1, 2, 0, 3) if whole_heads else (1, 0, 2, 3)).reshape(r, -1)

    def cut_turned(w):
        v = cut_values(w).reshape(size, -1, 2, 2, HALF)
        return v.transpose(0, 1, 3, 2, 4).reshape(size, -1, LANES)

    def join_turned(v):
        v = v.reshape(size, -1, 2, 2, HALF).transpose(0, 1, 3, 2, 4)
        return join_values(v.reshape(size, -1, LANES))

    def columns_of(cut):
        block = exchange(jnp.concatenate(cut, axis=2))
        return across(block.reshape(-1, block.shape[2])).reshape(-1, block.shape[2])

    def rows_of(grad, joins):
        grad = sum_across(grad.reshape(teams, -1, grad.shape[1])).astype(BF)
        got = exchange(grad.reshape(size, -1, grad.shape[1]))
        each = got.shape[2] // len(joins)
        return [
            join(got[:, :, i * each : (i + 1) * each]).astype(F32) for i, join in enumerate(joins)
        ]

    x_pieces = team.gather(tokens)
    small = jnp.concatenate([v.astype(F32) for v in (gain_attn, gain_mlp, segments, positions)])
    small = jnp.broadcast_to(small[None], (count, small.shape[0]))
    small = lax.all_to_all(small, "fsdp", 0, 0, tiled=True)
    gain_one = small[:, :own].reshape(1, -1)
    gain_two = small[:, own : 2 * own].reshape(1, -1)
    small = lax.dynamic_slice_in_dim(small, mine * size, size, 0)
    docs = small[:, 2 * own : 2 * own + rows].reshape(SEQ, 1)
    places = small[:, 2 * own + rows :].reshape(SEQ, 1)

    if whole_heads:
        out_rows = across(w_out).reshape(-1, width)
    else:
        out_rows = lax.dynamic_slice_in_dim(
            lax.all_gather(w_out, "fsdp", axis=0, tiled=True), place * LANES, LANES
        )
    w_qkv = columns_of([cut_turned(w_query), cut_turned(w_key), cut_values(w_value)])

    freqs = THETA ** (-jnp.arange(HALF, dtype=F32) * 2.0 / HEAD_DIM)
    angles = places * freqs[None, :]
    cosine, sine = jnp.cos(angles), jnp.sin(angles)
    cosine = jnp.concatenate([cosine] * 4, axis=1)
    sine = jnp.concatenate([-sine, -sine, sine, sine], axis=1)
    lane = jnp.arange(LANES)[None, :]
    number = (lane % HALF).astype(F32)
    carries = (lane < HEAD_DIM) & (lane % HALF < DOCS)
    q_mask = jnp.where(carries & (docs != number), HIDE, 0.0).astype(BF)
    tail = (lane >= HEAD_DIM) & (lane % HALF < 3)
    k_mask = jnp.where((carries & (docs == number)) | tail, 1.0, 0.0).astype(BF)
    offsets = team.offsets(place)
    subs = tuple(team.subs)

    h1 = jnp.concatenate([norm_rows(p.astype(F32), gain_one).astype(BF) for p in x_pieces])
    qkv = matmul(h1, w_qkv)
    qe, ke, vs, out, out32 = attend_forward(subs, offsets, qkv, cosine, sine, q_mask, k_mask)
    w_gu = columns_of([cut_ff(w_gate), cut_ff(w_up)])
    dy = jnp.concatenate(team.gather(cotangent))
    down_rows = across(w_down).reshape(-1, width)
    x = tokens.astype(F32)
    x2 = x + team.scatter(out, lambda v: matmul(v, out_rows))
    h2 = jnp.concatenate(team.gather(norm_rows(x2, gain_two).astype(BF)))
    gu = matmul(h2, w_gu)
    hidden = gu.shape[1] // 2
    gate, up = gu[:, :hidden], gu[:, hidden:]
    sig = jax.nn.sigmoid(gate)
    silu = gate * sig
    mixed = (silu * up).astype(BF)
    dm = times_t(dy, down_rows)
    dgate = (dm * up * (sig + silu * (1.0 - sig))).astype(BF)
    dup = (dm * silu).astype(BF)
    dgu = jnp.concatenate([dgate, dup], axis=1)
    dh2 = team.scatter(dgu, lambda v: times_t(v, w_gu))
    result = (x2 + team.scatter(mixed, lambda v: matmul(v, down_rows))).astype(BF)
    grad_gate, grad_up = rows_of(t_times(h2, dgu), [join_ff, join_ff])
    grad_down = sum_across(t_times(mixed, dy).reshape(teams, ff_own, width))

    back, gain_two_part = norm_back(x2, gain_two, dh2)
    dx2 = cotangent.astype(F32) + back
    da = jnp.concatenate(team.gather(dx2.astype(BF)))
    dout = times_t(da, out_rows).astype(BF)
    grad_out = t_times(out, da)
    if whole_heads:
        grad_out = sum_across(grad_out.reshape(teams, own, width))
    else:
        grad_out = lax.psum(grad_out, "fsdp", axis_index_groups=[list(t) for t in zip(*groups)])
        grad_out = lax.all_gather(grad_out, "fsdp", axis=0, tiled=True, axis_index_groups=groups)
        grad_out = lax.dynamic_slice_in_dim(grad_out, index * own, own)
    dqkv = attend_backward(subs, offsets, qe, ke, vs, out32, dout, cosine, sine)
    dh1 = team.scatter(dqkv, lambda v: times_t(v, w_qkv))
    grad_query, grad_key, grad_value = rows_of(
        t_times(h1, dqkv), [join_turned, join_turned, join_values]
    )
    back, gain_one_part = norm_back(x, gain_one, dh1)
    grad_tokens = dx2 + back
    gains = jnp.stack([gain_one_part, gain_two_part]).reshape(2, count, own).transpose(1, 0, 2)
    gains = jnp.sum(lax.all_to_all(gains, "fsdp", 0, 0, tiled=True), axis=0)
    return (
        result,
        grad_tokens,
        gains[0],
        grad_query,
        grad_key,
        grad_value,
        grad_out,
        gains[1],
        grad_gate,
        grad_up,
        grad_down,
    )


def solution(mesh):
    flat = P("fsdp")
    wide = P("fsdp", None)
    return jax.shard_map(
        local,
        mesh=mesh,
        in_specs=(wide, flat, flat, flat, wide, wide, wide, wide, flat, wide, wide, wide, wide),
        out_specs=(wide, wide, flat, wide, wide, wide, wide, flat, wide, wide, wide),
        check_vma=False,
    )
```

time: 1050 us -> 802 us (0.76)
  waiting for transfers between devices: 569 us -> 358 us
  blocking collectives: 99 us -> 0 us
  starting transfers between devices: 33.3 us -> 128 us
  matrix products: 188 us -> 101 us
  Pallas kernels: 0 us -> 37.6 us
  local copies, waits for them, and re-layouts: 59.1 us -> 84.5 us
  between operations: 15.6 us -> 3.13 us
    reduce_scatter x4 -> x0, waiting for transfers between devices: 182 us -> none  [scatter(): lax.psum_scatter(v, 'fsdp', scatter_dimension=0, tiled=True, axis_index_g...]
    ppermute x8 -> x116, starting transfers between devices: 16.1 us -> 104 us  [the longest x108 96 us: flip(): return lax.ppermute(v, 'fsdp', [(i, i ^ mask) for i in range(self.count)])]
    dot_general x10 -> x14, matrix products: 116 us -> 31 us  [matmul(): return jnp.dot(left, right, preferred_element_type=F32)]
    all_gather x4 -> x0, waiting for transfers between devices: 53.3 us -> none  [gather(): lax.all_gather(v, 'fsdp', axis=0, tiled=True, axis_index_groups=groups)]
    all_gather x1 -> x0, blocking collectives: 51.3 us -> none  [local(): small = lax.all_gather(small, 'fsdp', axis=0)]
    all_to_all x1 -> x0, blocking collectives: 47.7 us -> none  [exchange(): return lax.all_to_all(v, 'fsdp', 0, 0, tiled=True, axis_index_groups=groups)]
    pallas_call x0 -> x2, Pallas kernels: none -> 37.6 us  [the longest x1 23.1 us: attend_backward(): pl.pallas_call(functools.partial(backward_kernel, subs), out_shape=jax.Sh...]
    convert_element_type x9 -> x10, other arithmetic: 37.5 us -> 10.8 us  [the longest x2 4.42 us: rows_of(): join(got[:, :, i * each:(i + 1) * each]).astype(F32)]
  transfers between devices with their start and end apart: 20 -> 122, of which waited for: 9 -> 55; matrix products, arithmetic and copies ran while one was open for 12% -> 28% of each run, Pallas kernels for 0% -> 5%
where the time goes in v2:
time: 802 us; the launch traced here: 794 us
  waiting for transfers between devices  358 us (45%)
  starting transfers between devices  128 us (16%)
  matrix products  101 us (13%)
  local copies, waits for them, and re-layouts  84.5 us (11%)
  other arithmetic  81.4 us (10%)
  Pallas kernels  37.6 us (5%)
    ppermute x108, waiting for transfers between devices, flip(): return lax.ppermute(v, 'fsdp', [(i, i ^ mask) for i in range(self.count)])  197 us
    ppermute x8, waiting for transfers between devices, ahead(): lax.ppermute(v, 'fsdp', [(i, (i + step) % self.count) for i in range(self...  155 us
    ppermute x108, starting transfers between devices, flip(): return lax.ppermute(v, 'fsdp', [(i, i ^ mask) for i in range(self.count)])  96 us
    dot_general x14, matrix products, times_t(): lax.dot_general(left, right, (((1,), (1,)), ((), ())), preferred_element_...  39.5 us
    dot_general x14, matrix products, matmul(): return jnp.dot(left, right, preferred_element_type=F32)  31 us
    dot_general x4, matrix products, t_times(): lax.dot_general(left, right, (((0,), (0,)), ((), ())), preferred_element_...  30.5 us
    unnamed x155, local copies, waits for them, and re-layouts  29.2 us
    pallas_call x1, Pallas kernels, attend_backward(): pl.pallas_call(functools.partial(backward_kernel, subs), out_shape=jax.Sh...  23.1 us
  transfers between devices with their start and end apart: 122, of which 55 were waited for; matrix products, arithmetic and copies ran while one was open for 28% of the time, Pallas kernels for 5%

profile of v2, /device:TPU:0, one launch (start us, length us, event | category | flops | bytes accessed | tf_op | source)
XLA Modules:
  0.0 793.7 jit_solution(12439987086744003336)
XLA Ops:
  43.6 5.2 all-to-all-start.1
  49.6 4.4 fusion.89
  91.6 10.2 %collective-permute-done.6 = bf16[128,2048]{1,0:T(8,128)(2,1)} collective-permute-done((bf16[128,2048]{1,0:T(8,128)(2,1)S(1)}, bf16[128,2048]{1,0:T(8,128)(2,1)}, u32[]{:S(2)}, u32[]{:S(2)}) %collective-permute-start.6) | collective-permute-done | bytes 524320 | tf_op jit(solution)/shard_map/ppermute | solution.py:272
  104.2 4.4 collective-permute-done.7
  124.8 4.6 all-to-all-start.2
  143.2 43.1 %collective-permute-done.15 = bf16[1024,384]{1,0:T(8,128)(2,1)S(1)} collective-permute-done((bf16[1024,384]{1,0:T(8,128)(2,1)S(1)}, bf16[1024,384]{1,0:T(8,128)(2,1)S(1)}, u32[]{:S(2)}, u32[]{:S(2)}) %collective-permute-start.15) | collective-permute-done | bytes 786464 | tf_op jit(solution)/shard_map/ppermute | solution.py:276
  186.5 9.2 %fusion.119.qkv = f32[2048,384]{1,0:T(8,128)} fusion(bf16[2048,2048]{1,0:T(8,128)(2,1)} %fusion.55, bf16[2048,384]{1,0:T(8,128)(2,1)S(1)} %bitcast.165), kind=kOutput, calls=%fused_computation.387 | convolution fusion | flops 3221225472 | bytes 13107200 | tf_op jit(solution)/shard_map/dot_general | solution.py:45
  195.7 14.5 %shard_map.212 = (bf16[2,2048,128]{2,1,0:T(8,128)(2,1)}, bf16[2,2048,128]{2,1,0:T(8,128)(2,1)}, bf16[2048,128]{1,0:T(8,128)(2,1)}, bf16[2048,128]{1,0:T(8,128)(2,1)}, f32[2048,128]{1,0:T(8,128)}) custom-call(s32[48]{0:T(128)} %pad_add_fusion.offsets, f32[2048,384]{1,0:T(8,128)} %fusion.119.qkv, f32[2048,128]{1,0:T(8,128)} %get-tuple-element.352.cosine, ...), custom_call_target="tpu_custom_call" | custom-call | flops 4294967296 | bytes 12582912 | tf_op jit(solution)/shard_map/pallas_call | solution.py:221
  220.0 8.4 %collective-permute-done.64 = bf16[128,2048]{1,0:T(8,128)(2,1)S(1)} collective-permute-done((bf16[128,2048]{1,0:T(8,128)(2,1)S(1)}, bf16[128,2048]{1,0:T(8,128)(2,1)S(1)}, u32[]{:S(2)}, u32[]{:S(2)}) %collective-permute-start.64) | collective-permute-done | bytes 524320 | tf_op jit(solution)/shard_map/ppermute | solution.py:272
  232.1 5.1 collective-permute-done.65
  240.0 8.9 %collective-permute-done.66 = bf16[192,2048]{1,0:T(8,128)(2,1)S(1)} collective-permute-done((bf16[192,2048]{1,0:T(8,128)(2,1)S(1)}, bf16[192,2048]{1,0:T(8,128)(2,1)S(1)}, u32[]{:S(2)}, u32[]{:S(2)}) %collective-permute-start.66) | collective-permute-done | bytes 786464 | tf_op jit(solution)/shard_map/ppermute | solution.py:272
  253.4 9.9 %collective-permute-done.20 = bf16[128,2048]{1,0:T(8,128)(2,1)S(1)} collective-permute-done((bf16[128,2048]{1,0:T(8,128)(2,1)S(1)}, bf16[128,2048]{1,0:T(8,128)(2,1)S(1)}, u32[]{:S(2)}, u32[]{:S(2)}) %collective-permute-start.20) | collective-permute-done | bytes 524320 | tf_op jit(solution)/shard_map/ppermute | solution.py:272
  306.2 36.8 %collective-permute-done.33 = bf16[96,2048]{1,0:T(8,128)(2,1)S(1)} collective-permute-done((bf16[96,2048]{1,0:T(8,128)(2,1)S(1)}, bf16[96,2048]{1,0:T(8,128)(2,1)S(1)}, u32[]{:S(2)}, u32[]{:S(2)}) %collective-permute-start.33) | collective-permute-done | bytes 393248 | tf_op jit(solution)/shard_map/ppermute | solution.py:272
  349.6 29.0 %collective-permute-done.44 = bf16[1024,1024]{1,0:T(8,128)(2,1)S(1)} collective-permute-done((bf16[1024,1024]{1,0:T(8,128)(2,1)}, bf16[1024,1024]{1,0:T(8,128)(2,1)S(1)}, u32[]{:S(2)}, u32[]{:S(2)}) %collective-permute-start.44) | collective-permute-done | bytes 2097184 | tf_op jit(solution)/shard_map/ppermute | solution.py:276
  381.9 7.8 collective-permute-done.35
  399.3 12.2 %fusion.120 = f32[2048,1024]{0,1:T(8,128)S(1)} fusion(bf16[2048,2048]{1,0:T(8,128)(2,1)} %copy-done.55, bf16[2048,1024]{1,0:T(8,128)(2,1)S(1)} %bitcast.158), kind=kOutput, calls=%fused_computation.388 | convolution fusion | flops 8589934592 | bytes 20971520 | tf_op jit(solution)/shard_map/dot_general | solution.py:45
  411.5 9.8 %multiply_convert_fusion.1 = (bf16[2048,512]{0,1:T(8,128)(2,1)S(1)}, bf16[2048,512]{0,1:T(8,128)(2,1)S(1)}, bf16[2048,512]{0,1:T(8,128)(2,1)S(1)}) fusion(f32[2048,1024]{0,1:T(8,128)S(1)} %fusion.120, bf16[2048,2048]{1,0:T(8,128)(2,1)} %constant_dynamic-update-slice_fusion.12, bf16[512,2048]{1,0:T(8,128)(2,1)S(1)} %bitcast.172), kind=kOutput, calls=%fused_computation.8 | convolution fusion | flops 4309647360 | bytes 25165824 | tf_op jit(solution)/shard_map/dot_general | solution.py:49
  445.5 7.0 collective-permute-done.49
  452.8 4.4 collective-permute-done.50
  460.1 7.3 collective-permute-done.76
  467.7 6.4 collective-permute-done.77
  513.2 7.0 fusion.123
  521.9 11.8 %fusion = f32[2048,1024]{1,0:T(8,128)S(1)} fusion(bf16[2048,2048]{1,0:T(8,128)(2,1)} %copy-done.55, bf16[2048,512]{0,1:T(8,128)(2,1)S(1)} %get-tuple-element.318, bf16[2048,512]{0,1:T(8,128)(2,1)S(1)} %get-tuple-element.317), kind=kOutput, calls=%fused_computation | convolution fusion | flops 8598323200 | bytes 20971520 | tf_op jit(solution)/shard_map/dot_general | solution.py:53
  535.9 25.8 %collective-permute-done.115 = bf16[256,2048]{1,0:T(8,128)(2,1)S(1)} collective-permute-done((bf16[256,2048]{1,0:T(8,128)(2,1)S(1)}, bf16[256,2048]{1,0:T(8,128)(2,1)S(1)}, u32[]{:S(2)}, u32[]{:S(2)}) %collective-permute-start.115) | collective-permute-done | bytes 1048608 | tf_op jit(solution)/shard_map/ppermute | solution.py:276
  572.6 23.1 %shard_map.213 = bf16[2048,384]{1,0:T(8,128)(2,1)} custom-call(s32[48]{0:T(128)} %pad_add_fusion.offsets, bf16[2,2048,128]{2,1,0:T(8,128)(2,1)} %get-tuple-element.269.qe, bf16[2,2048,128]{2,1,0:T(8,128)(2,1)} %get-tuple-element.270.ke, bf16[2048,128]{1,0:T(8,128)(2,1)} %get-tuple-element.271.vs, f32[2048,128]{1,0:T(8,128)} %get-tuple-element.272.out32, ...), custom_call_target="tpu_custom_call" | custom-call | flops 10737418240 | bytes 12582912 | tf_op jit(solution)/shard_map/pallas_call | solution.py:242
  605.2 51.1 %collective-permute-done.114 = bf16[1024,1024]{1,0:T(8,128)(2,1)S(1)} collective-permute-done((bf16[1024,1024]{1,0:T(8,128)(2,1)S(1)}, bf16[1024,1024]{1,0:T(8,128)(2,1)S(1)}, u32[]{:S(2)}, u32[]{:S(2)}) %collective-permute-start.114) | collective-permute-done | bytes 2097184 | tf_op jit(solution)/shard_map/ppermute | solution.py:276
  660.7 4.6 all-to-all-start.5
  665.9 4.8 fusion.122
  681.8 7.0 fusion.121
  696.7 24.2 %collective-permute-done.103 = bf16[128,2048]{1,0:T(8,128)(2,1)S(1)} collective-permute-done((bf16[128,2048]{1,0:T(8,128)(2,1)S(1)}, bf16[128,2048]{1,0:T(8,128)(2,1)S(1)}, u32[]{:S(2)}, u32[]{:S(2)}) %collective-permute-start.103) | collective-permute-done | bytes 524320 | tf_op jit(solution)/shard_map/ppermute | solution.py:272
  724.5 5.8 collective-permute-start.108
  785.9 5.8 all-to-all-done.3
  (632 shorter events, 371.2 us)
Async XLA Ops:
  2.5 60.4 %collective-permute-start.59 = (bf16[48,2048]{1,0:T(8,128)(2,1)}, bf16[48,2048]{1,0:T(8,128)(2,1)}, u32[]{:S(2)}, u32[]{:S(2)}) collective-permute-start(bf16[48,2048]{1,0:T(8,128)(2,1)} %get-tuple-element.330), channel_id=1, source_target_pairs={{0,4},{1,5},{2,6},{3,7},{4,0},{5,1},{6,2},{7,3},{8,12},{9,13},{10,... | collective-permute-start | bytes 589832 | tf_op jit(solution)/shard_map/ppermute | solution.py:272
  5.5 58.9 %collective-permute-start.60 = (bf16[48,2048]{1,0:T(8,128)(2,1)}, bf16[48,2048]{1,0:T(8,128)(2,1)}, u32[]{:S(2)}, u32[]{:S(2)}) collective-permute-start(bf16[48,2048]{1,0:T(8,128)(2,1)} %get-tuple-element.329), channel_id=1, source_target_pairs={{0,8},{1,9},{2,10},{3,11},{4,12},{5,13},{6,14},{7,15},{8,0},{9,1},... | collective-permute-start | bytes 589832 | tf_op jit(solution)/shard_map/ppermute | solution.py:272
  8.0 52.8 %collective-permute-start.58 = (bf16[32,2048]{1,0:T(8,128)(2,1)S(1)}, bf16[32,2048]{1,0:T(8,128)(2,1)}, u32[]{:S(2)}, u32[]{:S(2)}) collective-permute-start(bf16[32,2048]{1,0:T(8,128)(2,1)S(1)} %slice.491), channel_id=1, source_target_pairs={{0,2},{1,3},{2,0},{3,1},{4,6},{5,7},{6,4},{7,5},{8,10},{9,11},{10,... | collective-permute-start | bytes 393224 | tf_op jit(solution)/shard_map/ppermute | solution.py:272
  11.3 58.5 %collective-permute-start.1 = (bf16[48,2048]{1,0:T(8,128)(2,1)}, bf16[48,2048]{1,0:T(8,128)(2,1)}, u32[]{:S(2)}, u32[]{:S(2)}) collective-permute-start(bf16[48,2048]{1,0:T(8,128)(2,1)} %get-tuple-element.334), channel_id=1, source_target_pairs={{0,4},{1,5},{2,6},{3,7},{4,0},{5,1},{6,2},{7,3},{8,12},{9,13},{10,... | collective-permute-start | bytes 589832 | tf_op jit(solution)/shard_map/ppermute | solution.py:272
  19.1 54.4 %collective-permute-start.16 = (bf16[64,2048]{1,0:T(8,128)(2,1)}, bf16[64,2048]{1,0:T(8,128)(2,1)}, u32[]{:S(2)}, u32[]{:S(2)}) collective-permute-start(bf16[64,2048]{1,0:T(8,128)(2,1)} %param.20), channel_id=1, source_target_pairs={{0,16},{1,17},{2,18},{3,19},{4,20},{5,21},{6,22},{7,23},{8,24},{9,... | collective-permute-start | bytes 786440 | tf_op jit(solution)/shard_map/ppermute | solution.py:276
  43.6 81.2 %all-to-all-start.1 = ((bf16[16,64,384]{2,1,0:T(8,128)(2,1)}), bf16[16,64,384]{2,1,0:T(8,128)(2,1)S(1)}, u32[]{:S(2)}, u32[]{:S(2)}) async-start(bf16[16,64,384]{2,1,0:T(8,128)(2,1)} %copy.78), calls=%async_computation.1 | async-start | bytes 1572864 | tf_op jit(solution)/shard_map/all_to_all | solution.py:355
  103.7 115.7 %collective-permute-start.45 = (bf16[256,2048]{1,0:T(8,128)(2,1)}, bf16[256,2048]{1,0:T(8,128)(2,1)}, u32[]{:S(2)}, u32[]{:S(2)}) collective-permute-start(bf16[256,2048]{1,0:T(8,128)(2,1)} %param.24), channel_id=1, source_target_pairs={{0,16},{1,17},{2,18},{3,19},{4,20},{5,21},{6,22},{7,23},{8,24},{9,... | collective-permute-start | bytes 3145736 | tf_op jit(solution)/shard_map/ppermute | solution.py:276
  124.8 164.6 %all-to-all-start.2 = ((bf16[16,64,1024]{2,1,0:T(8,128)(2,1)}), bf16[16,64,1024]{2,1,0:T(8,128)(2,1)}, u32[]{:S(2)}, u32[]{:S(2)}) async-start(bf16[16,64,1024]{2,1,0:T(8,128)(2,1)} %pad_maximum_fusion), calls=%async_computation.2 | async-start | bytes 4194304 | tf_op jit(solution)/shard_map/all_to_all | solution.py:355
  129.4 56.9 %collective-permute-start.15 = (bf16[1024,384]{1,0:T(8,128)(2,1)S(1)}, bf16[1024,384]{1,0:T(8,128)(2,1)S(1)}, u32[]{:S(2)}, u32[]{:S(2)}) collective-permute-start(bf16[1024,384]{1,0:T(8,128)(2,1)S(1)} %bitcast.204), channel_id=1, source_target_pairs={{0,16},{1,17},{2,18},{3,19},{4,20},{5,21},{6,22},{7,23},{8,24},{9,... | collective-permute-start | bytes 2359304 | tf_op jit(solution)/shard_map/ppermute | solution.py:276
  248.9 39.6 %collective-permute-start.70 = (bf16[128,2048]{1,0:T(8,128)(2,1)S(1)}, bf16[128,2048]{1,0:T(8,128)(2,1)S(1)}, u32[]{:S(2)}, u32[]{:S(2)}) collective-permute-start(bf16[128,2048]{1,0:T(8,128)(2,1)S(1)} %collective-permute-done.64), channel_id=1, source_target_pairs={{0,1},{1,0},{2,3},{3,2},{4,5},{5,4},{6,7},{7,6},{8,9},{9,8},{10,11... | collective-permute-start | bytes 1572872 | tf_op jit(solution)/shard_map/ppermute | solution.py:272
  250.3 51.9 %collective-permute-start.71 = (bf16[192,2048]{1,0:T(8,128)(2,1)}, bf16[192,2048]{1,0:T(8,128)(2,1)}, u32[]{:S(2)}, u32[]{:S(2)}) collective-permute-start(bf16[192,2048]{1,0:T(8,128)(2,1)} %collective-permute-done.65), channel_id=1, source_target_pairs={{0,1},{1,0},{2,3},{3,2},{4,5},{5,4},{6,7},{7,6},{8,9},{9,8},{10,11... | collective-permute-start | bytes 2359304 | tf_op jit(solution)/shard_map/ppermute | solution.py:272
  289.4 89.2 %collective-permute-start.44 = (bf16[1024,1024]{1,0:T(8,128)(2,1)}, bf16[1024,1024]{1,0:T(8,128)(2,1)S(1)}, u32[]{:S(2)}, u32[]{:S(2)}) collective-permute-start(bf16[1024,1024]{1,0:T(8,128)(2,1)} %bitcast.22), channel_id=1, source_target_pairs={{0,16},{1,17},{2,18},{3,19},{4,20},{5,21},{6,22},{7,23},{8,24},{9,... | collective-permute-start | bytes 6291464 | tf_op jit(solution)/shard_map/ppermute | solution.py:276
  297.9 45.0 %collective-permute-start.33 = (bf16[96,2048]{1,0:T(8,128)(2,1)S(1)}, bf16[96,2048]{1,0:T(8,128)(2,1)S(1)}, u32[]{:S(2)}, u32[]{:S(2)}) collective-permute-start(bf16[96,2048]{1,0:T(8,128)(2,1)S(1)} %pad_maximum_fusion.20), channel_id=1, source_target_pairs={{0,8},{1,9},{2,10},{3,11},{4,12},{5,13},{6,14},{7,15},{8,0},{9,1},... | collective-permute-start | bytes 1179656 | tf_op jit(solution)/shard_map/ppermute | solution.py:272
  298.3 44.6 %collective-permute-start.34 = (bf16[96,2048]{1,0:T(8,128)(2,1)S(1)}, bf16[96,2048]{1,0:T(8,128)(2,1)S(1)}, u32[]{:S(2)}, u32[]{:S(2)}) collective-permute-start(bf16[96,2048]{1,0:T(8,128)(2,1)S(1)} %pad_maximum_fusion.21), channel_id=1, source_target_pairs={{0,2},{1,3},{2,0},{3,1},{4,6},{5,7},{6,4},{7,5},{8,10},{9,11},{10,... | collective-permute-start | bytes 1179656 | tf_op jit(solution)/shard_map/ppermute | solution.py:272
  302.2 45.9 %collective-permute-start.72 = (bf16[192,2048]{1,0:T(8,128)(2,1)S(1)}, bf16[192,2048]{1,0:T(8,128)(2,1)S(1)}, u32[]{:S(2)}, u32[]{:S(2)}) collective-permute-start(bf16[192,2048]{1,0:T(8,128)(2,1)S(1)} %collective-permute-done.66), channel_id=1, source_target_pairs={{0,1},{1,0},{2,3},{3,2},{4,5},{5,4},{6,7},{7,6},{8,9},{9,8},{10,11... | collective-permute-start | bytes 2359304 | tf_op jit(solution)/shard_map/ppermute | solution.py:272
  343.2 46.5 %collective-permute-start.35 = (bf16[128,2048]{1,0:T(8,128)(2,1)S(1)}, bf16[128,2048]{1,0:T(8,128)(2,1)S(1)}, u32[]{:S(2)}, u32[]{:S(2)}) collective-permute-start(bf16[128,2048]{1,0:T(8,128)(2,1)S(1)} %pad_maximum_fusion.15), channel_id=1, source_target_pairs={{0,8},{1,9},{2,10},{3,11},{4,12},{5,13},{6,14},{7,15},{8,0},{9,1},... | collective-permute-start | bytes 1572872 | tf_op jit(solution)/shard_map/ppermute | solution.py:272
  346.7 44.9 %collective-permute-start.36 = (bf16[192,2048]{1,0:T(8,128)(2,1)S(1)}, bf16[192,2048]{1,0:T(8,128)(2,1)S(1)}, u32[]{:S(2)}, u32[]{:S(2)}) collective-permute-start(bf16[192,2048]{1,0:T(8,128)(2,1)S(1)} %pad_maximum_fusion.8), channel_id=1, source_target_pairs={{0,2},{1,3},{2,0},{3,1},{4,6},{5,7},{6,4},{7,5},{8,10},{9,11},{10,... | collective-permute-start | bytes 2359304 | tf_op jit(solution)/shard_map/ppermute | solution.py:272
  348.1 43.5 %collective-permute-start.39 = (bf16[192,2048]{1,0:T(8,128)(2,1)S(1)}, bf16[192,2048]{1,0:T(8,128)(2,1)S(1)}, u32[]{:S(2)}, u32[]{:S(2)}) collective-permute-start(bf16[192,2048]{1,0:T(8,128)(2,1)S(1)} %pad_maximum_fusion.8), channel_id=1, source_target_pairs={{0,1},{1,0},{2,3},{3,2},{4,5},{5,4},{6,7},{7,6},{8,9},{9,8},{10,11... | collective-permute-start | bytes 2359304 | tf_op jit(solution)/shard_map/ppermute | solution.py:272
  348.1 43.5 %collective-permute-start.37 = (bf16[192,2048]{1,0:T(8,128)(2,1)S(1)}, bf16[192,2048]{1,0:T(8,128)(2,1)S(1)}, u32[]{:S(2)}, u32[]{:S(2)}) collective-permute-start(bf16[192,2048]{1,0:T(8,128)(2,1)S(1)} %pad_maximum_fusion.9), channel_id=1, source_target_pairs={{0,4},{1,5},{2,6},{3,7},{4,0},{5,1},{6,2},{7,3},{8,12},{9,13},{10,... | collective-permute-start | bytes 2359304 | tf_op jit(solution)/shard_map/ppermute | solution.py:272
  520.3 41.4 %collective-permute-start.115 = (bf16[256,2048]{1,0:T(8,128)(2,1)S(1)}, bf16[256,2048]{1,0:T(8,128)(2,1)S(1)}, u32[]{:S(2)}, u32[]{:S(2)}) collective-permute-start(bf16[256,2048]{1,0:T(8,128)(2,1)S(1)} %fusion.52), channel_id=1, source_target_pairs={{0,16},{1,17},{2,18},{3,19},{4,20},{5,21},{6,22},{7,23},{8,24},{9,... | collective-permute-start | bytes 3145736 | tf_op jit(solution)/shard_map/ppermute | solution.py:276
  521.1 40.9 %collective-permute-start.91 = (bf16[128,2048]{1,0:T(8,128)(2,1)S(1)}, bf16[128,2048]{1,0:T(8,128)(2,1)S(1)}, u32[]{:S(2)}, u32[]{:S(2)}) collective-permute-start(bf16[128,2048]{1,0:T(8,128)(2,1)S(1)} %pad_maximum_fusion.17), channel_id=1, source_target_pairs={{0,8},{1,9},{2,10},{3,11},{4,12},{5,13},{6,14},{7,15},{8,0},{9,1},... | collective-permute-start | bytes 1572872 | tf_op jit(solution)/shard_map/ppermute | solution.py:272
  564.7 91.6 %collective-permute-start.114 = (bf16[1024,1024]{1,0:T(8,128)(2,1)S(1)}, bf16[1024,1024]{1,0:T(8,128)(2,1)S(1)}, u32[]{:S(2)}, u32[]{:S(2)}) collective-permute-start(bf16[1024,1024]{1,0:T(8,128)(2,1)S(1)} %fusion.5), channel_id=1, source_target_pairs={{0,16},{1,17},{2,18},{3,19},{4,20},{5,21},{6,22},{7,23},{8,24},{9,... | collective-permute-start | bytes 6291464 | tf_op jit(solution)/shard_map/ppermute | solution.py:276
  598.9 74.4 %collective-permute-start.101 = (bf16[384,2048]{1,0:T(8,128)(2,1)}, bf16[384,2048]{1,0:T(8,128)(2,1)}, u32[]{:S(2)}, u32[]{:S(2)}) collective-permute-start(bf16[384,2048]{1,0:T(8,128)(2,1)} %convolution_convert_fusion.1), channel_id=1, source_target_pairs={{0,1},{1,0},{2,3},{3,2},{4,5},{5,4},{6,7},{7,6},{8,9},{9,8},{10,11... | collective-permute-start | bytes 4718600 | tf_op jit(solution)/shard_map/ppermute | solution.py:272
  604.7 67.7 %collective-permute-start.100 = (bf16[256,2048]{1,0:T(8,128)(2,1)}, bf16[256,2048]{1,0:T(8,128)(2,1)S(1)}, u32[]{:S(2)}, u32[]{:S(2)}) collective-permute-start(bf16[256,2048]{1,0:T(8,128)(2,1)} %convolution_convert_fusion.8), channel_id=1, source_target_pairs={{0,1},{1,0},{2,3},{3,2},{4,5},{5,4},{6,7},{7,6},{8,9},{9,8},{10,11... | collective-permute-start | bytes 3145736 | tf_op jit(solution)/shard_map/ppermute | solution.py:272
  605.1 70.7 %collective-permute-start.102 = (bf16[384,2048]{1,0:T(8,128)(2,1)}, bf16[384,2048]{1,0:T(8,128)(2,1)}, u32[]{:S(2)}, u32[]{:S(2)}) collective-permute-start(bf16[384,2048]{1,0:T(8,128)(2,1)} %convolution_convert_fusion), channel_id=1, source_target_pairs={{0,1},{1,0},{2,3},{3,2},{4,5},{5,4},{6,7},{7,6},{8,9},{9,8},{10,11... | collective-permute-start | bytes 4718600 | tf_op jit(solution)/shard_map/ppermute | solution.py:272
  660.7 73.5 %all-to-all-start.5 = ((bf16[16,64,1024]{2,1,0:T(8,128)(2,1)}), bf16[16,64,1024]{2,1,0:T(8,128)(2,1)}, u32[]{:S(2)}, u32[]{:S(2)}) async-start(bf16[16,64,1024]{2,1,0:T(8,128)(2,1)} %bitcast.190), calls=%async_computation.5 | async-start | bytes 4194304 | tf_op jit(solution)/shard_map/all_to_all | solution.py:355
  678.4 42.5 %collective-permute-start.104 = (bf16[192,2048]{1,0:T(8,128)(2,1)S(1)}, bf16[192,2048]{1,0:T(8,128)(2,1)S(1)}, u32[]{:S(2)}, u32[]{:S(2)}) collective-permute-start(bf16[192,2048]{1,0:T(8,128)(2,1)S(1)} %slice.787), channel_id=1, source_target_pairs={{0,2},{1,3},{2,0},{3,1},{4,6},{5,7},{6,4},{7,5},{8,10},{9,11},{10,... | collective-permute-start | bytes 2359304 | tf_op jit(solution)/shard_map/ppermute | solution.py:272
  680.3 40.5 %collective-permute-start.105 = (bf16[192,2048]{1,0:T(8,128)(2,1)S(1)}, bf16[192,2048]{1,0:T(8,128)(2,1)S(1)}, u32[]{:S(2)}, u32[]{:S(2)}) collective-permute-start(bf16[192,2048]{1,0:T(8,128)(2,1)S(1)} %slice.786), channel_id=1, source_target_pairs={{0,4},{1,5},{2,6},{3,7},{4,0},{5,1},{6,2},{7,3},{8,12},{9,13},{10,... | collective-permute-start | bytes 2359304 | tf_op jit(solution)/shard_map/ppermute | solution.py:272
  690.4 42.1 %collective-permute-start.112 = (bf16[1024,384]{1,0:T(8,128)(2,1)S(1)}, bf16[1024,384]{1,0:T(8,128)(2,1)S(1)}, u32[]{:S(2)}, u32[]{:S(2)}) collective-permute-start(bf16[1024,384]{1,0:T(8,128)(2,1)S(1)} %fusion.54), channel_id=1, source_target_pairs={{0,16},{1,17},{2,18},{3,19},{4,20},{5,21},{6,22},{7,23},{8,24},{9,... | collective-permute-start | bytes 2359304 | tf_op jit(solution)/shard_map/ppermute | solution.py:276
  724.5 33.4 %collective-permute-start.107 = (bf16[96,2048]{1,0:T(8,128)(2,1)S(1)}, bf16[96,2048]{1,0:T(8,128)(2,1)}, u32[]{:S(2)}, u32[]{:S(2)}) collective-permute-start(bf16[96,2048]{1,0:T(8,128)(2,1)S(1)} %slice.799), channel_id=1, source_target_pairs={{0,8},{1,9},{2,10},{3,11},{4,12},{5,13},{6,14},{7,15},{8,0},{9,1},... | collective-permute-start | bytes 1179656 | tf_op jit(solution)/shard_map/ppermute | solution.py:272
  724.5 33.4 %collective-permute-start.108 = (bf16[96,2048]{1,0:T(8,128)(2,1)}, bf16[96,2048]{1,0:T(8,128)(2,1)}, u32[]{:S(2)}, u32[]{:S(2)}) collective-permute-start(bf16[96,2048]{1,0:T(8,128)(2,1)} %slice.798), channel_id=1, source_target_pairs={{0,2},{1,3},{2,0},{3,1},{4,6},{5,7},{6,4},{7,5},{8,10},{9,11},{10,... | collective-permute-start | bytes 1179656 | tf_op jit(solution)/shard_map/ppermute | solution.py:272
  734.1 34.3 %all-to-all-start.4 = ((bf16[16,64,384]{2,1,0:T(8,128)(2,1)}), bf16[16,64,384]{2,1,0:T(8,128)(2,1)S(1)}, u32[]{:S(2)}, u32[]{:S(2)}) async-start(bf16[16,64,384]{2,1,0:T(8,128)(2,1)} %bitcast.33), calls=%async_computation.4 | async-start | bytes 1572864 | tf_op jit(solution)/shard_map/all_to_all | solution.py:355
  (147 other events, 1741.4 us)

commit v3 on v2

v3 whole, which is shorter than its diff:
```python
import functools

import jax
import jax.numpy as jnp
from jax import lax
from jax.experimental import pallas as pl
from jax.experimental.pallas import tpu as pltpu
from jax.sharding import PartitionSpec as P

HEADS = 32
HEAD_DIM = 64
SEQ = 2048
DOCS = 16


EPS = 1e-05
THETA = 130000.0
HIDE = -1e30
BF = jnp.bfloat16
F32 = jnp.float32
LANES = 2 * HEAD_DIM
HALF = HEAD_DIM // 2
BLOCK = 512
VMEM = 56 * 2**20


def barrier(*values):
    return lax.optimization_barrier(values)


def norm_rows(v, gain):
    scale = lax.rsqrt(jnp.mean(v * v, axis=-1, keepdims=True) + EPS)
    return v * scale * gain


def norm_back(v, gain, grad):
    scale = lax.rsqrt(jnp.mean(v * v, axis=-1, keepdims=True) + EPS)
    hat = v * scale
    weighted = gain * grad
    back = scale * (weighted - hat * jnp.mean(hat * weighted, axis=-1, keepdims=True))
    return back, jnp.sum(grad * hat, axis=0)


def matmul(left, right):
    return jnp.dot(left, right, preferred_element_type=F32)


def times_t(left, right):
    return lax.dot_general(left, right, (((1,), (1,)), ((), ())), preferred_element_type=F32)


def t_times(left, right):
    return lax.dot_general(left, right, (((0,), (0,)), ((), ())), preferred_element_type=F32)


def call(kernel, out_shape, in_specs, out_specs, flops, moved, grid=(), scratch=()):
    return pl.pallas_call(
        kernel,
        grid=grid,
        out_shape=out_shape,
        in_specs=in_specs,
        out_specs=out_specs,
        scratch_shapes=list(scratch),
        compiler_params=pltpu.CompilerParams(vmem_limit_bytes=VMEM),
        cost_estimate=pl.CostEstimate(
            flops=int(flops) // 16, bytes_accessed=int(moved) // 16, transcendentals=0
        ),
    )


LIKE = jax.ShapeDtypeStruct
IN_SMEM = pl.BlockSpec(memory_space=pltpu.SMEM)
IN_VMEM = pl.BlockSpec(memory_space=pltpu.VMEM)


def lane_index(shape):
    return lax.broadcasted_iota(jnp.int32, shape, len(shape) - 1)


def of_head(head, shape):
    return lane_index(shape) // HEAD_DIM == head


def swapped(v):
    first = lane_index(v.shape) % HEAD_DIM < HALF
    return jnp.where(first, pltpu.roll(v, LANES - HALF, 1), pltpu.roll(v, HALF, 1))


def parts_of(v):
    high = v.astype(BF)
    rest = v - high.astype(F32)
    mid = rest.astype(BF)
    return high, mid, (rest - mid.astype(F32)).astype(BF)


def in_lanes(columns, first, shape):
    lane = lane_index(shape)
    out = jnp.zeros(shape, BF)
    for c, column in enumerate(columns):
        out = jnp.where(lane == first + c, column, out)
    return out


def send_rows(subs, offsets, give):
    rows = sum(subs)
    blocks = SEQ // rows

    def one(b, carry):
        start = 0
        for r, sub in enumerate(subs):
            there = pl.ds(pl.multiple_of(offsets[r * blocks + b], 16), sub)
            here = pl.ds(pl.multiple_of(b * rows + start, 16), sub)
            start += sub
            give(here, there)
        return carry

    lax.fori_loop(0, blocks, one, 0)


def forward_kernel(
    subs, offsets, qkv, cosine, sine, q_mask, k_mask, qe, ke, vs, out, out32, railed
):
    shape = (BLOCK, LANES)
    for i in range(SEQ // BLOCK):
        mine = slice(i * BLOCK, (i + 1) * BLOCK)
        c, s = cosine[mine, :], sine[mine, :]
        for at, ends, mask in ((0, qe, q_mask), (1, ke, k_mask)):
            v = qkv[mine, at * LANES : (at + 1) * LANES]
            turned = (v * c + swapped(v) * s).astype(BF)
            if at == 0:
                turned = turned * (HEAD_DIM**-0.5)
            for head in range(2):
                ends[head, mine, :] = jnp.where(of_head(head, shape), turned, mask[mine, :])
        vs[mine, :] = qkv[mine, 2 * LANES :].astype(BF)
    diagonal = lax.broadcasted_iota(jnp.int32, (BLOCK, BLOCK), 0) >= lane_index((BLOCK, BLOCK))
    for i in range(SEQ // BLOCK):
        mine = slice(i * BLOCK, (i + 1) * BLOCK)
        outs = []
        for head in range(2):
            spare = (1 - head) * HEAD_DIM
            query = qe[head, mine, :]
            scores = []
            for j in range(i + 1):
                s = times_t(query, ke[head, j * BLOCK : (j + 1) * BLOCK, :])
                scores.append(jnp.where(diagonal, s, HIDE) if j == i else s)
            top = functools.reduce(jnp.maximum, scores)
            top = jnp.max(top, axis=1, keepdims=True)
            total = jnp.zeros(shape, F32)
            for j, s in enumerate(scores):
                probs = jnp.exp(s - top).astype(BF)
                value = vs[j * BLOCK : (j + 1) * BLOCK, :]
                value = jnp.where(of_head(head, shape), value, jnp.ones((), BF))
                total += matmul(probs, value)
            weight = total[:, spare : spare + 1]
            outs.append(total / weight)
            logsum = top + jnp.log(weight)
            qe[head, mine, :] = query + in_lanes(parts_of(-logsum), spare + HALF, shape)
        both = jnp.where(of_head(0, shape), outs[0], outs[1])
        out32[mine, :] = both
        out[mine, :] = both.astype(BF)

    def give(here, there):
        railed[there, :] = out[here, :]

    send_rows(subs, offsets, give)


def backward_kernel(
    subs, offsets, qe, ke, vs, out32, dout, cosine, sine, grads, railed, de, dq, dk, dv
):
    shape = (BLOCK, LANES)
    for i in range(SEQ // BLOCK):
        mine = slice(i * BLOCK, (i + 1) * BLOCK)
        grad = dout[mine, :]
        weighted = grad.astype(F32) * out32[mine, :]
        for head in range(2):
            own = of_head(head, shape)
            delta = jnp.sum(jnp.where(own, weighted, 0.0), axis=1, keepdims=True)
            extra = in_lanes(parts_of(-delta), (1 - head) * HEAD_DIM, shape)
            de[head, mine, :] = jnp.where(own, grad, extra)
    diagonal = lax.broadcasted_iota(jnp.int32, (BLOCK, BLOCK), 0) <= lane_index((BLOCK, BLOCK))
    lane = lane_index(shape)
    for head in range(2):
        spare = (1 - head) * HEAD_DIM
        ones = jnp.where((lane >= spare) & (lane < spare + 3), jnp.ones((), BF), jnp.zeros((), BF))
        for j in range(SEQ // BLOCK):
            theirs = slice(j * BLOCK, (j + 1) * BLOCK)
            key = ke[head, theirs, :]
            value = jnp.where(of_head(head, shape), vs[theirs, :], ones)
            dkey = jnp.zeros(shape, F32)
            dvalue = jnp.zeros(shape, F32)
            for i in range(j, SEQ // BLOCK):
                mine = slice(i * BLOCK, (i + 1) * BLOCK)
                query = qe[head, mine, :]
                grad = de[head, mine, :]
                probs = jnp.exp(times_t(key, query))
                if i == j:
                    probs = jnp.where(diagonal, probs, 0.0)
                dscore = (probs * times_t(value, grad)).astype(BF)
                dvalue += matmul(probs.astype(BF), grad)
                dkey += matmul(dscore, query)
                dquery = t_times(dscore, key)
                if j > 0:
                    dquery += dq[head, mine, :]
                dq[head, mine, :] = dquery
            dk[head, theirs, :] = dkey
            dv[head, theirs, :] = dvalue
    for i in range(SEQ // BLOCK):
        mine = slice(i * BLOCK, (i + 1) * BLOCK)
        c, s = cosine[mine, :], sine[mine, :]
        first = of_head(0, shape)
        query = jnp.where(first, dq[0, mine, :], dq[1, mine, :]) * (HEAD_DIM**-0.5)
        key = jnp.where(first, dk[0, mine, :], dk[1, mine, :])
        for at, v in ((0, query), (1, key)):
            turned = v * c - swapped(v) * s
            grads[mine, at * LANES : (at + 1) * LANES] = turned.astype(BF)
        value = jnp.where(first, dv[0, mine, :], dv[1, mine, :])
        grads[mine, 2 * LANES :] = value.astype(BF)

    def give(here, there):
        railed[there, :] = grads[here, :]

    send_rows(subs, offsets, give)


def attend_forward(subs, offsets, qkv, cosine, sine, q_mask, k_mask):
    return call(
        functools.partial(forward_kernel, subs),
        [
            LIKE((2, SEQ, LANES), BF),
            LIKE((2, SEQ, LANES), BF),
            LIKE((SEQ, LANES), BF),
            LIKE((SEQ, LANES), BF),
            LIKE((SEQ, LANES), F32),
            LIKE((SEQ, LANES), BF),
        ],
        [IN_SMEM] + [IN_VMEM] * 5,
        [IN_VMEM] * 6,
        8 * SEQ * SEQ * LANES,
        12 * 2**20,
    )(offsets, qkv, cosine, sine, q_mask, k_mask)


def attend_backward(subs, offsets, qe, ke, vs, out32, dout, cosine, sine):
    return call(
        functools.partial(backward_kernel, subs),
        [LIKE((SEQ, 3 * LANES), BF)] * 2,
        [IN_SMEM] + [IN_VMEM] * 7,
        [IN_VMEM] * 2,
        20 * SEQ * SEQ * LANES,
        12 * 2**20,
        scratch=[
            pltpu.VMEM((2, SEQ, LANES), BF),
            pltpu.VMEM((2, SEQ, LANES), F32),
            pltpu.VMEM((2, SEQ, LANES), F32),
            pltpu.VMEM((2, SEQ, LANES), F32),
        ],
    )(offsets, qe, ke, vs, out32, dout, cosine, sine)


def project_kernel(x, gain, w, h, out):
    h[...] = norm_rows(x[...].astype(F32), gain[...]).astype(BF)
    out[...] = matmul(h[...], w[...])


def norm_project(x, gain, w):
    rows, width = x.shape
    step, columns = 256, w.shape[1]
    return call(
        project_kernel,
        [LIKE((rows, width), BF), LIKE((rows, columns), F32)],
        [
            pl.BlockSpec((step, width), lambda i: (i, 0)),
            pl.BlockSpec((1, width), lambda i: (0, 0)),
            pl.BlockSpec((width, columns), lambda i: (0, 0)),
        ],
        [
            pl.BlockSpec((step, width), lambda i: (i, 0)),
            pl.BlockSpec((step, columns), lambda i: (i, 0)),
        ],
        2 * rows * width * columns,
        4 * rows * width,
        grid=(rows // step,),
    )(x, gain, w)


def hidden_kernel(subs, spots, h, w, dm, mixed, dgu, *refs):
    rails = len(subs)
    sent, kept, held = refs[:rails], refs[rails : 2 * rails], refs[2 * rails]
    hidden = dm.shape[1]
    gu = matmul(h[...], w[...])
    gate, up = gu[:, :hidden], gu[:, hidden:]
    sig = 1.0 / (1.0 + jnp.exp(-gate))
    silu = gate * sig
    mixed[...] = (silu * up).astype(BF)
    grad = dm[...]
    dgu[:, :hidden] = (grad * up * (sig + silu * (1.0 - sig))).astype(BF)
    dgu[:, hidden:] = (grad * silu).astype(BF)
    held[...] = times_t(dgu[...], w[...]).astype(BF)
    rows = sum(subs)
    core = spots[0]
    chips = SEQ // (2 * rows)
    start = 0
    for r, sub in enumerate(subs):
        there = pl.ds(pl.multiple_of(spots[1 + r * chips + pl.program_id(0)], 16), sub)
        near = pl.ds(pl.multiple_of(core * rows + start, 16), sub)
        far = pl.ds(pl.multiple_of((1 - core) * rows + start, 16), sub)
        kept[r][there, :] = held[near, :]
        sent[r][there, :] = held[far, :]
        start += sub


def hidden_rows(subs, spots, h, w, dm):
    rows, width = h.shape
    hidden = dm.shape[1]
    step = 2 * sum(subs)
    chips = rows // step
    rails = [LIKE((chips * sub, width), BF) for sub in subs]
    made = call(
        functools.partial(hidden_kernel, subs),
        [LIKE((rows, hidden), BF), LIKE((rows, 2 * hidden), BF)] + rails + rails,
        [
            IN_SMEM,
            pl.BlockSpec((step, width), lambda i: (i, 0)),
            pl.BlockSpec((width, 2 * hidden), lambda i: (0, 0)),
            pl.BlockSpec((step, hidden), lambda i: (i, 0)),
        ],
        [
            pl.BlockSpec((step, hidden), lambda i: (i, 0)),
            pl.BlockSpec((step, 2 * hidden), lambda i: (i, 0)),
        ]
        + [IN_VMEM] * (2 * len(subs)),
        8 * rows * width * hidden,
        6 * rows * width,
        grid=(chips,),
        scratch=[pltpu.VMEM((step, width), BF)],
    )(spots, h, w, dm)
    return made[0], made[1], made[2 : 2 + len(subs)], made[2 + len(subs) :]


def cut_kernel(first, each, blocks, *refs):
    out = refs[-1]
    for p in range(out.shape[0]):
        at = 0
        for w in refs[:-1]:
            for j in range(blocks):
                out[p, :, at : at + each] = w[:, first(j, p) : first(j, p) + each]
                at += each


def cut_columns(weights, size, first, each, blocks):
    rows = weights[0].shape[0]
    columns = each * blocks * len(weights)
    return call(
        functools.partial(cut_kernel, first, each, blocks),
        LIKE((size, rows, columns), BF),
        [IN_VMEM] * len(weights),
        IN_VMEM,
        0,
        4 * size * rows * columns,
    )(*weights)


def join_kernel(first, each, blocks, v, *outs):
    for p in range(v.shape[0]):
        at = 0
        for out in outs:
            for j in range(blocks):
                out[:, first(j, p) : first(j, p) + each] = v[p, :, at : at + each].astype(F32)
                at += each


def join_columns(v, parts, first, each, blocks):
    size, rows, _ = v.shape
    return call(
        functools.partial(join_kernel, first, each, blocks),
        [LIKE((rows, size * each * blocks), F32)] * parts,
        [IN_VMEM],
        [IN_VMEM] * parts,
        0,
        6 * v.size,
    )(v)


class Team:
    def __init__(self, rows, count):
        self.rows, self.count = rows, count
        self.size = SEQ // rows
        self.teams = count // self.size
        self.groups = [[t * self.size + p for p in range(self.size)] for t in range(self.teams)]
        axes = [2 << k for k in range(self.size.bit_length() - 2)]
        self.rails = [tuple(axes[r:] + axes[:r]) for r in range(len(axes))]
        share = rows // (8 * 16) * 16
        self.subs = [2 * share] + [3 * share] * (len(axes) - 1)
        self.subs[-1] += rows - sum(self.subs)

    def flip(self, mask):
        pairs = [(i, i ^ mask) for i in range(self.count)]
        return lambda v: lax.ppermute(v, "fsdp", pairs)

    def ahead(self, teams):
        step = teams * self.size
        pairs = [(i, (i + step) % self.count) for i in range(self.count)]
        return lambda v: lax.ppermute(v, "fsdp", pairs)

    def stay(self, v):
        return v

    def exchange(self, v):
        return lax.all_to_all(v, "fsdp", 0, 0, tiled=True, axis_index_groups=self.groups)

    def gather(self, v):
        return lax.all_gather(v, "fsdp", axis=0, tiled=True, axis_index_groups=self.groups)

    def reduce(self, v):
        return lax.psum_scatter(
            v, "fsdp", scatter_dimension=0, tiled=True, axis_index_groups=self.groups
        )

    def spots(self, place):
        away = 2 * jnp.arange(self.size // 2, dtype=jnp.int32) ^ place
        out = []
        for rail, sub in zip(self.rails, self.subs):
            at = jnp.zeros_like(away)
            for k, mask in enumerate(rail):
                at = at + jnp.where(away & mask != 0, sub << k, 0)
            out.append(at)
        return jnp.stack(out).astype(jnp.int32)

    def offsets(self, place):
        starts = jnp.cumsum(jnp.array([0] + self.subs[:-1], jnp.int32)) * (self.size // 2)
        chip = self.spots(place) + starts[:, None]
        other = (jnp.arange(2, dtype=jnp.int32) ^ place) & 1
        return (chip[:, :, None] + other * (SEQ // 2)).reshape(-1).astype(jnp.int32)

    def cut(self, v):
        out, start = [], 0
        for sub in self.subs:
            each = sub * self.size // 2
            out.append(v[start : start + each])
            start += each
        return out

    def one(self, v, move):
        [got] = yield [(v, move)]
        return got

    def scatter(self, sent, kept):
        got = yield [(s, self.flip(1)) for s in sent]
        held = [k.astype(F32) + g.astype(F32) for k, g in zip(kept, got)]
        for step in reversed(range(len(self.rails[0]))):
            upper = [h[h.shape[0] // 2 :].astype(BF) for h in held]
            got = yield [(u, self.flip(rail[step])) for u, rail in zip(upper, self.rails)]
            held = [h[: h.shape[0] // 2] + g.astype(F32) for h, g in zip(held, got)]
        return jnp.concatenate(held)

    def spread(self, block, chunks, mine):
        got, start = [[] for _ in range(self.teams)], 0
        for chunk in chunks:
            each = block.shape[0] * chunk // 16
            part = block[start : start + each]
            start += each
            new = yield [(part, self.ahead(s)) for s in range(1, self.teams)]
            for s, piece in enumerate(new):
                got[s + 1].append(piece)
        held = jnp.zeros((self.teams,) + block.shape, block.dtype)
        held = lax.dynamic_update_index_in_dim(held, block, mine, 0)
        for s in range(1, self.teams):
            at, start = (mine - s) % self.teams, 0
            for piece in got[s]:
                held = lax.dynamic_update_slice(held, piece[None], (at, start, 0))
                start += piece.shape[0]
        return held.reshape((-1,) + block.shape[1:])

    def columns(self, cut, chunks, mine):
        [block] = yield [(cut, self.exchange)]
        return (yield from self.spread(block.reshape(-1, block.shape[2]), chunks, mine))

    def add(self, left, right, chunks, mine):
        width = left.shape[1] // self.teams

        def product(team):
            return t_times(lax.dynamic_slice_in_dim(left, team * width, width, 1), right)

        sent = [product((mine + s) % self.teams).astype(BF) for s in range(1, self.teams)]
        got, start, total = [[] for _ in sent], 0, None
        for chunk in chunks:
            each = width * chunk // 16
            moves = [(v[start : start + each], self.ahead(s + 1)) for s, v in enumerate(sent)]
            if start == 0:
                new = yield moves
            else:
                *new, total = yield moves + [(total, self.stay)]
            start += each
            if total is None:
                total = product(mine)
            for s, piece in enumerate(new):
                got[s].append(piece)
        for pieces in got:
            total = total + jnp.concatenate(pieces).astype(F32)
        return total

    def owners(self, left, right, chunks, mine):
        total = yield from self.add(left, right, chunks, mine)
        [got] = yield [(total.astype(BF).reshape(self.size, -1, total.shape[1]), self.exchange)]
        return got


class Transfer:
    def __init__(self, steps):
        self.steps, self.value, self.over, self.got = steps, None, False, None
        self.moves = next(steps)

    def take(self):
        got, self.got = self.got, None
        try:
            self.moves = self.steps.send(got)
        except StopIteration as end:
            self.value, self.over, self.moves = end.value, True, []


class Clock:
    def __init__(self, token):
        self.token = token

    def start(self, *transfers):
        given = [v for t in transfers for v, _ in t.moves]
        given = list(barrier(self.token, *given)[1:])
        for t in transfers:
            t.got = [move(given.pop(0)) for _, move in t.moves]

    def wait(self, transfers, *values):
        tied = list(barrier(self.token, *values, *[g for t in transfers for g in t.got]))
        self.token, values, rest = tied[0], tied[1 : 1 + len(values)], tied[1 + len(values) :]
        for t in transfers:
            t.got = [rest.pop(0) for _ in t.got]
        for t in transfers:
            t.take()
        return values


def local(
    tokens,
    segments,
    positions,
    gain_attn,
    w_query,
    w_key,
    w_value,
    w_out,
    gain_mlp,
    w_gate,
    w_up,
    w_down,
    cotangent,
):
    rows, width = tokens.shape
    count = lax.axis_size("fsdp")
    team = Team(rows, count)
    size, teams = team.size, team.teams
    index = lax.axis_index("fsdp")
    mine = index // size
    place = index % size
    own = w_query.shape[0]
    whole_heads = own % HEAD_DIM == 0
    ff_own = w_down.shape[0]
    if whole_heads:
        head_cut = (lambda j, p: (j * size + p) * HEAD_DIM, HEAD_DIM, 2)
    else:
        head_cut = (lambda j, p: p * LANES, LANES, 1)
    ff_cut = (lambda j, p: (j * size + p) * ff_own, ff_own, teams)

    def everywhere(v):
        return lax.all_to_all(v, "fsdp", 0, 0, tiled=True)

    def across(move, *args):
        return Transfer(move(*args, mine))

    clock = Clock(positions)
    start, wait = clock.start, clock.wait

    get_x = Transfer(team.one(tokens, team.gather))
    start(get_x)
    small = jnp.concatenate([v.astype(F32) for v in (gain_attn, gain_mlp, segments, positions)])
    small = jnp.broadcast_to(small[None], (count, small.shape[0]))
    small = Transfer(team.one(small, everywhere))
    get_qkv = across(team.columns, cut_columns([w_query, w_key, w_value], size, *head_cut), [8, 8])
    get_down = across(team.spread, w_down, [4, 4, 4, 4])
    moving = [get_qkv]
    if whole_heads:
        get_out = across(team.spread, w_out, [16])
        moving.append(get_out)
    start(*moving)
    wait(moving)
    out_rows = (
        get_out.value
        if whole_heads
        else lax.dynamic_slice_in_dim(
            lax.all_gather(w_out, "fsdp", axis=0, tiled=True), place * LANES, LANES
        )
    )
    get_dy = Transfer(team.one(cotangent, team.gather))
    start(get_qkv, small, get_dy)
    wait([get_qkv, small])
    start(get_qkv)
    small = small.value
    gain_one = small[:, :own].reshape(1, -1)
    gain_two = small[:, own : 2 * own].reshape(1, -1)
    small = lax.dynamic_slice_in_dim(small, mine * size, size, 0)
    docs = small[:, 2 * own : 2 * own + rows].reshape(SEQ, 1)
    places = small[:, 2 * own + rows :].reshape(SEQ, 1)
    freqs = THETA ** (-jnp.arange(HALF, dtype=F32) * 2.0 / HEAD_DIM)
    angles = places * freqs[None, :]
    cosine, sine = jnp.cos(angles), jnp.sin(angles)
    cosine = jnp.concatenate([cosine] * 4, axis=1)
    sine = jnp.concatenate([-sine, sine] * 2, axis=1)
    lane = jnp.arange(LANES)[None, :] % HEAD_DIM
    number = lane.astype(F32)
    q_mask = jnp.where((lane < DOCS) & (docs != number), HIDE, 0.0).astype(BF)
    tail = (lane >= HALF) & (lane < HALF + 3)
    k_mask = jnp.where(((lane < DOCS) & (docs == number)) | tail, 1.0, 0.0).astype(BF)
    offsets = team.offsets(place)
    spots = jnp.concatenate([place[None] % 2, team.spots(place).reshape(-1)]).astype(jnp.int32)
    subs = tuple(team.subs)
    cut_gu = cut_columns([w_gate, w_up], size, *ff_cut)
    get_gu = across(team.columns, cut_gu, [4, 4, 4, 4])
    cosine, sine, q_mask, k_mask = wait([get_qkv, get_x], cosine, sine, q_mask, k_mask)

    x_all, w_qkv = get_x.value, get_qkv.value
    start(get_gu, get_down)
    h1, qkv = norm_project(x_all, gain_one, w_qkv)
    qe, ke, vs, out, out32, railed = attend_forward(
        subs, offsets, qkv, cosine, sine, q_mask, k_mask
    )
    [railed] = wait([get_down, get_gu], railed)

    def products(left, times):
        cut = team.cut(left[: SEQ // 2]), team.cut(left[SEQ // 2 :])
        return [times(v).astype(BF) for v in cut[1]], [times(v) for v in cut[0]]

    add_out = Transfer(team.scatter(*products(railed, lambda v: matmul(v, out_rows))))
    start(add_out, get_down)
    wait([add_out, get_down])
    start(add_out, get_gu)
    wait([add_out, get_gu])
    start(add_out, get_down)
    wait([add_out, get_down])
    start(add_out, get_down)
    wait([add_out, get_down])
    x = tokens.astype(F32)
    x2 = x + add_out.value
    get_h2 = Transfer(team.one(norm_rows(x2, gain_two).astype(BF), team.gather))
    start(get_h2, get_gu)
    wait([get_gu, get_dy])
    start(get_gu)
    dy = get_dy.value
    down_rows = get_down.value
    dm = times_t(dy, down_rows)
    [dm] = wait([get_gu], dm)
    start(get_gu)
    wait([get_gu, get_h2])
    w_gu = get_gu.value
    h2 = get_h2.value
    mixed, dgu, sent, kept = hidden_rows(subs, spots, h2, w_gu, dm)

    add_dh2 = Transfer(team.scatter(sent, kept))
    start(add_dh2)
    send_gu = across(team.owners, h2, dgu, [4, 2, 2, 4, 4])
    wait([add_dh2])
    for _ in range(3):
        start(add_dh2, send_gu)
        wait([add_dh2, send_gu])
    back, gain_two_part = norm_back(x2, gain_two, add_dh2.value)
    dx2 = cotangent.astype(F32) + back
    get_da = Transfer(team.one(dx2.astype(BF), team.gather))
    start(get_da, send_gu)
    send_down = across(team.add, mixed, dy, [4, 8, 4])
    wait([send_gu])
    start(send_gu)
    partial = matmul(mixed, down_rows).astype(BF)
    [partial] = wait([send_gu, get_da], partial)
    da = get_da.value
    dout = times_t(da, out_rows).astype(BF)
    if whole_heads:
        send_out = across(team.add, out, da, [16])
        start(send_out)
        [dout] = wait([send_out], dout)
        grad_out = send_out.value
    else:
        grad_out = lax.psum(
            t_times(out, da), "fsdp", axis_index_groups=[list(t) for t in zip(*team.groups)]
        )
        grad_out = lax.dynamic_slice_in_dim(team.gather(grad_out), index * own, own)
    add_result = Transfer(team.one(partial, team.reduce))
    start(add_result, send_gu, send_down)
    dqkv, railed = attend_backward(subs, offsets, qe, ke, vs, out32, dout, cosine, sine)
    dqkv, railed = wait([send_down, send_gu], dqkv, railed)
    grad_gate, grad_up = join_columns(send_gu.value, 2, *ff_cut)
    add_dh1 = Transfer(team.scatter(*products(railed, lambda v: times_t(v, w_qkv))))
    start(add_dh1, send_down)
    send_qkv = across(team.owners, h1, dqkv, [8, 8])
    wait([add_dh1, send_down])
    start(add_dh1, send_qkv)
    wait([add_dh1, send_qkv])
    start(add_dh1, send_qkv)
    wait([add_dh1, send_qkv])
    start(add_dh1, send_qkv, send_down)
    wait([add_dh1, send_qkv, send_down])
    back, gain_one_part = norm_back(x, gain_one, add_dh1.value)
    grad_tokens = dx2 + back
    gains = jnp.stack([gain_one_part, gain_two_part]).reshape(2, count, own).transpose(1, 0, 2)
    gains = Transfer(team.one(gains, everywhere))
    start(gains)
    wait([gains, add_result])
    gains = jnp.sum(gains.value, axis=0)
    result = (x2 + add_result.value.astype(F32)).astype(BF)
    grad_query, grad_key, grad_value = join_columns(send_qkv.value, 3, *head_cut)
    return (
        result,
        grad_tokens,
        gains[0],
        grad_query,
        grad_key,
        grad_value,
        grad_out,
        gains[1],
        grad_gate,
        grad_up,
        send_down.value,
    )


def solution(mesh):
    flat = P("fsdp")
    wide = P("fsdp", None)
    return jax.shard_map(
        local,
        mesh=mesh,
        in_specs=(wide, flat, flat, flat, wide, wide, wide, wide, flat, wide, wide, wide, wide),
        out_specs=(wide, wide, flat, wide, wide, wide, wide, flat, wide, wide, wide),
        check_vma=False,
    )
```

time: 802 us -> 736 us (0.918)
  Pallas kernels: 37.6 us -> 85.1 us
  other arithmetic: 81.4 us -> 41.8 us
  starting transfers between devices: 128 us -> 93.5 us
  local copies, waits for them, and re-layouts: 84.5 us -> 51 us
  matrix products: 101 us -> 81.5 us
  between operations: 3.13 us -> 15.4 us
    pallas_call x2 -> x8, Pallas kernels: 37.6 us -> 85.1 us  [the longest x1 27.6 us: hidden_rows(): call(functools.partial(hidden_kernel, subs), [LIKE((rows, hidden), BF), L...]
    ppermute x116 -> x58, starting transfers between devices: 104 us -> 63.2 us  [the longest x22 35.8 us: ahead(): return lambda v: lax.ppermute(v, 'fsdp', pairs)]
    convert_element_type x19 -> x0, local copies, waits for them, and re-layouts: 19.4 us -> none  [the longest x15 18.8 us: rows_of(): join(got[:, :, i * each:(i + 1) * each]).astype(F32)]
    ppermute x116 -> x58, waiting for transfers between devices: 352 us -> 334 us  [the longest x22 240 us: ahead(): return lambda v: lax.ppermute(v, 'fsdp', pairs)]
    unnamed x11 -> x2, other arithmetic: 17.5 us -> 0.01 us
    dot_general x14 -> x7, matrix products: 31 us -> 15 us  [matmul(): return jnp.dot(left, right, preferred_element_type=F32)]
    dot_general x14 -> x8, matrix products: 39.5 us -> 24 us  [times_t(): lax.dot_general(left, right, (((1,), (1,)), ((), ())), preferred_element_...]
    unnamed x155 -> x132, local copies, waits for them, and re-layouts: 29.2 us -> 14.1 us
  transfers between devices with their start and end apart: 122 -> 69, of which waited for: 55 -> 36; matrix products, arithmetic and copies ran while one was open for 28% -> 20% of each run, Pallas kernels for 5% -> 8%
where the time goes in v3:
time: 736 us; the launch traced here: 728 us
  waiting for transfers between devices  360 us (49%)
  starting transfers between devices  93.5 us (13%)
  Pallas kernels  85.1 us (12%)
  matrix products  81.5 us (11%)
  local copies, waits for them, and re-layouts  51 us (7%)
  other arithmetic  41.8 us (6%)
  between operations  15.4 us (2%)
    ppermute x22, waiting for transfers between devices, ahead(): return lambda v: lax.ppermute(v, 'fsdp', pairs)  240 us
    ppermute x36, waiting for transfers between devices, flip(): return lambda v: lax.ppermute(v, 'fsdp', pairs)  93.7 us
    dot_general x8, matrix products, t_times(): lax.dot_general(left, right, (((0,), (0,)), ((), ())), preferred_element_...  42.5 us
    ppermute x22, starting transfers between devices, ahead(): return lambda v: lax.ppermute(v, 'fsdp', pairs)  35.8 us
    pallas_call x1, Pallas kernels, hidden_rows(): call(functools.partial(hidden_kernel, subs), [LIKE((rows, hidden), BF), L...  27.6 us
    ppermute x36, starting transfers between devices, flip(): return lambda v: lax.ppermute(v, 'fsdp', pairs)  27.3 us
    dot_general x8, matrix products, times_t(): lax.dot_general(left, right, (((1,), (1,)), ((), ())), preferred_element_...  24 us
    all_to_all x4, starting transfers between devices, exchange(): lax.all_to_all(v, 'fsdp', 0, 0, tiled=True, axis_index_groups=self.groups)  20.2 us
  transfers between devices with their start and end apart: 69, of which 36 were waited for; matrix products, arithmetic and copies ran while one was open for 20% of the time, Pallas kernels for 8%

profile of v3, /device:TPU:0, one launch (start us, length us, event | category | flops | bytes accessed | tf_op | source)
XLA Modules:
  0.0 728.1 jit_solution(13410273149796635896)
XLA Ops:
  10.5 6.3 all-to-all-start
  19.6 25.1 %collective-permute-done = bf16[64,2048]{1,0:T(8,128)(2,1)} collective-permute-done((bf16[64,2048]{1,0:T(8,128)(2,1)S(1)}, bf16[64,2048]{1,0:T(8,128)(2,1)}, u32[]{:S(2)}, u32[]{:S(2)}) %collective-permute-start) | collective-permute-done | bytes 262176 | tf_op jit(solution)/shard_map/ppermute | solution.py:404
  59.9 12.5 %all-to-all-done.1 = f32[32,1,384]{2,1,0:T(1,128)S(1)} async-done(((f32[32,1,384]{2,1,0:T(1,128)}), f32[32,1,384]{2,1,0:T(1,128)S(1)}, u32[]{:S(2)}, u32[]{:S(2)}) %all-to-all-start.1) | async-done | bytes 49184 | tf_op jit(solution)/shard_map/all_to_all | solution.py:574
  81.4 11.7 %collective-permute-done.2 = bf16[512,384]{1,0:T(8,128)(2,1)} collective-permute-done((bf16[512,384]{1,0:T(8,128)(2,1)S(1)}, bf16[512,384]{1,0:T(8,128)(2,1)}, u32[]{:S(2)}, u32[]{:S(2)}) %collective-permute-start.2) | collective-permute-done | bytes 393248 | tf_op jit(solution)/shard_map/ppermute | solution.py:404
  106.2 11.8 %shard_map.222 = (bf16[2048,2048]{1,0:T(8,128)(2,1)}, f32[2048,384]{1,0:T(8,128)}) custom-call(bf16[2048,2048]{1,0:T(8,128)(2,1)} %all-gather.5.cloned.1.call-done.x, f32[1,2048]{1,0:T(1,128)} %reshape.273.gain, bf16[2048,384]{1,0:T(8,128)(2,1)} %bitcast.84), custom_call_target="tpu_custom_call" | custom-call | flops 201326592 | bytes 1048576 | tf_op jit(solution)/shard_map/pallas_call | solution.py:269
  118.0 13.5 %shard_map.223 = (bf16[2,2048,128]{2,1,0:T(8,128)(2,1)}, bf16[2,2048,128]{2,1,0:T(8,128)(2,1)}, bf16[2048,128]{1,0:T(8,128)(2,1)}, bf16[2048,128]{1,0:T(8,128)(2...) custom-call(s32[48]{0:T(128)} %add.373.offsets, f32[2048,384]{1,0:T(8,128)} %get-tuple-element.233.qkv, ...), custom_call_target="tpu_custom_call" | custom-call | flops 268435456 | bytes 786432 | tf_op jit(solution)/shard_map/pallas_call | solution.py:227
  131.5 17.5 %collective-permute-done.3 = bf16[64,2048]{1,0:T(8,128)(2,1)S(1)} collective-permute-done((bf16[64,2048]{1,0:T(8,128)(2,1)S(1)}, bf16[64,2048]{1,0:T(8,128)(2,1)S(1)}, u32[]{:S(2)}, u32[]{:S(2)}) %collective-permute-start.3) | collective-permute-done | bytes 262176 | tf_op jit(solution)/shard_map/ppermute | solution.py:404
  159.1 9.4 %collective-permute-done.7 = bf16[64,2048]{1,0:T(8,128)(2,1)S(1)} collective-permute-done((bf16[64,2048]{1,0:T(8,128)(2,1)S(1)}, bf16[64,2048]{1,0:T(8,128)(2,1)S(1)}, u32[]{:S(2)}, u32[]{:S(2)}) %collective-permute-start.7) | collective-permute-done | bytes 262176 | tf_op jit(solution)/shard_map/ppermute | solution.py:404
  177.5 19.8 %collective-permute-done.8 = bf16[128,2048]{1,0:T(8,128)(2,1)S(1)} collective-permute-done((bf16[128,2048]{1,0:T(8,128)(2,1)S(1)}, bf16[128,2048]{1,0:T(8,128)(2,1)S(1)}, u32[]{:S(2)}, u32[]{:S(2)}) %collective-permute-start.8) | collective-permute-done | bytes 524320 | tf_op jit(solution)/shard_map/ppermute | solution.py:399
  211.9 6.8 collective-permute-done.15
  249.9 21.5 %collective-permute-done.20 = bf16[256,1024]{1,0:T(8,128)(2,1)S(1)} collective-permute-done((bf16[256,1024]{1,0:T(8,128)(2,1)S(1)}, bf16[256,1024]{1,0:T(8,128)(2,1)S(1)}, u32[]{:S(2)}, u32[]{:S(2)}) %collective-permute-start.20) | collective-permute-done | bytes 524320 | tf_op jit(solution)/shard_map/ppermute | solution.py:404
  274.6 10.7 %fusion.59.dm = f32[2048,512]{1,0:T(8,128)} fusion(bf16[2048,2048]{1,0:T(8,128)(2,1)} %all-gather.7.cloned.1.call-done, bf16[512,2048]{1,0:T(8,128)(2,1)} %bitcast.18), kind=kOutput, calls=%fused_computation.196 | convolution fusion | flops 4294967296 | bytes 14680064 | tf_op jit(solution)/shard_map/dot_general | solution.py:49
  285.3 11.7 %collective-permute-done.21 = bf16[256,1024]{1,0:T(8,128)(2,1)S(1)} collective-permute-done((bf16[256,1024]{1,0:T(8,128)(2,1)S(1)}, bf16[256,1024]{1,0:T(8,128)(2,1)S(1)}, u32[]{:S(2)}, u32[]{:S(2)}) %collective-permute-start.21) | collective-permute-done | bytes 524320 | tf_op jit(solution)/shard_map/ppermute | solution.py:404
  302.9 17.6 %collective-permute-done.22 = bf16[256,1024]{1,0:T(8,128)(2,1)S(1)} collective-permute-done((bf16[256,1024]{1,0:T(8,128)(2,1)S(1)}, bf16[256,1024]{1,0:T(8,128)(2,1)S(1)}, u32[]{:S(2)}, u32[]{:S(2)}) %collective-permute-start.22) | collective-permute-done | bytes 524320 | tf_op jit(solution)/shard_map/ppermute | solution.py:404
  321.4 27.6 %shard_map.225 = (bf16[2048,512]{1,0:T(8,128)(2,1)}, bf16[2048,1024]{1,0:T(8,128)(2,1)}, bf16[256,2048]{1,0:T(8,128)(2,1)}, bf16[384,2048]{1,0:T(8,128)(2,1)}, b...) custom-call(s32[25]{0:T(128)} %pad_add_fusion.1.spots, ...), custom_call_target="tpu_custom_call" | custom-call | flops 1073741824 | bytes 1572864 | tf_op jit(solution)/shard_map/pallas_call | solution.py:319
  349.6 8.0 %fusion.8 = bf16[1024,1024]{1,0:T(8,128)(2,1)S(1)} fusion(bf16[2048,1024]{1,0:T(8,128)(2,1)} %get-tuple-element.309, bf16[2048,2048]{1,0:T(8,128)(2,1)} %all-gather.9.cloned.1.call-done.h, s32[]{:T(128)S(6)} %select_n.253), kind=kOutput, calls=%fused_computation.31 | convolution fusion | flops 4296015872 | bytes 10485764 | tf_op jit(solution)/shard_map/dot_general | solution.py:53
  373.9 15.6 %collective-permute-done.26 = bf16[128,2048]{1,0:T(8,128)(2,1)S(1)} collective-permute-done((bf16[128,2048]{1,0:T(8,128)(2,1)S(1)}, bf16[128,2048]{1,0:T(8,128)(2,1)S(1)}, u32[]{:S(2)}, u32[]{:S(2)}) %collective-permute-start.26) | collective-permute-done | bytes 524320 | tf_op jit(solution)/shard_map/ppermute | solution.py:399
  426.4 10.1 %convolution_convert_fusion = bf16[2048,2048]{1,0:T(8,128)(2,1)} fusion(bf16[2048,512]{1,0:T(8,128)(2,1)} %get-tuple-element.341, bf16[512,2048]{1,0:T(8,128)(2,1)} %bitcast.18), kind=kOutput, calls=%fused_computation | convolution fusion | flops 4299161600 | bytes 12582912 | tf_op jit(solution)/shard_map/dot_general | solution.py:45
  436.5 6.3 convolution_convert_fusion.7
  442.8 18.8 %collective-permute-done.38 = bf16[256,1024]{1,0:T(8,128)(2,1)S(1)} collective-permute-done((bf16[256,1024]{1,0:T(8,128)(2,1)}, bf16[256,1024]{1,0:T(8,128)(2,1)S(1)}, u32[]{:S(2)}, u32[]{:S(2)}) %collective-permute-start.38) | collective-permute-done | bytes 524320 | tf_op jit(solution)/shard_map/ppermute | solution.py:404
  467.3 19.1 %collective-permute-done.39 = bf16[256,1024]{1,0:T(8,128)(2,1)} collective-permute-done((bf16[256,1024]{1,0:T(8,128)(2,1)S(1)}, bf16[256,1024]{1,0:T(8,128)(2,1)}, u32[]{:S(2)}, u32[]{:S(2)}) %collective-permute-start.39) | collective-permute-done | bytes 524320 | tf_op jit(solution)/shard_map/ppermute | solution.py:404
  486.4 8.3 %all-gather.11.cloned.1.call-done = bf16[2048,2048]{1,0:T(8,128)(2,1)} async-done(((bf16[128,2048]{1,0:T(8,128)(2,1)}), bf16[2048,2048]{1,0:T(8,128)(2,1)}) %all-gather.11.cloned.1.call-update) | async-done | bytes 8388624 | tf_op jit(solution)/shard_map/all_gather | solution.py:413
  494.7 6.7 convolution_convert_fusion.8.dout
  511.2 6.6 collective-permute-done.40
  524.0 7.5 %fusion.23 = f32[256,2048]{1,0:T(8,128)} fusion(bf16[2048,2048]{1,0:T(8,128)(2,1)} %all-gather.7.cloned.1.call-done, bf16[2048,512]{1,0:T(8,128)(2,1)} %get-tuple-element.341, s32[]{:T(128)S(6)} %select_n.257), kind=kOutput, calls=%fused_computation.73 | convolution fusion | flops 2147483648 | bytes 11534340 | tf_op jit(solution)/shard_map/dot_general | solution.py:53
  532.3 20.0 %shard_map.226 = (bf16[2048,384]{1,0:T(8,128)(2,1)}, bf16[2048,384]{1,0:T(8,128)(2,1)}) custom-call(s32[48]{0:T(128)} %add.373.offsets, bf16[2,2048,128]{2,1,0:T(8,128)(2,1)} %get-tuple-element.351.qe, bf16[2,2048,128]{2,1,0:T(8,128)(2,1)} %get-tuple-element.352.ke, bf16[2048,128]{1,0:T(8,128)(2,1)} %get-tuple-element.353.vs, ...), custom_call_target="tpu_custom_call" | custom-call | flops 671088640 | bytes 786432 | tf_op jit(solution)/shard_map/pallas_call | solution.py:245
  552.3 11.6 %collective-permute-done.41 = bf16[64,2048]{1,0:T(8,128)(2,1)} collective-permute-done((bf16[64,2048]{1,0:T(8,128)(2,1)}, bf16[64,2048]{1,0:T(8,128)(2,1)}, u32[]{:S(2)}, u32[]{:S(2)}) %collective-permute-start.41) | collective-permute-done | bytes 262176 | tf_op jit(solution)/shard_map/ppermute | solution.py:404
  577.0 20.4 %collective-permute-done.45 = bf16[128,2048]{1,0:T(8,128)(2,1)S(1)} collective-permute-done((bf16[128,2048]{1,0:T(8,128)(2,1)S(1)}, bf16[128,2048]{1,0:T(8,128)(2,1)S(1)}, u32[]{:S(2)}, u32[]{:S(2)}) %collective-permute-start.45) | collective-permute-done | bytes 524320 | tf_op jit(solution)/shard_map/ppermute | solution.py:404
  607.7 22.4 %collective-permute-done.49 = bf16[512,384]{1,0:T(8,128)(2,1)S(1)} collective-permute-done((bf16[512,384]{1,0:T(8,128)(2,1)S(1)}, bf16[512,384]{1,0:T(8,128)(2,1)S(1)}, u32[]{:S(2)}, u32[]{:S(2)}) %collective-permute-start.49) | collective-permute-done | bytes 393248 | tf_op jit(solution)/shard_map/ppermute | solution.py:404
  630.6 10.5 %collective-permute-done.47 = bf16[192,2048]{1,0:T(8,128)(2,1)S(1)} collective-permute-done((bf16[192,2048]{1,0:T(8,128)(2,1)S(1)}, bf16[192,2048]{1,0:T(8,128)(2,1)S(1)}, u32[]{:S(2)}, u32[]{:S(2)}) %collective-permute-start.47) | collective-permute-done | bytes 786464 | tf_op jit(solution)/shard_map/ppermute | solution.py:399
  646.9 7.7 %collective-permute-done.50 = bf16[64,2048]{1,0:T(8,128)(2,1)S(1)} collective-permute-done((bf16[64,2048]{1,0:T(8,128)(2,1)S(1)}, bf16[64,2048]{1,0:T(8,128)(2,1)S(1)}, u32[]{:S(2)}, u32[]{:S(2)}) %collective-permute-start.50) | collective-permute-done | bytes 262176 | tf_op jit(solution)/shard_map/ppermute | solution.py:399
  654.6 10.3 %collective-permute-done.51 = bf16[96,2048]{1,0:T(8,128)(2,1)S(1)} collective-permute-done((bf16[96,2048]{1,0:T(8,128)(2,1)S(1)}, bf16[96,2048]{1,0:T(8,128)(2,1)S(1)}, u32[]{:S(2)}, u32[]{:S(2)}) %collective-permute-start.51) | collective-permute-done | bytes 393248 | tf_op jit(solution)/shard_map/ppermute | solution.py:399
  (409 shorter events, 279.5 us)
Async XLA Ops:
  7.2 85.9 %all-gather.5.cloned.1.call-start = ((), (), s32[]{:S(2)}) async-start(), calls=%async_computation.7 | async-start | bytes 8912896 | tf_op jit(solution)/shard_map/all_gather | solution.py:413
  10.5 34.2 %all-to-all-start = ((bf16[16,64,384]{2,1,0:T(8,128)(2,1)}), bf16[16,64,384]{2,1,0:T(8,128)(2,1)S(1)}, u32[]{:S(2)}, u32[]{:S(2)}) async-start(bf16[16,64,384]{2,1,0:T(8,128)(2,1)} %shard_map.221), calls=%async_computation | async-start | bytes 1572864 | tf_op jit(solution)/shard_map/all_to_all | solution.py:410
  16.8 27.9 %collective-permute-start = (bf16[64,2048]{1,0:T(8,128)(2,1)S(1)}, bf16[64,2048]{1,0:T(8,128)(2,1)}, u32[]{:S(2)}, u32[]{:S(2)}) collective-permute-start(bf16[64,2048]{1,0:T(8,128)(2,1)S(1)} %copy-done.32), channel_id=1, source_target_pairs={{0,16},{1,17},{2,18},{3,19},{4,20},{5,21},{6,22},{7,23},{8,24},{9,... | collective-permute-start | bytes 786440 | tf_op jit(solution)/shard_map/ppermute | solution.py:404
  44.8 27.5 %collective-permute-start.1 = (bf16[512,384]{1,0:T(8,128)(2,1)S(1)}, bf16[512,384]{1,0:T(8,128)(2,1)S(1)}, u32[]{:S(2)}, u32[]{:S(2)}) collective-permute-start(bf16[512,384]{1,0:T(8,128)(2,1)S(1)} %bitcast.106), channel_id=1, source_target_pairs={{0,16},{1,17},{2,18},{3,19},{4,20},{5,21},{6,22},{7,23},{8,24},{9,... | collective-permute-start | bytes 1179656 | tf_op jit(solution)/shard_map/ppermute | solution.py:404
  55.9 194.0 %all-gather.7.cloned.1.call-start = ((), (), s32[]{:S(2)}) async-start(), calls=%async_computation.8 | async-start | bytes 8912896 | tf_op jit(solution)/shard_map/all_gather | solution.py:413
  93.1 55.9 %all-to-all-start.2 = ((bf16[16,64,1024]{2,1,0:T(8,128)(2,1)}), bf16[16,64,1024]{2,1,0:T(8,128)(2,1)}, u32[]{:S(2)}, u32[]{:S(2)}) async-start(bf16[16,64,1024]{2,1,0:T(8,128)(2,1)} %shard_map.224), calls=%async_computation.2 | async-start | bytes 4194304 | tf_op jit(solution)/shard_map/all_to_all | solution.py:410
  97.7 222.8 %all-gather.9.cloned.1.call-start = ((), (), s32[]{:S(2)}) async-start(), calls=%async_computation.9 | async-start | bytes 8912896 | tf_op jit(solution)/shard_map/all_gather | solution.py:413
  102.1 46.8 %collective-permute-start.3 = (bf16[64,2048]{1,0:T(8,128)(2,1)S(1)}, bf16[64,2048]{1,0:T(8,128)(2,1)S(1)}, u32[]{:S(2)}, u32[]{:S(2)}) collective-permute-start(bf16[64,2048]{1,0:T(8,128)(2,1)S(1)} %copy-done.45), channel_id=1, source_target_pairs={{0,16},{1,17},{2,18},{3,19},{4,20},{5,21},{6,22},{7,23},{8,24},{9,... | collective-permute-start | bytes 786440 | tf_op jit(solution)/shard_map/ppermute | solution.py:404
  171.1 31.5 %collective-permute-start.9 = (bf16[192,2048]{1,0:T(8,128)(2,1)S(1)}, bf16[192,2048]{1,0:T(8,128)(2,1)S(1)}, u32[]{:S(2)}, u32[]{:S(2)}) collective-permute-start(bf16[192,2048]{1,0:T(8,128)(2,1)S(1)} %slice.584), channel_id=1, source_target_pairs={{0,2},{1,3},{2,0},{3,1},{4,6},{5,7},{6,4},{7,5},{8,10},{9,11},{10,... | collective-permute-start | bytes 2359304 | tf_op jit(solution)/shard_map/ppermute | solution.py:399
  171.1 31.5 %collective-permute-start.10 = (bf16[192,2048]{1,0:T(8,128)(2,1)S(1)}, bf16[192,2048]{1,0:T(8,128)(2,1)S(1)}, u32[]{:S(2)}, u32[]{:S(2)}) collective-permute-start(bf16[192,2048]{1,0:T(8,128)(2,1)S(1)} %slice.583), channel_id=1, source_target_pairs={{0,4},{1,5},{2,6},{3,7},{4,0},{5,1},{6,2},{7,3},{8,12},{9,13},{10,... | collective-permute-start | bytes 2359304 | tf_op jit(solution)/shard_map/ppermute | solution.py:399
  172.3 25.0 %collective-permute-start.8 = (bf16[128,2048]{1,0:T(8,128)(2,1)S(1)}, bf16[128,2048]{1,0:T(8,128)(2,1)S(1)}, u32[]{:S(2)}, u32[]{:S(2)}) collective-permute-start(bf16[128,2048]{1,0:T(8,128)(2,1)S(1)} %slice.587), channel_id=1, source_target_pairs={{0,8},{1,9},{2,10},{3,11},{4,12},{5,13},{6,14},{7,15},{8,0},{9,1},... | collective-permute-start | bytes 1572872 | tf_op jit(solution)/shard_map/ppermute | solution.py:399
  177.5 25.0 %collective-permute-start.11 = (bf16[256,1024]{1,0:T(8,128)(2,1)S(1)}, bf16[256,1024]{1,0:T(8,128)(2,1)S(1)}, u32[]{:S(2)}, u32[]{:S(2)}) collective-permute-start(bf16[256,1024]{1,0:T(8,128)(2,1)S(1)} %bitcast.104), channel_id=1, source_target_pairs={{0,16},{1,17},{2,18},{3,19},{4,20},{5,21},{6,22},{7,23},{8,24},{9,... | collective-permute-start | bytes 1572872 | tf_op jit(solution)/shard_map/ppermute | solution.py:404
  237.6 257.1 %all-gather.11.cloned.1.call-start = ((), (), s32[]{:S(2)}) async-start(), calls=%async_computation.10 | async-start | bytes 8912896 | tf_op jit(solution)/shard_map/all_gather | solution.py:413
  271.4 25.7 %collective-permute-start.21 = (bf16[256,1024]{1,0:T(8,128)(2,1)S(1)}, bf16[256,1024]{1,0:T(8,128)(2,1)S(1)}, u32[]{:S(2)}, u32[]{:S(2)}) collective-permute-start(bf16[256,1024]{1,0:T(8,128)(2,1)S(1)} %bitcast.102), channel_id=1, source_target_pairs={{0,16},{1,17},{2,18},{3,19},{4,20},{5,21},{6,22},{7,23},{8,24},{9,... | collective-permute-start | bytes 1572872 | tf_op jit(solution)/shard_map/ppermute | solution.py:404
  365.9 23.6 %collective-permute-start.26 = (bf16[128,2048]{1,0:T(8,128)(2,1)S(1)}, bf16[128,2048]{1,0:T(8,128)(2,1)S(1)}, u32[]{:S(2)}, u32[]{:S(2)}) collective-permute-start(bf16[128,2048]{1,0:T(8,128)(2,1)S(1)} %slice.586), channel_id=1, source_target_pairs={{0,8},{1,9},{2,10},{3,11},{4,12},{5,13},{6,14},{7,15},{8,0},{9,1},... | collective-permute-start | bytes 1572872 | tf_op jit(solution)/shard_map/ppermute | solution.py:399
  366.0 26.5 %collective-permute-start.29 = (bf16[256,1024]{1,0:T(8,128)(2,1)S(1)}, bf16[256,1024]{1,0:T(8,128)(2,1)S(1)}, u32[]{:S(2)}, u32[]{:S(2)}) collective-permute-start(bf16[256,1024]{1,0:T(8,128)(2,1)S(1)} %get-tuple-element.313), channel_id=1, source_target_pairs={{0,16},{1,17},{2,18},{3,19},{4,20},{5,21},{6,22},{7,23},{8,24},{9,... | collective-permute-start | bytes 1572872 | tf_op jit(solution)/shard_map/ppermute | solution.py:404
  367.2 25.4 %collective-permute-start.27 = (bf16[192,2048]{1,0:T(8,128)(2,1)S(1)}, bf16[192,2048]{1,0:T(8,128)(2,1)S(1)}, u32[]{:S(2)}, u32[]{:S(2)}) collective-permute-start(bf16[192,2048]{1,0:T(8,128)(2,1)S(1)} %slice.582), channel_id=1, source_target_pairs={{0,2},{1,3},{2,0},{3,1},{4,6},{5,7},{6,4},{7,5},{8,10},{9,11},{10,... | collective-permute-start | bytes 2359304 | tf_op jit(solution)/shard_map/ppermute | solution.py:399
  367.2 25.4 %collective-permute-start.28 = (bf16[192,2048]{1,0:T(8,128)(2,1)S(1)}, bf16[192,2048]{1,0:T(8,128)(2,1)S(1)}, u32[]{:S(2)}, u32[]{:S(2)}) collective-permute-start(bf16[192,2048]{1,0:T(8,128)(2,1)S(1)} %slice.581), channel_id=1, source_target_pairs={{0,4},{1,5},{2,6},{3,7},{4,0},{5,1},{6,2},{7,3},{8,12},{9,13},{10,... | collective-permute-start | bytes 2359304 | tf_op jit(solution)/shard_map/ppermute | solution.py:399
  426.1 292.7 %reduce-scatter.2.cloned.1.call-start = ((), (), s32[]{:S(2)}) async-start(), calls=%async_computation.11 | async-start | bytes 8912896 | tf_op jit(solution)/shard_map/reduce_scatter | solution.py:416
  436.5 25.1 %collective-permute-start.38 = (bf16[256,1024]{1,0:T(8,128)(2,1)}, bf16[256,1024]{1,0:T(8,128)(2,1)S(1)}, u32[]{:S(2)}, u32[]{:S(2)}) collective-permute-start(bf16[256,1024]{1,0:T(8,128)(2,1)} %get-tuple-element.338), channel_id=1, source_target_pairs={{0,16},{1,17},{2,18},{3,19},{4,20},{5,21},{6,22},{7,23},{8,24},{9,... | collective-permute-start | bytes 1572872 | tf_op jit(solution)/shard_map/ppermute | solution.py:404
  461.6 24.8 %collective-permute-start.39 = (bf16[256,1024]{1,0:T(8,128)(2,1)S(1)}, bf16[256,1024]{1,0:T(8,128)(2,1)}, u32[]{:S(2)}, u32[]{:S(2)}) collective-permute-start(bf16[256,1024]{1,0:T(8,128)(2,1)S(1)} %copy-done.27), channel_id=1, source_target_pairs={{0,16},{1,17},{2,18},{3,19},{4,20},{5,21},{6,22},{7,23},{8,24},{9,... | collective-permute-start | bytes 1572872 | tf_op jit(solution)/shard_map/ppermute | solution.py:404
  517.8 49.9 %all-to-all-start.3 = ((bf16[16,64,1024]{2,1,0:T(8,128)(2,1)}), bf16[16,64,1024]{2,1,0:T(8,128)(2,1)}, u32[]{:S(2)}, u32[]{:S(2)}) async-start(bf16[16,64,1024]{2,1,0:T(8,128)(2,1)} %bitcast.28), calls=%async_computation.3 | async-start | bytes 4194304 | tf_op jit(solution)/shard_map/all_to_all | solution.py:410
  522.7 41.2 %collective-permute-start.41 = (bf16[64,2048]{1,0:T(8,128)(2,1)}, bf16[64,2048]{1,0:T(8,128)(2,1)}, u32[]{:S(2)}, u32[]{:S(2)}) collective-permute-start(bf16[64,2048]{1,0:T(8,128)(2,1)} %get-tuple-element.365), channel_id=1, source_target_pairs={{0,16},{1,17},{2,18},{3,19},{4,20},{5,21},{6,22},{7,23},{8,24},{9,... | collective-permute-start | bytes 786440 | tf_op jit(solution)/shard_map/ppermute | solution.py:404
  571.6 25.8 %collective-permute-start.43 = (bf16[384,2048]{1,0:T(8,128)(2,1)S(1)}, bf16[384,2048]{1,0:T(8,128)(2,1)S(1)}, u32[]{:S(2)}, u32[]{:S(2)}) collective-permute-start(bf16[384,2048]{1,0:T(8,128)(2,1)S(1)} %convolution_convert_fusion.2), channel_id=1, source_target_pairs={{0,1},{1,0},{2,3},{3,2},{4,5},{5,4},{6,7},{7,6},{8,9},{9,8},{10,11... | collective-permute-start | bytes 4718600 | tf_op jit(solution)/shard_map/ppermute | solution.py:399
  571.7 25.7 %collective-permute-start.44 = (bf16[384,2048]{1,0:T(8,128)(2,1)S(1)}, bf16[384,2048]{1,0:T(8,128)(2,1)S(1)}, u32[]{:S(2)}, u32[]{:S(2)}) collective-permute-start(bf16[384,2048]{1,0:T(8,128)(2,1)S(1)} %convolution_convert_fusion.1), channel_id=1, source_target_pairs={{0,1},{1,0},{2,3},{3,2},{4,5},{5,4},{6,7},{7,6},{8,9},{9,8},{10,11... | collective-permute-start | bytes 4718600 | tf_op jit(solution)/shard_map/ppermute | solution.py:399
  572.2 25.2 %collective-permute-start.42 = (bf16[256,2048]{1,0:T(8,128)(2,1)S(1)}, bf16[256,2048]{1,0:T(8,128)(2,1)S(1)}, u32[]{:S(2)}, u32[]{:S(2)}) collective-permute-start(bf16[256,2048]{1,0:T(8,128)(2,1)S(1)} %convolution_convert_fusion.5), channel_id=1, source_target_pairs={{0,1},{1,0},{2,3},{3,2},{4,5},{5,4},{6,7},{7,6},{8,9},{9,8},{10,11... | collective-permute-start | bytes 3145736 | tf_op jit(solution)/shard_map/ppermute | solution.py:399
  572.3 25.1 %collective-permute-start.45 = (bf16[128,2048]{1,0:T(8,128)(2,1)S(1)}, bf16[128,2048]{1,0:T(8,128)(2,1)S(1)}, u32[]{:S(2)}, u32[]{:S(2)}) collective-permute-start(bf16[128,2048]{1,0:T(8,128)(2,1)S(1)} %copy-done.24), channel_id=1, source_target_pairs={{0,16},{1,17},{2,18},{3,19},{4,20},{5,21},{6,22},{7,23},{8,24},{9,... | collective-permute-start | bytes 1572872 | tf_op jit(solution)/shard_map/ppermute | solution.py:404
  600.6 40.5 %collective-permute-start.47 = (bf16[192,2048]{1,0:T(8,128)(2,1)S(1)}, bf16[192,2048]{1,0:T(8,128)(2,1)S(1)}, u32[]{:S(2)}, u32[]{:S(2)}) collective-permute-start(bf16[192,2048]{1,0:T(8,128)(2,1)S(1)} %slice.580), channel_id=1, source_target_pairs={{0,2},{1,3},{2,0},{3,1},{4,6},{5,7},{6,4},{7,5},{8,10},{9,11},{10,... | collective-permute-start | bytes 2359304 | tf_op jit(solution)/shard_map/ppermute | solution.py:399
  600.7 40.4 %collective-permute-start.48 = (bf16[192,2048]{1,0:T(8,128)(2,1)S(1)}, bf16[192,2048]{1,0:T(8,128)(2,1)S(1)}, u32[]{:S(2)}, u32[]{:S(2)}) collective-permute-start(bf16[192,2048]{1,0:T(8,128)(2,1)S(1)} %slice.579), channel_id=1, source_target_pairs={{0,4},{1,5},{2,6},{3,7},{4,0},{5,1},{6,2},{7,3},{8,12},{9,13},{10,... | collective-permute-start | bytes 2359304 | tf_op jit(solution)/shard_map/ppermute | solution.py:399
  603.1 27.5 %collective-permute-start.46 = (bf16[128,2048]{1,0:T(8,128)(2,1)S(1)}, bf16[128,2048]{1,0:T(8,128)(2,1)S(1)}, u32[]{:S(2)}, u32[]{:S(2)}) collective-permute-start(bf16[128,2048]{1,0:T(8,128)(2,1)S(1)} %slice.585), channel_id=1, source_target_pairs={{0,8},{1,9},{2,10},{3,11},{4,12},{5,13},{6,14},{7,15},{8,0},{9,1},... | collective-permute-start | bytes 1572872 | tf_op jit(solution)/shard_map/ppermute | solution.py:399
  603.1 26.9 %collective-permute-start.49 = (bf16[512,384]{1,0:T(8,128)(2,1)S(1)}, bf16[512,384]{1,0:T(8,128)(2,1)S(1)}, u32[]{:S(2)}, u32[]{:S(2)}) collective-permute-start(bf16[512,384]{1,0:T(8,128)(2,1)S(1)} %get-tuple-element.383), channel_id=1, source_target_pairs={{0,16},{1,17},{2,18},{3,19},{4,20},{5,21},{6,22},{7,23},{8,24},{9,... | collective-permute-start | bytes 1179656 | tf_op jit(solution)/shard_map/ppermute | solution.py:404
  670.1 25.9 %all-to-all-start.4 = ((bf16[16,64,384]{2,1,0:T(8,128)(2,1)}), bf16[16,64,384]{2,1,0:T(8,128)(2,1)}, u32[]{:S(2)}, u32[]{:S(2)}) async-start(bf16[16,64,384]{2,1,0:T(8,128)(2,1)} %bitcast.29), calls=%async_computation.4 | async-start | bytes 1572864 | tf_op jit(solution)/shard_map/all_to_all | solution.py:410
  (100 other events, 1012.1 us)
Sparse Core Ops, SparseCore 0:
  9.7 81.2 all-gather.4
  92.5 82.8 all-gather.6
  237.7 78.1 all-gather.8
  426.2 68.4 all-gather.10
  518.0 144.1 reduce-scatter.1

commit v4 on v3

v4 whole, which is shorter than its diff:
```python
import functools

import jax
import jax.numpy as jnp
from jax import lax
from jax.experimental import pallas as pl
from jax.experimental.pallas import tpu as pltpu
from jax.sharding import PartitionSpec as P

HEADS = 32
HEAD_DIM = 64
SEQ = 2048
DOCS = 16


EPS = 1e-05
THETA = 130000.0
HIDE = -1e30
BF = jnp.bfloat16
F32 = jnp.float32
LANES = 2 * HEAD_DIM
HALF = HEAD_DIM // 2
BLOCK = 512
MIB = 2**20


def barrier(*values):
    return lax.optimization_barrier(values)


def norm_rows(v, gain):
    scale = lax.rsqrt(jnp.mean(v * v, axis=-1, keepdims=True) + EPS)
    return v * scale * gain


def matmul(left, right):
    return jnp.dot(left, right, preferred_element_type=F32)


def times_t(left, right):
    return lax.dot_general(left, right, (((1,), (1,)), ((), ())), preferred_element_type=F32)


def t_times(left, right):
    return lax.dot_general(left, right, (((0,), (0,)), ((), ())), preferred_element_type=F32)


def call(kernel, out_shape, in_specs, out_specs, vmem=56, grid=(), scratch=()):
    return pl.pallas_call(
        kernel,
        grid=grid,
        out_shape=out_shape,
        in_specs=in_specs,
        out_specs=out_specs,
        scratch_shapes=list(scratch),
        compiler_params=pltpu.CompilerParams(vmem_limit_bytes=vmem * MIB),
        cost_estimate=pl.CostEstimate(flops=2**26, bytes_accessed=2**20, transcendentals=0),
    )


LIKE = jax.ShapeDtypeStruct
IN_SMEM = pl.BlockSpec(memory_space=pltpu.SMEM)
IN_VMEM = pl.BlockSpec(memory_space=pltpu.VMEM)


def per_step(rows, columns):
    return pl.BlockSpec((rows, columns), lambda i: (i, 0))


def same(shape):
    return pl.BlockSpec(shape, lambda i: (0, 0))


def lane_index(shape):
    return lax.broadcasted_iota(jnp.int32, shape, len(shape) - 1)


def of_head(head, shape):
    return lane_index(shape) // HEAD_DIM == head


def swapped(v):
    first = lane_index(v.shape) % HEAD_DIM < HALF
    return jnp.where(first, pltpu.roll(v, LANES - HALF, 1), pltpu.roll(v, HALF, 1))


def parts_of(v):
    high = v.astype(BF)
    rest = v - high.astype(F32)
    mid = rest.astype(BF)
    return high, mid, (rest - mid.astype(F32)).astype(BF)


def in_lanes(columns, first, shape):
    lane = lane_index(shape)
    out = jnp.zeros(shape, BF)
    for c, column in enumerate(columns):
        out = jnp.where(lane == first + c, column, out)
    return out


def each_block(size, give):
    rows = SEQ // size

    def one(b, carry):
        q = (b % (size // 2)) * 2 + b // (size // 2)
        give(pl.ds(pl.multiple_of(b * rows, 128), rows), pl.ds(pl.multiple_of(q * rows, 128), rows))
        return carry

    lax.fori_loop(0, size, one, 0)


def each_piece(size, subs, offsets, give):
    rows = SEQ // size

    def one(b, carry):
        start = 0
        for r, sub in enumerate(subs):
            there = pl.ds(pl.multiple_of(offsets[r * size + b], 16), sub)
            give(pl.ds(pl.multiple_of(b * rows + start, 16), sub), there)
            start += sub
        return carry

    lax.fori_loop(0, size, one, 0)


def forward_kernel(
    size, subs, offsets, qkv, cosine, sine, q_mask, k_mask, qe, ke, vs, out, out32, railed
):
    def place(there, here):
        c, s = cosine[there, :], sine[there, :]
        for at, ends, mask in ((0, qe, q_mask), (1, ke, k_mask)):
            v = qkv[here, at * LANES : (at + 1) * LANES]
            turned = (v * c + swapped(v) * s).astype(BF)
            if at == 0:
                turned = turned * (HEAD_DIM**-0.5)
            hidden = mask[there, :]
            for head in range(2):
                ends[head, there, :] = jnp.where(of_head(head, turned.shape), turned, hidden)
        vs[there, :] = qkv[here, 2 * LANES :].astype(BF)

    each_block(size, place)
    shape = (BLOCK, LANES)
    diagonal = lax.broadcasted_iota(jnp.int32, (BLOCK, BLOCK), 0) >= lane_index((BLOCK, BLOCK))
    for i in range(SEQ // BLOCK):
        mine = slice(i * BLOCK, (i + 1) * BLOCK)
        outs = []
        for head in range(2):
            spare = (1 - head) * HEAD_DIM
            query = qe[head, mine, :]
            scores = []
            for j in range(i + 1):
                s = times_t(query, ke[head, j * BLOCK : (j + 1) * BLOCK, :])
                scores.append(jnp.where(diagonal, s, HIDE) if j == i else s)
            top = functools.reduce(jnp.maximum, scores)
            top = jnp.max(top, axis=1, keepdims=True)
            total = jnp.zeros(shape, F32)
            for j, s in enumerate(scores):
                probs = jnp.exp(s - top).astype(BF)
                value = vs[j * BLOCK : (j + 1) * BLOCK, :]
                value = jnp.where(of_head(head, shape), value, jnp.ones((), BF))
                total += matmul(probs, value)
            weight = total[:, spare : spare + 1]
            outs.append(total / weight)
            logsum = top + jnp.log(weight)
            qe[head, mine, :] = query + in_lanes(parts_of(-logsum), spare + HALF, shape)
        out32[mine, :] = jnp.where(of_head(0, shape), outs[0], outs[1])

    def send(there, here):
        out[here, :] = out32[there, :].astype(BF)

    def rail(there, here):
        railed[here, :] = out32[there, :].astype(BF)

    each_block(size, send)
    each_piece(size, subs, offsets, rail)


def backward_kernel(
    size,
    subs,
    offsets,
    qe,
    ke,
    vs,
    out32,
    dout,
    cosine,
    sine,
    grads,
    railed,
    de,
    dq,
    dk,
    dv,
    turned,
):
    def place(there, here):
        grad = dout[here, :]
        weighted = grad.astype(F32) * out32[there, :]
        for head in range(2):
            own = of_head(head, grad.shape)
            delta = jnp.sum(jnp.where(own, weighted, 0.0), axis=1, keepdims=True)
            extra = in_lanes(parts_of(-delta), (1 - head) * HEAD_DIM, grad.shape)
            de[head, there, :] = jnp.where(own, grad, extra)

    each_block(size, place)
    shape = (BLOCK, LANES)
    diagonal = lax.broadcasted_iota(jnp.int32, (BLOCK, BLOCK), 0) <= lane_index((BLOCK, BLOCK))
    lane = lane_index(shape)
    for head in range(2):
        spare = (1 - head) * HEAD_DIM
        ones = jnp.where((lane >= spare) & (lane < spare + 3), jnp.ones((), BF), jnp.zeros((), BF))
        for j in range(SEQ // BLOCK):
            theirs = slice(j * BLOCK, (j + 1) * BLOCK)
            key = ke[head, theirs, :]
            value = jnp.where(of_head(head, shape), vs[theirs, :], ones)
            dkey = jnp.zeros(shape, F32)
            dvalue = jnp.zeros(shape, F32)
            for i in range(j, SEQ // BLOCK):
                mine = slice(i * BLOCK, (i + 1) * BLOCK)
                query = qe[head, mine, :]
                grad = de[head, mine, :]
                probs = jnp.exp(times_t(key, query))
                if i == j:
                    probs = jnp.where(diagonal, probs, 0.0)
                dscore = (probs * times_t(value, grad)).astype(BF)
                dvalue += matmul(probs.astype(BF), grad)
                dkey += matmul(dscore, query)
                dquery = t_times(dscore, key)
                if j > 0:
                    dquery += dq[head, mine, :]
                dq[head, mine, :] = dquery
            dk[head, theirs, :] = dkey
            dv[head, theirs, :] = dvalue
    for i in range(SEQ // BLOCK):
        mine = slice(i * BLOCK, (i + 1) * BLOCK)
        c, s = cosine[mine, :], sine[mine, :]
        first = of_head(0, shape)
        query = jnp.where(first, dq[0, mine, :], dq[1, mine, :]) * (HEAD_DIM**-0.5)
        key = jnp.where(first, dk[0, mine, :], dk[1, mine, :])
        for at, v in ((0, query), (1, key)):
            back = v * c - swapped(v) * s
            turned[mine, at * LANES : (at + 1) * LANES] = back.astype(BF)
        value = jnp.where(first, dv[0, mine, :], dv[1, mine, :])
        turned[mine, 2 * LANES :] = value.astype(BF)

    def send(there, here):
        grads[here, :] = turned[there, :]

    def rail(there, here):
        railed[here, :] = turned[there, :]

    each_block(size, send)
    each_piece(size, subs, offsets, rail)


def attend_forward(size, subs, offsets, qkv, cosine, sine, q_mask, k_mask):
    return call(
        functools.partial(forward_kernel, size, subs),
        [
            LIKE((2, SEQ, LANES), BF),
            LIKE((2, SEQ, LANES), BF),
            LIKE((SEQ, LANES), BF),
            LIKE((SEQ, LANES), BF),
            LIKE((SEQ, LANES), F32),
            LIKE((SEQ, LANES), BF),
        ],
        [IN_SMEM] + [IN_VMEM] * 5,
        [IN_VMEM] * 6,
    )(offsets, qkv, cosine, sine, q_mask, k_mask)


def attend_backward(size, subs, offsets, qe, ke, vs, out32, dout, cosine, sine):
    return call(
        functools.partial(backward_kernel, size, subs),
        [LIKE((SEQ, 3 * LANES), BF)] * 2,
        [IN_SMEM] + [IN_VMEM] * 7,
        [IN_VMEM] * 2,
        scratch=[
            pltpu.VMEM((2, SEQ, LANES), BF),
            pltpu.VMEM((2, SEQ, LANES), F32),
            pltpu.VMEM((2, SEQ, LANES), F32),
            pltpu.VMEM((2, SEQ, LANES), F32),
            pltpu.VMEM((SEQ, 3 * LANES), BF),
        ],
    )(offsets, qe, ke, vs, out32, dout, cosine, sine)


def project_kernel(x, gain, w, h, out):
    h[...] = norm_rows(x[...].astype(F32), gain[...]).astype(BF)
    out[...] = matmul(h[...], w[...])


def norm_project(x, gain, w):
    rows, width = x.shape
    step, columns = 256, w.shape[1]
    return call(
        project_kernel,
        [LIKE((rows, width), BF), LIKE((rows, columns), F32)],
        [per_step(step, width), same((1, width)), same((width, columns))],
        [per_step(step, width), per_step(step, columns)],
        grid=(rows // step,),
    )(x, gain, w)


def hand_out(subs, spots, product, sent, kept):
    rows = sum(subs)
    chips = SEQ // (2 * rows)
    core, chip = pl.program_id(0) % 2, pl.program_id(0) // 2
    for side, outs in ((spots[0], kept), (1 - spots[0], sent)):

        @pl.when(core == side)
        def _():
            for half in range(2):
                start = half * rows
                for r, sub in enumerate(subs):
                    there = spots[1 + r * chips + half * (chips // 2) + chip]
                    outs[r][pl.ds(pl.multiple_of(there, 16), sub), :] = product[start : start + sub]
                    start += sub


def hidden_kernel(subs, spots, h, w_gate, w_up, dm, mixed, dgate, dup, *outs):
    rails = len(subs)
    gate, up, grad = matmul(h[...], w_gate[...]), matmul(h[...], w_up[...]), dm[...]
    sig = 1.0 / (1.0 + jnp.exp(-gate))
    silu = gate * sig
    mixed[...] = (silu * up).astype(BF)
    dgate[...] = (grad * up * (sig + silu * (1.0 - sig))).astype(BF)
    dup[...] = (grad * silu).astype(BF)
    product = times_t(dgate[...], w_gate[...]) + times_t(dup[...], w_up[...])
    hand_out(subs, spots, product.astype(BF), outs[:rails], outs[rails:])


def hidden_rows(subs, spots, h, w_gate, w_up, dm):
    rows, width = h.shape
    hidden = dm.shape[1]
    step = 2 * sum(subs)
    rails = [LIKE((rows // step * sub, width), BF) for sub in subs]
    made = call(
        functools.partial(hidden_kernel, subs),
        [LIKE((rows, hidden), BF)] * 3 + rails + rails,
        [IN_SMEM, per_step(step, width), same(w_gate.shape), same(w_up.shape), per_step(step, hidden)],
        [per_step(step, hidden)] * 3 + [IN_VMEM] * (2 * len(subs)),
        grid=(rows // step,),
    )(spots, h, w_gate, w_up, dm)
    return *made[:3], made[3 : 3 + len(subs)], made[3 + len(subs) :]


def product_kernel(subs, spots, left, right, *outs):
    product = matmul(left[...], right[...]).astype(BF)
    hand_out(subs, spots, product, outs[: len(subs)], outs[len(subs) :])


def products(subs, spots, left, right):
    rows, depth = left.shape
    width = right.shape[1]
    step = 2 * sum(subs)
    rails = [LIKE((rows // step * sub, width), BF) for sub in subs]
    made = call(
        functools.partial(product_kernel, subs),
        rails + rails,
        [IN_SMEM, per_step(step, depth), same(right.shape)],
        [IN_VMEM] * (2 * len(subs)),
        vmem=24,
        grid=(rows // step,),
    )(spots, left, right)
    return made[: len(subs)], made[len(subs) :]


def fold_kernel(rails, last, *refs):
    held, got, outs = refs[:rails], refs[rails : 2 * rails], refs[2 * rails :]
    for r in range(rails):
        half = held[r].shape[0] // 2
        total = held[r][...].astype(F32) + got[r][...].astype(F32)
        outs[r][...] = total[half:].astype(BF)
        outs[rails + r][...] = total[:half]
        if last:
            outs[2 * rails + r][...] = total[:half].astype(BF)


def fold(held, got, last=False):
    rails, width = len(held), held[0].shape[1]
    step = width // 4

    def block(rows):
        return pl.BlockSpec((rows, step), lambda i: (0, i))

    halves = [v.shape[0] // 2 for v in held]
    kinds = [BF, F32] + [BF] * last
    made = call(
        functools.partial(fold_kernel, rails, last),
        [LIKE((h, width), kind) for kind in kinds for h in halves],
        [block(v.shape[0]) for v in (*held, *got)],
        [block(h) for kind in kinds for h in halves],
        vmem=16,
        grid=(4,),
    )(*held, *got)
    return [made[i : i + rails] for i in range(0, len(made), rails)]


def pair_rows(rails, half, refs):
    lower, came, upper, other = (refs[i * rails : (i + 1) * rails] for i in range(4))
    sub = lower[0].shape[0]
    for r in range(rails):
        for side, a, b in ((half, lower, came), (1 - half, upper, other)):
            at = pl.ds(pl.multiple_of(side * (rails * sub) + r * sub, 16), sub)
            yield at, a[r][...].astype(F32) + b[r][...].astype(F32)


def residual_kernel(rails, half, x, gain, *refs):
    sums, (x2, h) = refs[:-2], refs[-2:]
    for at, total in pair_rows(rails, half[0], sums):
        v = x[at, :].astype(F32) + total
        x2[at, :] = v
        h[at, :] = norm_rows(v, gain[...]).astype(BF)


def residual(half, x, gain, sums):
    return call(
        functools.partial(residual_kernel, len(sums) // 4),
        [LIKE(x.shape, F32), LIKE(x.shape, BF)],
        [IN_SMEM] + [IN_VMEM] * (2 + len(sums)),
        [IN_VMEM] * 2,
        vmem=24,
    )(half, x, gain, *sums)


def norm_back(v, gain, grad):
    scale = lax.rsqrt(jnp.mean(v * v, axis=-1, keepdims=True) + EPS)
    hat = v * scale
    weighted = gain * grad
    back = scale * (weighted - hat * jnp.mean(hat * weighted, axis=-1, keepdims=True))
    return back, jnp.sum(grad * hat, axis=0, keepdims=True)


def pair_back_kernel(rails, half, v, base, gain, *refs):
    sums, (out, rounded, part) = refs[:-3], refs[-3:]
    part[...] = jnp.zeros_like(part)
    for at, total in pair_rows(rails, half[0], sums):
        back, share = norm_back(v[at, :], gain[...], total)
        made = base[at, :].astype(F32) + back
        out[at, :] = made
        rounded[at, :] = made.astype(BF)
        part[...] += 0.5 * share


def pair_back(half, v, base, gain, sums):
    return call(
        functools.partial(pair_back_kernel, len(sums) // 4),
        [LIKE(v.shape, F32), LIKE(v.shape, BF), LIKE((1, v.shape[1]), F32)],
        [IN_SMEM] + [IN_VMEM] * (3 + len(sums)),
        [IN_VMEM] * 3,
        vmem=32,
    )(half, v, base, gain, *sums)


def own_rows(rails, half, refs, rows):
    lower, came = refs[:rails], refs[rails : 2 * rails]
    sub = lower[0].shape[0]
    for r in range(rails):
        at = pl.ds(pl.multiple_of(half * rows + r * sub, 16), sub)
        yield slice(r * sub, (r + 1) * sub), at, lower[r][...] + came[r][...].astype(F32)


def own_back_kernel(rails, half, v, base, gain, *refs):
    sums, (out, part) = refs[:-2], refs[-2:]
    part[...] = jnp.zeros_like(part)
    for mine, at, total in own_rows(rails, half[0], sums, v.shape[0]):
        back, share = norm_back(v[mine, :].astype(F32), gain[...], total)
        out[mine, :] = base[at, :] + back
        part[...] += share


def own_back(half, v, base, gain, sums):
    return call(
        functools.partial(own_back_kernel, len(sums) // 2),
        [LIKE(v.shape, F32), LIKE((1, v.shape[1]), F32)],
        [IN_SMEM] + [IN_VMEM] * (3 + len(sums)),
        [IN_VMEM] * 2,
        vmem=24,
    )(half, v, base, gain, *sums)


def result_kernel(rails, half, base, *refs):
    sums, out = refs[:-1], refs[-1]
    for mine, at, total in own_rows(rails, half[0], sums, out.shape[0]):
        out[mine, :] = (base[at, :] + total).astype(BF)


def own_result(half, base, sums):
    rows, width = base.shape
    return call(
        functools.partial(result_kernel, len(sums) // 2),
        LIKE((rows // 2, width), BF),
        [IN_SMEM] + [IN_VMEM] * (1 + len(sums)),
        IN_VMEM,
        vmem=24,
    )(half, base, *sums)


def cut_kernel(size, first, each, blocks, *refs):
    out = refs[-1]
    for d in range(out.shape[0]):
        p, at = d % size, 0
        for w in refs[:-1]:
            for j in range(blocks):
                out[d, :, at : at + each] = w[:, first(j, p) : first(j, p) + each]
                at += each


def cut_columns(weights, count, size, first, each, blocks):
    rows = weights[0].shape[0]
    columns = each * blocks * len(weights)
    return call(
        functools.partial(cut_kernel, size, first, each, blocks),
        LIKE((count, rows, columns), BF),
        [IN_VMEM] * len(weights),
        IN_VMEM,
        vmem=32,
    )(*weights)


def join_kernel(size, first, each, blocks, v, *outs):
    for p in range(size):
        at = 0
        for out in outs:
            for j in range(blocks):
                total = v[p, :, at : at + each].astype(F32)
                for d in range(p + size, v.shape[0], size):
                    total += v[d, :, at : at + each].astype(F32)
                out[:, first(j, p) : first(j, p) + each] = total
                at += each


def join_columns(v, parts, size, first, each, blocks):
    rows = v.shape[1]
    return call(
        functools.partial(join_kernel, size, first, each, blocks),
        [LIKE((rows, size * each * blocks), F32)] * parts,
        [IN_VMEM],
        [IN_VMEM] * parts,
        vmem=32,
    )(v)


class Team:
    def __init__(self, rows, count):
        self.rows, self.count = rows, count
        self.size = SEQ // rows
        self.teams = count // self.size
        self.groups = [[t * self.size + p for p in range(self.size)] for t in range(self.teams)]
        each = self.size // 2
        self.halves = [[h * each + p for p in range(each)] for h in range(2 * self.teams)]
        axes = [2 << k for k in range(self.size.bit_length() - 2)]
        first, rest = axes[-1:], axes[:-1]
        self.rails = [tuple(first + rest[r:] + rest[:r]) for r in range(len(rest))]
        self.subs = (rows // len(rest),) * len(rest)

    def flip(self, mask):
        pairs = [(i, i ^ mask) for i in range(self.count)]
        return lambda v: lax.ppermute(v, "fsdp", pairs)

    def ahead(self, teams):
        step = teams * self.size
        pairs = [(i, (i + step) % self.count) for i in range(self.count)]
        return lambda v: lax.ppermute(v, "fsdp", pairs)

    def stay(self, v):
        return v

    def everywhere(self, v):
        return lax.all_to_all(v, "fsdp", 0, 0, tiled=True)

    def gather(self, v):
        return lax.all_gather(v, "fsdp", axis=0, tiled=True, axis_index_groups=self.halves)

    def spots(self, place):
        away = 2 * jnp.arange(self.size // 2, dtype=jnp.int32) ^ place
        out = []
        for rail, sub in zip(self.rails, self.subs):
            at = jnp.zeros_like(away)
            for k, mask in enumerate(rail):
                at = at + jnp.where(away & mask != 0, sub << k, 0)
            out.append(at)
        return jnp.stack(out).astype(jnp.int32)

    def offsets(self, place):
        starts = jnp.cumsum(jnp.array((0,) + self.subs[:-1], jnp.int32)) * (self.size // 2)
        chip = self.spots(place) + starts[:, None]
        other = (jnp.arange(2, dtype=jnp.int32) ^ place) & 1
        return (chip[:, :, None] + other * (SEQ // 2)).reshape(-1).astype(jnp.int32)

    def cut(self, v):
        out, start = [], 0
        for sub in self.subs:
            each = sub * self.size // 2
            out.append(v[start : start + each])
            start += each
        return out

    def one(self, v, move):
        [got] = yield [(v, move)]
        return got

    def pair_up(self, v, half):
        [got] = yield [(v, self.flip(self.size // 2))]
        return jnp.where(half == 0, jnp.concatenate([v, got]), jnp.concatenate([got, v]))

    def scatter(self, sent, kept, pair):
        held, got = kept, (yield [(s, self.flip(1)) for s in sent])
        for step in reversed(range(1, len(self.rails[0]))):
            upper, held = fold(held, got)
            got = yield [(u, self.flip(rail[step])) for u, rail in zip(upper, self.rails)]
        upper, held, rounded = fold(held, got, last=True)
        move = self.flip(self.size // 2)
        if not pair:
            got = yield [(u, move) for u in upper]
            return [*held, *got]
        got = yield [(u, move) for u in (*upper, *rounded)]
        return [*held, *got[: len(held)], *upper, *got[len(held) :]]

    def spread(self, block, chunks, mine):
        got, start = [[] for _ in range(self.teams)], 0
        for chunk in chunks:
            each = block.shape[0] * chunk // 16
            part = block[start : start + each]
            start += each
            new = yield [(part, self.ahead(s)) for s in range(1, self.teams)]
            for s, piece in enumerate(new):
                got[s + 1].append(piece)
        held = jnp.zeros((self.teams,) + block.shape, block.dtype)
        held = lax.dynamic_update_index_in_dim(held, block, mine, 0)
        for s in range(1, self.teams):
            at, start = (mine - s) % self.teams, 0
            for piece in got[s]:
                held = lax.dynamic_update_slice(held, piece[None], (at, start, 0))
                start += piece.shape[0]
        return held.reshape((-1,) + block.shape[1:])

    def columns(self, cut):
        [got] = yield [(cut, self.everywhere)]
        return got.reshape(-1, got.shape[2])

    def owners(self, made):
        [got] = yield [(made.reshape(self.count, -1, made.shape[1]), self.everywhere)]
        return got

    def add(self, left, right, chunks, mine):
        width = left.shape[1] // self.teams

        def product(team):
            return t_times(lax.dynamic_slice_in_dim(left, team * width, width, 1), right)

        sent = [product((mine + s) % self.teams).astype(BF) for s in range(1, self.teams)]
        got, start = [[] for _ in sent], 0
        for chunk in chunks:
            each = width * chunk // 16
            moves = [(v[start : start + each], self.ahead(s + 1)) for s, v in enumerate(sent)]
            start += each
            if start == width:
                *new, total = yield moves + [(product(mine), self.stay)]
            else:
                new = yield moves
            for s, piece in enumerate(new):
                got[s].append(piece)
        for pieces in got:
            total = total + jnp.concatenate(pieces).astype(F32)
        return total


class Transfer:
    def __init__(self, steps):
        self.steps, self.value, self.over, self.got = steps, None, False, None
        self.moves = next(steps)

    def take(self):
        got, self.got = self.got, None
        try:
            self.moves = self.steps.send(got)
        except StopIteration as end:
            self.value, self.over, self.moves = end.value, True, []


class Clock:
    def __init__(self, token):
        self.token = token

    def start(self, *transfers):
        given = [v for t in transfers for v, _ in t.moves]
        given = list(barrier(self.token, *given)[1:])
        for t in transfers:
            t.got = [move(given.pop(0)) for _, move in t.moves]

    def beside(self, transfer, *values):
        tied = list(barrier(*values, *[v for v, _ in transfer.moves]))
        values, rest = tied[: len(values)], tied[len(values) :]
        transfer.moves = [(v, move) for v, (_, move) in zip(rest, transfer.moves)]
        return values

    def wait(self, transfers, *values):
        tied = list(barrier(self.token, *values, *[g for t in transfers for g in t.got]))
        self.token, values, rest = tied[0], tied[1 : 1 + len(values)], tied[1 + len(values) :]
        for t in transfers:
            t.got = [rest.pop(0) for _ in t.got]
        for t in transfers:
            t.take()
        return values


def local(
    tokens,
    segments,
    positions,
    gain_attn,
    w_query,
    w_key,
    w_value,
    w_out,
    gain_mlp,
    w_gate,
    w_up,
    w_down,
    cotangent,
):
    rows, width = tokens.shape
    count = lax.axis_size("fsdp")
    team = Team(rows, count)
    size, teams = team.size, team.teams
    index = lax.axis_index("fsdp")
    mine = index // size
    place = index % size
    own = w_query.shape[0]
    whole_heads = own % HEAD_DIM == 0
    ff_own = w_down.shape[0]
    if whole_heads:
        head_cut = (lambda j, p: (j * size + p) * HEAD_DIM, HEAD_DIM, 2)
    else:
        head_cut = (lambda j, p: p * LANES, LANES, 1)
    ff_cut = (lambda j, p: (j * size + p) * ff_own, ff_own, teams)

    def across(move, *args):
        return Transfer(move(*args, mine))

    clock = Clock(positions)
    start, wait = clock.start, clock.wait
    half = place // (size // 2)
    subs = team.subs

    pair_x = Transfer(team.pair_up(tokens, half))
    pair_dy = Transfer(team.pair_up(cotangent, half))
    start(pair_x)
    cut_qkv = cut_columns([w_query, w_key, w_value], count, size, *head_cut)
    [cut_qkv] = wait([pair_x], cut_qkv)
    x_pair = pair_x.value
    get_qkv = Transfer(team.columns(cut_qkv))
    get_x = Transfer(team.one(x_pair, team.gather))
    start(get_x, get_qkv, pair_dy)
    cut_gate = cut_columns([w_gate], count, size, *ff_cut)
    cut_up = cut_columns([w_up], count, size, *ff_cut)
    small = jnp.concatenate([v.astype(F32) for v in (gain_attn, gain_mlp, segments, positions)])
    small = jnp.broadcast_to(small[None], (count, small.shape[0]))
    small = Transfer(team.one(small, team.everywhere))
    cut_gate, cut_up = wait([pair_dy, get_qkv], cut_gate, cut_up)
    dy_pair = pair_dy.value
    get_dy = Transfer(team.one(dy_pair, team.gather))
    get_gate = Transfer(team.columns(cut_gate))
    get_up = Transfer(team.columns(cut_up))
    get_down = across(team.spread, w_down, [16])
    start(get_gate, small, get_dy)
    moving = []
    if whole_heads:
        get_out = across(team.spread, w_out, [16])
        start(get_out)
        moving.append(get_out)
    wait([small])
    small = small.value
    gain_one = small[:, :own].reshape(1, -1)
    gain_two = small[:, own : 2 * own].reshape(1, -1)
    small = lax.dynamic_slice_in_dim(small, mine * size, size, 0)
    docs = small[:, 2 * own : 2 * own + rows].reshape(SEQ, 1)
    places = small[:, 2 * own + rows :].reshape(SEQ, 1)
    freqs = THETA ** (-jnp.arange(HALF, dtype=F32) * 2.0 / HEAD_DIM)
    angles = places * freqs[None, :]
    cosine, sine = jnp.cos(angles), jnp.sin(angles)
    cosine = jnp.concatenate([cosine] * 4, axis=1)
    sine = jnp.concatenate([-sine, sine] * 2, axis=1)
    lane = jnp.arange(LANES)[None, :] % HEAD_DIM
    number = lane.astype(F32)
    q_mask = jnp.where((lane < DOCS) & (docs != number), HIDE, 0.0).astype(BF)
    tail = (lane >= HALF) & (lane < HALF + 3)
    k_mask = jnp.where(((lane < DOCS) & (docs == number)) | tail, 1.0, 0.0).astype(BF)
    offsets = team.offsets(place)
    spots = jnp.concatenate([place[None] % 2, team.spots(place).reshape(-1)]).astype(jnp.int32)
    here = half[None].astype(jnp.int32)
    cosine, sine, q_mask, k_mask, gain_one, gain_two, offsets, spots = wait(
        moving, cosine, sine, q_mask, k_mask, gain_one, gain_two, offsets, spots
    )
    w_qkv = get_qkv.value
    if whole_heads:
        out_rows = get_out.value
    else:
        out_rows = lax.dynamic_slice_in_dim(
            lax.all_gather(w_out, "fsdp", axis=0, tiled=True), place * LANES, LANES
        )
    [w_qkv] = wait([get_x], w_qkv)
    h1, qkv = norm_project(get_x.value, gain_one, w_qkv)
    qe, ke, vs, out, out32, railed = attend_forward(
        size, subs, offsets, qkv, cosine, sine, q_mask, k_mask
    )
    [railed] = wait([], railed)

    def rail_products(left, times):
        cut = team.cut(left[: SEQ // 2]), team.cut(left[SEQ // 2 :])
        return [times(v).astype(BF) for v in cut[1]], [times(v).astype(BF) for v in cut[0]]

    sent, kept = rail_products(railed, lambda v: matmul(v, out_rows))
    sent = wait([], *sent)
    add_out = Transfer(team.scatter(sent, kept, True))
    start(add_out)
    wait([add_out, get_gate])
    start(add_out, get_down)
    wait([add_out])
    start(add_out)
    wait([add_out, get_down])
    start(add_out)
    wait([add_out])
    x2, h2 = residual(here, x_pair, gain_two, add_out.value)
    get_h2 = Transfer(team.one(h2, team.gather))
    start(get_h2, get_up)
    wait([get_dy])
    dy, down_rows = get_dy.value, get_down.value
    dm = times_t(dy, down_rows)
    [dm] = wait([get_h2, get_up], dm)
    h2 = get_h2.value
    mixed, dgate, dup, sent, kept = hidden_rows(
        subs, spots, h2, get_gate.value, get_up.value, dm
    )

    add_dh2 = Transfer(team.scatter(sent, kept, True))
    start(add_dh2)
    send_down = across(team.add, mixed, dy, [16])
    wait([add_dh2])
    start(add_dh2, send_down)
    grad_gate = t_times(h2, dgate).astype(BF)
    [grad_gate] = wait([add_dh2], grad_gate)
    start(add_dh2)
    result_parts = products(subs, spots, mixed, down_rows)
    result_parts = [wait([], *part) for part in result_parts]
    wait([add_dh2, send_down])
    add_result = Transfer(team.scatter(*result_parts, False))
    start(add_dh2, add_result)
    wait([add_result])
    start(add_result)
    grad_up = t_times(h2, dup).astype(BF)
    [grad_up] = wait([add_dh2, add_result], grad_up)
    dx2, da, gain_two_part = pair_back(here, x2, dy_pair, gain_two, add_dh2.value)
    get_da = Transfer(team.one(da, team.gather))
    send_gate = Transfer(team.owners(grad_gate))
    send_up = Transfer(team.owners(grad_up))
    start(get_da, send_gate)
    wait([get_da, send_gate])
    da = get_da.value
    start(send_up, add_result)
    dout = times_t(da, out_rows).astype(BF)
    dqkv, railed = attend_backward(size, subs, offsets, qe, ke, vs, out32, dout, cosine, sine)
    sent, kept = rail_products(railed, lambda v: times_t(v, w_qkv))
    dqkv, *sent = wait([add_result], dqkv, *sent)
    add_dh1 = Transfer(team.scatter(sent, kept, False))
    start(add_dh1)
    grad_qkv = t_times(h1, dqkv).astype(BF)
    [grad_qkv] = wait([add_dh1, send_up], grad_qkv)
    send_qkv = Transfer(team.owners(grad_qkv))
    start(add_dh1, add_result, send_qkv)
    grad_gate = join_columns(send_gate.value, 1, size, *ff_cut)[0]
    [grad_gate] = wait([add_dh1, add_result], grad_gate)
    start(add_dh1)
    if whole_heads:
        send_out = across(team.add, out, da, [16])
        start(send_out)
    else:
        grad_out = lax.psum(
            t_times(out, da), "fsdp", axis_index_groups=[list(t) for t in zip(*team.groups)]
        )
        grad_out = lax.all_gather(
            grad_out, "fsdp", axis=0, tiled=True, axis_index_groups=team.groups
        )
        grad_out = lax.dynamic_slice_in_dim(grad_out, index * own, own)
    grad_up = join_columns(send_up.value, 1, size, *ff_cut)[0]
    result = own_result(here, x2, add_result.value)
    grad_up, result = wait([add_dh1], grad_up, result)
    start(add_dh1)
    if whole_heads:
        wait([add_dh1, send_qkv, send_out])
        grad_out = send_out.value
    else:
        wait([add_dh1, send_qkv])
    grad_tokens, gain_one_part = own_back(here, tokens, dx2, gain_one, add_dh1.value)
    gains = jnp.stack([gain_one_part, gain_two_part]).reshape(2, count, own).transpose(1, 0, 2)
    gains = Transfer(team.one(gains, team.everywhere))
    start(gains)
    wait([gains])
    grad_query, grad_key, grad_value = join_columns(send_qkv.value, 3, size, *head_cut)
    gains = jnp.sum(gains.value, axis=0)
    return (
        result,
        grad_tokens,
        gains[0],
        grad_query,
        grad_key,
        grad_value,
        grad_out,
        gains[1],
        grad_gate,
        grad_up,
        send_down.value,
    )


def solution(mesh):
    flat = P("fsdp")
    wide = P("fsdp", None)
    return jax.shard_map(
        local,
        mesh=mesh,
        in_specs=(wide, flat, flat, flat, wide, wide, wide, wide, flat, wide, wide, wide, wide),
        out_specs=(wide, wide, flat, wide, wide, wide, wide, flat, wide, wide, wide),
        check_vma=False,
    )
```

time: 736 us -> 704 us (0.957)
  Pallas kernels: 85.1 us -> 128 us
  waiting for transfers between devices: 360 us -> 319 us
  other arithmetic: 41.8 us -> 18.8 us
  starting transfers between devices: 93.5 us -> 84.6 us
    ppermute x22 -> x4, waiting for transfers between devices: 240 us -> 30.3 us  [ahead(): return lambda v: lax.ppermute(v, 'fsdp', pairs)]
    all_to_all x2 -> x8, waiting for transfers between devices: 12.5 us -> 85.6 us  [everywhere(): return lax.all_to_all(v, 'fsdp', 0, 0, tiled=True)]
    ppermute x36 -> x38, waiting for transfers between devices: 93.7 us -> 165 us  [flip(): return lambda v: lax.ppermute(v, 'fsdp', pairs)]
    pallas_call x7 -> x26, Pallas kernels: 73.3 us -> 116 us  [the longest x1 27.2 us: hidden_rows(): call(functools.partial(hidden_kernel, subs), [LIKE((rows, hidden), BF)] *...]
    all_gather x4, waiting for transfers between devices: 8.35 us -> 38.6 us  [gather(): lax.all_gather(v, 'fsdp', axis=0, tiled=True, axis_index_groups=self.halves)]
    all_to_all x2 -> x8, starting transfers between devices: 9.62 us -> 36.7 us  [everywhere(): return lax.all_to_all(v, 'fsdp', 0, 0, tiled=True)]
    ppermute x22 -> x4, starting transfers between devices: 35.8 us -> 9.26 us  [ahead(): return lambda v: lax.ppermute(v, 'fsdp', pairs)]
    unnamed x132 -> x146, local copies, waits for them, and re-layouts: 14.1 us -> 40.6 us
  transfers between devices with their start and end apart: 69 -> 54, of which waited for: 36 -> 31; matrix products, arithmetic and copies ran while one was open for 20% -> 15% of each run, Pallas kernels for 8% -> 13%
where the time goes in v4:
time: 704 us; the launch traced here: 696 us
  waiting for transfers between devices  319 us (45%)
  Pallas kernels  128 us (18%)
  starting transfers between devices  84.6 us (12%)
  matrix products  81.6 us (12%)
  local copies, waits for them, and re-layouts  48.3 us (7%)
  other arithmetic  18.8 us (3%)
  between operations  14.8 us (2%)
    ppermute x38, waiting for transfers between devices, flip(): return lambda v: lax.ppermute(v, 'fsdp', pairs)  165 us
    all_to_all x8, waiting for transfers between devices, everywhere(): return lax.all_to_all(v, 'fsdp', 0, 0, tiled=True)  85.6 us
    dot_general x7, matrix products, t_times(): lax.dot_general(left, right, (((0,), (0,)), ((), ())), preferred_element_...  42.5 us
    unnamed x146, local copies, waits for them, and re-layouts  40.6 us
    all_gather x4, waiting for transfers between devices, gather(): lax.all_gather(v, 'fsdp', axis=0, tiled=True, axis_index_groups=self.halves)  38.6 us
    ppermute x38, starting transfers between devices, flip(): return lambda v: lax.ppermute(v, 'fsdp', pairs)  38.4 us
    all_to_all x8, starting transfers between devices, everywhere(): return lax.all_to_all(v, 'fsdp', 0, 0, tiled=True)  36.7 us
    dot_general x6, matrix products, times_t(): lax.dot_general(left, right, (((1,), (1,)), ((), ())), preferred_element_...  31.3 us
  transfers between devices with their start and end apart: 54, of which 31 were waited for; matrix products, arithmetic and copies ran while one was open for 15% of the time, Pallas kernels for 13%

profile of v4, /device:TPU:0, one launch (start us, length us, event | category | flops | bytes accessed | tf_op | source)
XLA Modules:
  0.0 695.6 jit_solution(1102940074502086835)
XLA Ops:
  15.2 7.3 %collective-permute-done = bf16[128,2048]{1,0:T(8,128)(2,1)S(1)} collective-permute-done((bf16[128,2048]{1,0:T(8,128)(2,1)}, bf16[128,2048]{1,0:T(8,128)(2,1)S(1)}, u32[]{:S(2)}, u32[]{:S(2)}) %collective-permute-start) | collective-permute-done | bytes 524320 | tf_op jit(solution)/shard_map/ppermute | solution.py:562
  23.8 6.1 all-to-all-start
  34.9 34.4 %collective-permute-done.1 = bf16[128,2048]{1,0:T(8,128)(2,1)} collective-permute-done((bf16[128,2048]{1,0:T(8,128)(2,1)S(1)}, bf16[128,2048]{1,0:T(8,128)(2,1)}, u32[]{:S(2)}, u32[]{:S(2)}) %collective-permute-start.1) | collective-permute-done | bytes 524320 | tf_op jit(solution)/shard_map/ppermute | solution.py:562
  98.6 12.3 %shard_map.224 = (bf16[2048,2048]{1,0:T(8,128)(2,1)}, f32[2048,384]{1,0:T(8,128)}) custom-call(bf16[2048,2048]{1,0:T(8,128)(2,1)} %all-gather.5.cloned.1.call-done.x, f32[1,2048]{1,0:T(1,128)} %reshape.219.gain, bf16[2048,384]{1,0:T(8,128)(2,1)} %bitcast.5.w), custom_call_target="tpu_custom_call" | custom-call | flops 67108864 | bytes 1048576 | tf_op jit(solution)/shard_map/pallas_call | solution.py:298
  110.9 15.4 %shard_map.225 = (bf16[2,2048,128]{2,1,0:T(8,128)(2,1)}, bf16[2,2048,128]{2,1,0:T(8,128)(2,1)}, bf16[2048,128]{1,0:T(8,128)(2,1)}, bf16[2048,128]{1,0:T(8,128)(2...) custom-call(s32[32]{0:T(128)} %add.174.offsets, f32[2048,384]{1,0:T(8,128)} %get-tuple-element.284.qkv, ...), custom_call_target="tpu_custom_call" | custom-call | flops 67108864 | bytes 1048576 | tf_op jit(solution)/shard_map/pallas_call | solution.py:259
  134.6 5.6 all-to-all-done.2
  151.9 27.8 %collective-permute-done.5.refs_2_ = bf16[256,2048]{1,0:T(8,128)(2,1)S(1)} collective-permute-done((bf16[256,2048]{1,0:T(8,128)(2,1)S(1)}, bf16[256,2048]{1,0:T(8,128)(2,1)S(1)}, u32[]{:S(2)}, u32[]{:S(2)}) %collective-permute-start.5) | collective-permute-done | bytes 1048608 | tf_op jit(solution)/shard_map/ppermute | solution.py:562
  182.9 14.7 %collective-permute-done.9 = bf16[256,2048]{1,0:T(8,128)(2,1)S(1)} collective-permute-done((bf16[256,2048]{1,0:T(8,128)(2,1)S(1)}, bf16[256,2048]{1,0:T(8,128)(2,1)S(1)}, u32[]{:S(2)}, u32[]{:S(2)}) %collective-permute-start.9) | collective-permute-done | bytes 1048608 | tf_op jit(solution)/shard_map/ppermute | solution.py:567
  207.6 5.6 collective-permute-done.11.refs_3_
  213.2 5.6 collective-permute-done.12.refs_6_
  232.8 10.9 %fusion.25.dm = f32[2048,512]{1,0:T(8,128)} fusion(bf16[2048,2048]{1,0:T(8,128)(2,1)} %all-gather.7.cloned.1.call-done, bf16[512,2048]{1,0:T(8,128)(2,1)} %bitcast.11.right), kind=kOutput, calls=%fused_computation.77 | convolution fusion | flops 4294967296 | bytes 14680064 | tf_op jit(solution)/shard_map/dot_general | solution.py:41
  243.7 34.4 %all-to-all-done.3 = bf16[32,64,512]{2,1,0:T(8,128)(2,1)} async-done(((bf16[32,64,512]{2,1,0:T(8,128)(2,1)}), bf16[32,64,512]{2,1,0:T(8,128)(2,1)}, u32[]{:S(2)}, u32[]{:S(2)}) %all-to-all-start.3) | async-done | bytes 2097184 | tf_op jit(solution)/shard_map/all_to_all | solution.py:573
  278.2 19.3 %all-gather.9.cloned.1.call-done.h = bf16[2048,2048]{1,0:T(8,128)(2,1)} async-done(((bf16[256,2048]{1,0:T(8,128)(2,1)}), bf16[2048,2048]{1,0:T(8,128)(2,1)}) %all-gather.9.cloned.1.call-update) | async-done | bytes 8388624 | tf_op jit(solution)/shard_map/all_gather | solution.py:576
  297.4 27.2 %shard_map.230 = (bf16[2048,512]{1,0:T(8,128)(2,1)}, bf16[2048,512]{1,0:T(8,128)(2,1)}, bf16[2048,512]{1,0:T(8,128)(2,1)}, bf16[512,2048]{1,0:T(8,128)(2,1)}, bf...) custom-call(s32[17]{0:T(128)} %pad_add_fusion.1.spots, ...), custom_call_target="tpu_custom_call" | custom-call | flops 67108864 | bytes 1048576 | tf_op jit(solution)/shard_map/pallas_call | solution.py:340
  325.2 6.2 convolution_convert_fusion.11
  343.6 5.7 convolution_convert_fusion.9
  349.3 15.6 %collective-permute-done.16.refs_2_ = bf16[256,2048]{1,0:T(8,128)(2,1)S(1)} collective-permute-done((bf16[256,2048]{1,0:T(8,128)(2,1)S(1)}, bf16[256,2048]{1,0:T(8,128)(2,1)S(1)}, u32[]{:S(2)}, u32[]{:S(2)}) %collective-permute-start.16) | collective-permute-done | bytes 1048608 | tf_op jit(solution)/shard_map/ppermute | solution.py:562
  368.8 8.4 %shard_map.232 = (bf16[512,2048]{1,0:T(8,128)(2,1)S(1)}, bf16[512,2048]{1,0:T(8,128)(2,1)S(1)}, bf16[512,2048]{1,0:T(8,128)(2,1)S(1)}, bf16[512,2048]{1,0:T(8,128)(2,1)S(1)}) custom-call(s32[17]{0:T(128)S(1)} %copy-done.44, bf16[2048,512]{1,0:T(8,128)(2,1)S(1)} %copy-done.2, bf16[512,2048]{1,0:T(8,128)(2,1)} %bitcast.11.right), custom_call_target="tpu_custom_call" | custom-call | flops 67108864 | bytes 1048576 | tf_op jit(solution)/shard_map/pallas_call | solution.py:360
  377.2 12.8 %collective-permute-done.20 = bf16[256,2048]{1,0:T(8,128)(2,1)S(1)} collective-permute-done((bf16[256,2048]{1,0:T(8,128)(2,1)S(1)}, bf16[256,2048]{1,0:T(8,128)(2,1)S(1)}, u32[]{:S(2)}, u32[]{:S(2)}) %collective-permute-start.20) | collective-permute-done | bytes 1048608 | tf_op jit(solution)/shard_map/ppermute | solution.py:567
  404.5 6.0 convolution_convert_fusion.8
  416.4 11.4 %collective-permute-done.27.refs_2_ = bf16[256,2048]{1,0:T(8,128)(2,1)S(1)} collective-permute-done((bf16[256,2048]{1,0:T(8,128)(2,1)S(1)}, bf16[256,2048]{1,0:T(8,128)(2,1)S(1)}, u32[]{:S(2)}, u32[]{:S(2)}) %collective-permute-start.27) | collective-permute-done | bytes 1048608 | tf_op jit(solution)/shard_map/ppermute | solution.py:562
  447.5 39.3 %all-to-all-done.4.v = bf16[32,64,512]{2,1,0:T(8,128)(2,1)} async-done(((bf16[32,64,512]{2,1,0:T(8,128)(2,1)}), bf16[32,64,512]{2,1,0:T(8,128)(2,1)}, u32[]{:S(2)}, u32[]{:S(2)}) %all-to-all-start.4) | async-done | bytes 2097184 | tf_op jit(solution)/shard_map/all_to_all | solution.py:573
  486.8 19.3 %all-gather.11.cloned.1.call-done = bf16[2048,2048]{1,0:T(8,128)(2,1)} async-done(((bf16[256,2048]{1,0:T(8,128)(2,1)}), bf16[2048,2048]{1,0:T(8,128)(2,1)}) %all-gather.11.cloned.1.call-update) | async-done | bytes 8388624 | tf_op jit(solution)/shard_map/all_gather | solution.py:576
  513.5 6.6 convolution_convert_fusion.12.dout
  520.0 22.4 %shard_map.237 = (bf16[2048,384]{1,0:T(8,128)(2,1)}, bf16[2048,384]{1,0:T(8,128)(2,1)}) custom-call(s32[32]{0:T(128)} %add.174.offsets, bf16[2,2048,128]{2,1,0:T(8,128)(2,1)} %get-tuple-element.423.qe, bf16[2,2048,128]{2,1,0:T(8,128)(2,1)} %get-tuple-element.424.ke, bf16[2048,128]{1,0:T(8,128)(2,1)} %get-tuple-element.425.vs, ...), custom_call_target="tpu_custom_call" | custom-call | flops 67108864 | bytes 1048576 | tf_op jit(solution)/shard_map/pallas_call | solution.py:275
  560.2 9.1 %convolution_convert_fusion.10 = bf16[2048,384]{1,0:T(8,128)(2,1)} fusion(bf16[2048,2048]{1,0:T(8,128)(2,1)} %get-tuple-element.440, bf16[2048,384]{1,0:T(8,128)(2,1)S(1)} %copy-done.65), kind=kOutput, calls=%fused_computation.10 | convolution fusion | flops 3222011904 | bytes 11534336 | tf_op jit(solution)/shard_map/dot_general | solution.py:45
  594.4 6.0 convolution_convert_fusion.13
  603.7 17.7 %collective-permute-done.35.refs_2_ = bf16[64,2048]{1,0:T(8,128)(2,1)S(1)} collective-permute-done((bf16[64,2048]{1,0:T(8,128)(2,1)}, bf16[64,2048]{1,0:T(8,128)(2,1)S(1)}, u32[]{:S(2)}, u32[]{:S(2)}) %collective-permute-start.35) | collective-permute-done | bytes 262176 | tf_op jit(solution)/shard_map/ppermute | solution.py:562
  621.4 6.9 collective-permute-done.36.refs_3_
  636.1 5.9 fusion.3
  659.7 5.6 collective-permute-done.39.refs_2_
  674.5 5.3 all-to-all-start.7
  (319 shorter events, 244.1 us)
Async XLA Ops:
  7.2 91.4 %all-gather.5.cloned.1.call-start = ((), (), s32[]{:S(2)}) async-start(), calls=%async_computation.8 | async-start | bytes 9437184 | tf_op jit(solution)/shard_map/all_gather | solution.py:576
  23.8 45.5 %all-to-all-start = ((bf16[32,64,384]{2,1,0:T(8,128)(2,1)}), bf16[32,64,384]{2,1,0:T(8,128)(2,1)}, u32[]{:S(2)}, u32[]{:S(2)}) async-start(bf16[32,64,384]{2,1,0:T(8,128)(2,1)} %shard_map.221), calls=%async_computation | async-start | bytes 3145728 | tf_op jit(solution)/shard_map/all_to_all | solution.py:573
  29.9 202.9 %all-gather.7.cloned.1.call-start = ((), (), s32[]{:S(2)}) async-start(), calls=%async_computation.9 | async-start | bytes 9437184 | tf_op jit(solution)/shard_map/all_gather | solution.py:576
  30.0 39.3 %collective-permute-start.1 = (bf16[128,2048]{1,0:T(8,128)(2,1)S(1)}, bf16[128,2048]{1,0:T(8,128)(2,1)}, u32[]{:S(2)}, u32[]{:S(2)}) collective-permute-start(bf16[128,2048]{1,0:T(8,128)(2,1)S(1)} %copy-done.60), channel_id=1, source_target_pairs={{0,8},{1,9},{2,10},{3,11},{4,12},{5,13},{6,14},{7,15},{8,0},{9,1},... | collective-permute-start | bytes 1572872 | tf_op jit(solution)/shard_map/ppermute | solution.py:562
  79.1 19.4 %collective-permute-start.2 = (bf16[64,2048]{1,0:T(8,128)(2,1)S(1)}, bf16[64,2048]{1,0:T(8,128)(2,1)S(1)}, u32[]{:S(2)}, u32[]{:S(2)}) collective-permute-start(bf16[64,2048]{1,0:T(8,128)(2,1)S(1)} %copy-done.62), channel_id=1, source_target_pairs={{0,16},{1,17},{2,18},{3,19},{4,20},{5,21},{6,22},{7,23},{8,24},{9,... | collective-permute-start | bytes 786440 | tf_op jit(solution)/shard_map/ppermute | solution.py:567
  85.9 54.3 %all-to-all-start.2 = ((bf16[32,64,512]{2,1,0:T(8,128)(2,1)}), bf16[32,64,512]{2,1,0:T(8,128)(2,1)}, u32[]{:S(2)}, u32[]{:S(2)}) async-start(bf16[32,64,512]{2,1,0:T(8,128)(2,1)} %shard_map.222), calls=%async_computation.2 | async-start | bytes 4194304 | tf_op jit(solution)/shard_map/all_to_all | solution.py:573
  89.4 208.0 %all-gather.9.cloned.1.call-start = ((), (), s32[]{:S(2)}) async-start(), calls=%async_computation.10 | async-start | bytes 9437184 | tf_op jit(solution)/shard_map/all_gather | solution.py:576
  146.1 33.6 %collective-permute-start.5 = (bf16[256,2048]{1,0:T(8,128)(2,1)S(1)}, bf16[256,2048]{1,0:T(8,128)(2,1)S(1)}, u32[]{:S(2)}, u32[]{:S(2)}) collective-permute-start(bf16[256,2048]{1,0:T(8,128)(2,1)S(1)} %get-tuple-element.304), channel_id=1, source_target_pairs={{0,4},{1,5},{2,6},{3,7},{4,0},{5,1},{6,2},{7,3},{8,12},{9,13},{10,... | collective-permute-start | bytes 3145736 | tf_op jit(solution)/shard_map/ppermute | solution.py:562
  148.0 31.8 %collective-permute-start.6 = (bf16[256,2048]{1,0:T(8,128)(2,1)S(1)}, bf16[256,2048]{1,0:T(8,128)(2,1)S(1)}, u32[]{:S(2)}, u32[]{:S(2)}) collective-permute-start(bf16[256,2048]{1,0:T(8,128)(2,1)S(1)} %get-tuple-element.305), channel_id=1, source_target_pairs={{0,2},{1,3},{2,0},{3,1},{4,6},{5,7},{6,4},{7,5},{8,10},{9,11},{10,... | collective-permute-start | bytes 3145736 | tf_op jit(solution)/shard_map/ppermute | solution.py:562
  149.4 48.1 %collective-permute-start.9 = (bf16[256,2048]{1,0:T(8,128)(2,1)S(1)}, bf16[256,2048]{1,0:T(8,128)(2,1)S(1)}, u32[]{:S(2)}, u32[]{:S(2)}) collective-permute-start(bf16[256,2048]{1,0:T(8,128)(2,1)S(1)} %copy-done.56), channel_id=1, source_target_pairs={{0,16},{1,17},{2,18},{3,19},{4,20},{5,21},{6,22},{7,23},{8,24},{9,... | collective-permute-start | bytes 3145736 | tf_op jit(solution)/shard_map/ppermute | solution.py:567
  200.7 21.5 %collective-permute-start.13 = (bf16[64,2048]{1,0:T(8,128)(2,1)S(1)}, bf16[64,2048]{1,0:T(8,128)(2,1)S(1)}, u32[]{:S(2)}, u32[]{:S(2)}) collective-permute-start(bf16[64,2048]{1,0:T(8,128)(2,1)S(1)} %get-tuple-element.328), channel_id=1, source_target_pairs={{0,8},{1,9},{2,10},{3,11},{4,12},{5,13},{6,14},{7,15},{8,0},{9,1},... | collective-permute-start | bytes 786440 | tf_op jit(solution)/shard_map/ppermute | solution.py:562
  224.1 54.0 %all-to-all-start.3 = ((bf16[32,64,512]{2,1,0:T(8,128)(2,1)}), bf16[32,64,512]{2,1,0:T(8,128)(2,1)}, u32[]{:S(2)}, u32[]{:S(2)}) async-start(bf16[32,64,512]{2,1,0:T(8,128)(2,1)} %copy-done.3), calls=%async_computation.3 | async-start | bytes 4194304 | tf_op jit(solution)/shard_map/all_to_all | solution.py:573
  229.1 276.9 %all-gather.11.cloned.1.call-start = ((), (), s32[]{:S(2)}) async-start(), calls=%async_computation.11 | async-start | bytes 9437184 | tf_op jit(solution)/shard_map/all_gather | solution.py:576
  339.6 25.4 %collective-permute-start.16 = (bf16[256,2048]{1,0:T(8,128)(2,1)S(1)}, bf16[256,2048]{1,0:T(8,128)(2,1)S(1)}, u32[]{:S(2)}, u32[]{:S(2)}) collective-permute-start(bf16[256,2048]{1,0:T(8,128)(2,1)S(1)} %get-tuple-element.364), channel_id=1, source_target_pairs={{0,4},{1,5},{2,6},{3,7},{4,0},{5,1},{6,2},{7,3},{8,12},{9,13},{10,... | collective-permute-start | bytes 3145736 | tf_op jit(solution)/shard_map/ppermute | solution.py:562
  340.2 25.0 %collective-permute-start.17 = (bf16[256,2048]{1,0:T(8,128)(2,1)S(1)}, bf16[256,2048]{1,0:T(8,128)(2,1)S(1)}, u32[]{:S(2)}, u32[]{:S(2)}) collective-permute-start(bf16[256,2048]{1,0:T(8,128)(2,1)S(1)} %get-tuple-element.365), channel_id=1, source_target_pairs={{0,2},{1,3},{2,0},{3,1},{4,6},{5,7},{6,4},{7,5},{8,10},{9,11},{10,... | collective-permute-start | bytes 3145736 | tf_op jit(solution)/shard_map/ppermute | solution.py:562
  341.8 48.1 %collective-permute-start.20 = (bf16[256,2048]{1,0:T(8,128)(2,1)S(1)}, bf16[256,2048]{1,0:T(8,128)(2,1)S(1)}, u32[]{:S(2)}, u32[]{:S(2)}) collective-permute-start(bf16[256,2048]{1,0:T(8,128)(2,1)S(1)} %convolution_convert_fusion.11), channel_id=1, source_target_pairs={{0,16},{1,17},{2,18},{3,19},{4,20},{5,21},{6,22},{7,23},{8,24},{9,... | collective-permute-start | bytes 3145736 | tf_op jit(solution)/shard_map/ppermute | solution.py:567
  366.3 23.7 %collective-permute-start.18 = (bf16[128,2048]{1,0:T(8,128)(2,1)S(1)}, bf16[128,2048]{1,0:T(8,128)(2,1)S(1)}, u32[]{:S(2)}, u32[]{:S(2)}) collective-permute-start(bf16[128,2048]{1,0:T(8,128)(2,1)S(1)} %get-tuple-element.379), channel_id=1, source_target_pairs={{0,2},{1,3},{2,0},{3,1},{4,6},{5,7},{6,4},{7,5},{8,10},{9,11},{10,... | collective-permute-start | bytes 1572872 | tf_op jit(solution)/shard_map/ppermute | solution.py:562
  368.0 22.0 %collective-permute-start.19 = (bf16[128,2048]{1,0:T(8,128)(2,1)S(1)}, bf16[128,2048]{1,0:T(8,128)(2,1)S(1)}, u32[]{:S(2)}, u32[]{:S(2)}) collective-permute-start(bf16[128,2048]{1,0:T(8,128)(2,1)S(1)} %get-tuple-element.380), channel_id=1, source_target_pairs={{0,4},{1,5},{2,6},{3,7},{4,0},{5,1},{6,2},{7,3},{8,12},{9,13},{10,... | collective-permute-start | bytes 1572872 | tf_op jit(solution)/shard_map/ppermute | solution.py:562
  394.9 21.5 %collective-permute-start.26 = (bf16[64,2048]{1,0:T(8,128)(2,1)S(1)}, bf16[64,2048]{1,0:T(8,128)(2,1)S(1)}, u32[]{:S(2)}, u32[]{:S(2)}) collective-permute-start(bf16[64,2048]{1,0:T(8,128)(2,1)S(1)} %get-tuple-element.401), channel_id=1, source_target_pairs={{0,8},{1,9},{2,10},{3,11},{4,12},{5,13},{6,14},{7,15},{8,0},{9,1},... | collective-permute-start | bytes 786440 | tf_op jit(solution)/shard_map/ppermute | solution.py:562
  402.6 25.2 %collective-permute-start.27 = (bf16[256,2048]{1,0:T(8,128)(2,1)S(1)}, bf16[256,2048]{1,0:T(8,128)(2,1)S(1)}, u32[]{:S(2)}, u32[]{:S(2)}) collective-permute-start(bf16[256,2048]{1,0:T(8,128)(2,1)S(1)} %get-tuple-element.408), channel_id=1, source_target_pairs={{0,4},{1,5},{2,6},{3,7},{4,0},{5,1},{6,2},{7,3},{8,12},{9,13},{10,... | collective-permute-start | bytes 3145736 | tf_op jit(solution)/shard_map/ppermute | solution.py:562
  403.4 25.4 %collective-permute-start.28 = (bf16[256,2048]{1,0:T(8,128)(2,1)S(1)}, bf16[256,2048]{1,0:T(8,128)(2,1)S(1)}, u32[]{:S(2)}, u32[]{:S(2)}) collective-permute-start(bf16[256,2048]{1,0:T(8,128)(2,1)S(1)} %get-tuple-element.409), channel_id=1, source_target_pairs={{0,2},{1,3},{2,0},{3,1},{4,6},{5,7},{6,4},{7,5},{8,10},{9,11},{10,... | collective-permute-start | bytes 3145736 | tf_op jit(solution)/shard_map/ppermute | solution.py:562
  433.8 52.9 %all-to-all-start.4 = ((bf16[32,64,512]{2,1,0:T(8,128)(2,1)}), bf16[32,64,512]{2,1,0:T(8,128)(2,1)}, u32[]{:S(2)}, u32[]{:S(2)}) async-start(bf16[32,64,512]{2,1,0:T(8,128)(2,1)} %bitcast.66), calls=%async_computation.4 | async-start | bytes 4194304 | tf_op jit(solution)/shard_map/all_to_all | solution.py:573
  506.0 65.9 %all-to-all-start.5 = ((bf16[32,64,512]{2,1,0:T(8,128)(2,1)}), bf16[32,64,512]{2,1,0:T(8,128)(2,1)}, u32[]{:S(2)}, u32[]{:S(2)}) async-start(bf16[32,64,512]{2,1,0:T(8,128)(2,1)} %bitcast.67), calls=%async_computation.5 | async-start | bytes 4194304 | tf_op jit(solution)/shard_map/all_to_all | solution.py:573
  510.2 37.9 %collective-permute-start.29 = (bf16[128,2048]{1,0:T(8,128)(2,1)}, bf16[128,2048]{1,0:T(8,128)(2,1)S(1)}, u32[]{:S(2)}, u32[]{:S(2)}) collective-permute-start(bf16[128,2048]{1,0:T(8,128)(2,1)} %copy-done.47), channel_id=1, source_target_pairs={{0,2},{1,3},{2,0},{3,1},{4,6},{5,7},{6,4},{7,5},{8,10},{9,11},{10,... | collective-permute-start | bytes 1572872 | tf_op jit(solution)/shard_map/ppermute | solution.py:562
  512.0 36.1 %collective-permute-start.30 = (bf16[128,2048]{1,0:T(8,128)(2,1)S(1)}, bf16[128,2048]{1,0:T(8,128)(2,1)S(1)}, u32[]{:S(2)}, u32[]{:S(2)}) collective-permute-start(bf16[128,2048]{1,0:T(8,128)(2,1)S(1)} %get-tuple-element.438), channel_id=1, source_target_pairs={{0,4},{1,5},{2,6},{3,7},{4,0},{5,1},{6,2},{7,3},{8,12},{9,13},{10,... | collective-permute-start | bytes 1572872 | tf_op jit(solution)/shard_map/ppermute | solution.py:562
  548.1 21.2 %collective-permute-start.31 = (bf16[512,2048]{1,0:T(8,128)(2,1)S(1)}, bf16[512,2048]{1,0:T(8,128)(2,1)S(1)}, u32[]{:S(2)}, u32[]{:S(2)}) collective-permute-start(bf16[512,2048]{1,0:T(8,128)(2,1)S(1)} %convolution_convert_fusion.7), channel_id=1, source_target_pairs={{0,1},{1,0},{2,3},{3,2},{4,5},{5,4},{6,7},{7,6},{8,9},{9,8},{10,11... | collective-permute-start | bytes 6291464 | tf_op jit(solution)/shard_map/ppermute | solution.py:562
  548.2 22.4 %collective-permute-start.32 = (bf16[512,2048]{1,0:T(8,128)(2,1)S(1)}, bf16[512,2048]{1,0:T(8,128)(2,1)S(1)}, u32[]{:S(2)}, u32[]{:S(2)}) collective-permute-start(bf16[512,2048]{1,0:T(8,128)(2,1)S(1)} %convolution_convert_fusion.6), channel_id=1, source_target_pairs={{0,1},{1,0},{2,3},{3,2},{4,5},{5,4},{6,7},{7,6},{8,9},{9,8},{10,11... | collective-permute-start | bytes 6291464 | tf_op jit(solution)/shard_map/ppermute | solution.py:562
  584.9 84.3 %all-to-all-start.6 = ((bf16[32,64,384]{2,1,0:T(8,128)(2,1)}), bf16[32,64,384]{2,1,0:T(8,128)(2,1)}, u32[]{:S(2)}, u32[]{:S(2)}) async-start(bf16[32,64,384]{2,1,0:T(8,128)(2,1)} %bitcast.68), calls=%async_computation.6 | async-start | bytes 3145728 | tf_op jit(solution)/shard_map/all_to_all | solution.py:573
  589.0 42.2 %collective-permute-start.33 = (bf16[256,2048]{1,0:T(8,128)(2,1)}, bf16[256,2048]{1,0:T(8,128)(2,1)}, u32[]{:S(2)}, u32[]{:S(2)}) collective-permute-start(bf16[256,2048]{1,0:T(8,128)(2,1)} %copy-done.46), channel_id=1, source_target_pairs={{0,4},{1,5},{2,6},{3,7},{4,0},{5,1},{6,2},{7,3},{8,12},{9,13},{10,... | collective-permute-start | bytes 3145736 | tf_op jit(solution)/shard_map/ppermute | solution.py:562
  591.0 40.3 %collective-permute-start.34 = (bf16[256,2048]{1,0:T(8,128)(2,1)}, bf16[256,2048]{1,0:T(8,128)(2,1)}, u32[]{:S(2)}, u32[]{:S(2)}) collective-permute-start(bf16[256,2048]{1,0:T(8,128)(2,1)} %copy-done.45), channel_id=1, source_target_pairs={{0,2},{1,3},{2,0},{3,1},{4,6},{5,7},{6,4},{7,5},{8,10},{9,11},{10,... | collective-permute-start | bytes 3145736 | tf_op jit(solution)/shard_map/ppermute | solution.py:562
  592.4 29.0 %collective-permute-start.35 = (bf16[64,2048]{1,0:T(8,128)(2,1)}, bf16[64,2048]{1,0:T(8,128)(2,1)S(1)}, u32[]{:S(2)}, u32[]{:S(2)}) collective-permute-start(bf16[64,2048]{1,0:T(8,128)(2,1)} %copy-done.48), channel_id=1, source_target_pairs={{0,8},{1,9},{2,10},{3,11},{4,12},{5,13},{6,14},{7,15},{8,0},{9,1},... | collective-permute-start | bytes 786440 | tf_op jit(solution)/shard_map/ppermute | solution.py:562
  593.9 34.4 %collective-permute-start.36 = (bf16[64,2048]{1,0:T(8,128)(2,1)S(1)}, bf16[64,2048]{1,0:T(8,128)(2,1)S(1)}, u32[]{:S(2)}, u32[]{:S(2)}) collective-permute-start(bf16[64,2048]{1,0:T(8,128)(2,1)S(1)} %get-tuple-element.463), channel_id=1, source_target_pairs={{0,8},{1,9},{2,10},{3,11},{4,12},{5,13},{6,14},{7,15},{8,0},{9,1},... | collective-permute-start | bytes 786440 | tf_op jit(solution)/shard_map/ppermute | solution.py:562
  (94 other events, 789.1 us)
Sparse Core Ops, SparseCore 0:
  23.9 67.9 all-gather.4
  93.8 73.4 all-gather.6
  224.3 73.1 all-gather.8
  433.9 72.0 all-gather.10

commit v5 on v4

--- a/solution.py
+++ b/solution.py
@@ -21,6 +21,7 @@
 LANES = 2 * HEAD_DIM
 HALF = HEAD_DIM // 2
 BLOCK = 512
+STEP = 1024
 MIB = 2**20
 
 
@@ -294,7 +295,7 @@
 
 def norm_project(x, gain, w):
     rows, width = x.shape
-    step, columns = 256, w.shape[1]
+    step, columns = STEP, w.shape[1]
     return call(
         project_kernel,
         [LIKE((rows, width), BF), LIKE((rows, columns), F32)],
@@ -307,17 +308,21 @@
 def hand_out(subs, spots, product, sent, kept):
     rows = sum(subs)
     chips = SEQ // (2 * rows)
-    core, chip = pl.program_id(0) % 2, pl.program_id(0) // 2
-    for side, outs in ((spots[0], kept), (1 - spots[0], sent)):
-
-        @pl.when(core == side)
-        def _():
-            for half in range(2):
-                start = half * rows
-                for r, sub in enumerate(subs):
-                    there = spots[1 + r * chips + half * (chips // 2) + chip]
-                    outs[r][pl.ds(pl.multiple_of(there, 16), sub), :] = product[start : start + sub]
-                    start += sub
+    pairs = product.shape[0] // (2 * rows)
+    for j in range(pairs):
+        pair = pl.program_id(0) * pairs + j
+        core, chip = pair % 2, pair // 2
+        for side, outs in ((spots[0], kept), (1 - spots[0], sent)):
+
+            @pl.when(core == side)
+            def _():
+                for half in range(2):
+                    start = (2 * j + half) * rows
+                    for r, sub in enumerate(subs):
+                        there = spots[1 + r * chips + half * (chips // 2) + chip]
+                        there = pl.ds(pl.multiple_of(there, 16), sub)
+                        outs[r][there, :] = product[start : start + sub]
+                        start += sub
 
 
 def hidden_kernel(subs, spots, h, w_gate, w_up, dm, mixed, dgate, dup, *outs):
@@ -335,8 +340,8 @@
 def hidden_rows(subs, spots, h, w_gate, w_up, dm):
     rows, width = h.shape
     hidden = dm.shape[1]
-    step = 2 * sum(subs)
-    rails = [LIKE((rows // step * sub, width), BF) for sub in subs]
+    step = STEP
+    rails = [LIKE((rows // (2 * sum(subs)) * sub, width), BF) for sub in subs]
     made = call(
         functools.partial(hidden_kernel, subs),
         [LIKE((rows, hidden), BF)] * 3 + rails + rails,
@@ -355,8 +360,8 @@
 def products(subs, spots, left, right):
     rows, depth = left.shape
     width = right.shape[1]
-    step = 2 * sum(subs)
-    rails = [LIKE((rows // step * sub, width), BF) for sub in subs]
+    step = STEP
+    rails = [LIKE((rows // (2 * sum(subs)) * sub, width), BF) for sub in subs]
     made = call(
         functools.partial(product_kernel, subs),
         rails + rails,
@@ -430,27 +435,23 @@
     scale = lax.rsqrt(jnp.mean(v * v, axis=-1, keepdims=True) + EPS)
     hat = v * scale
     weighted = gain * grad
-    back = scale * (weighted - hat * jnp.mean(hat * weighted, axis=-1, keepdims=True))
-    return back, jnp.sum(grad * hat, axis=0, keepdims=True)
+    return scale * (weighted - hat * jnp.mean(hat * weighted, axis=-1, keepdims=True))
 
 
 def pair_back_kernel(rails, half, v, base, gain, *refs):
-    sums, (out, rounded, part) = refs[:-3], refs[-3:]
-    part[...] = jnp.zeros_like(part)
+    sums, (out, rounded) = refs[:-2], refs[-2:]
     for at, total in pair_rows(rails, half[0], sums):
-        back, share = norm_back(v[at, :], gain[...], total)
-        made = base[at, :].astype(F32) + back
+        made = base[at, :].astype(F32) + norm_back(v[at, :], gain[...], total)
         out[at, :] = made
         rounded[at, :] = made.astype(BF)
-        part[...] += 0.5 * share
 
 
 def pair_back(half, v, base, gain, sums):
     return call(
         functools.partial(pair_back_kernel, len(sums) // 4),
-        [LIKE(v.shape, F32), LIKE(v.shape, BF), LIKE((1, v.shape[1]), F32)],
+        [LIKE(v.shape, F32), LIKE(v.shape, BF)],
         [IN_SMEM] + [IN_VMEM] * (3 + len(sums)),
-        [IN_VMEM] * 3,
+        [IN_VMEM] * 2,
         vmem=32,
     )(half, v, base, gain, *sums)
 
@@ -464,20 +465,17 @@
 
 
 def own_back_kernel(rails, half, v, base, gain, *refs):
-    sums, (out, part) = refs[:-2], refs[-2:]
-    part[...] = jnp.zeros_like(part)
+    sums, out = refs[:-1], refs[-1]
     for mine, at, total in own_rows(rails, half[0], sums, v.shape[0]):
-        back, share = norm_back(v[mine, :].astype(F32), gain[...], total)
-        out[mine, :] = base[at, :] + back
-        part[...] += share
+        out[mine, :] = base[at, :] + norm_back(v[mine, :].astype(F32), gain[...], total)
 
 
 def own_back(half, v, base, gain, sums):
     return call(
         functools.partial(own_back_kernel, len(sums) // 2),
-        [LIKE(v.shape, F32), LIKE((1, v.shape[1]), F32)],
+        LIKE(v.shape, F32),
         [IN_SMEM] + [IN_VMEM] * (3 + len(sums)),
-        [IN_VMEM] * 2,
+        IN_VMEM,
         vmem=24,
     )(half, v, base, gain, *sums)
 
@@ -521,27 +519,34 @@
     )(*weights)
 
 
-def join_kernel(size, first, each, blocks, v, *outs):
+def join_kernel(size, first, each, blocks, v, *refs):
+    parts = (len(refs) - 1) // 2
+    weights, outs, share = refs[:parts], refs[parts:-1], refs[-1]
+    along = jnp.zeros((v.shape[1], each), F32)
     for p in range(size):
         at = 0
-        for out in outs:
+        for w, out in zip(weights, outs):
             for j in range(blocks):
                 total = v[p, :, at : at + each].astype(F32)
                 for d in range(p + size, v.shape[0], size):
                     total += v[d, :, at : at + each].astype(F32)
-                out[:, first(j, p) : first(j, p) + each] = total
+                here = slice(first(j, p), first(j, p) + each)
+                out[:, here] = total
+                along += total * w[:, here].astype(F32)
                 at += each
-
-
-def join_columns(v, parts, size, first, each, blocks):
+    share[...] = jnp.sum(along, axis=1, keepdims=True)
+
+
+def join_columns(v, weights, size, first, each, blocks):
     rows = v.shape[1]
-    return call(
+    made = call(
         functools.partial(join_kernel, size, first, each, blocks),
-        [LIKE((rows, size * each * blocks), F32)] * parts,
-        [IN_VMEM],
-        [IN_VMEM] * parts,
+        [LIKE((rows, size * each * blocks), F32)] * len(weights) + [LIKE((rows, 1), F32)],
+        [IN_VMEM] * (1 + len(weights)),
+        [IN_VMEM] * (len(weights) + 1),
         vmem=32,
-    )(v)
+    )(v, *weights)
+    return made
 
 
 class Team:
@@ -687,6 +692,10 @@
         self.token = token
 
     def start(self, *transfers):
+        for t in transfers:
+            t.got = [move(barrier(self.token, v)[1]) for v, move in t.moves]
+
+    def start_together(self, *transfers):
         given = [v for t in transfers for v, _ in t.moves]
         given = list(barrier(self.token, *given)[1:])
         for t in transfers:
@@ -755,7 +764,7 @@
     x_pair = pair_x.value
     get_qkv = Transfer(team.columns(cut_qkv))
     get_x = Transfer(team.one(x_pair, team.gather))
-    start(get_x, get_qkv, pair_dy)
+    clock.start_together(get_x, get_qkv, pair_dy)
     cut_gate = cut_columns([w_gate], count, size, *ff_cut)
     cut_up = cut_columns([w_up], count, size, *ff_cut)
     small = jnp.concatenate([v.astype(F32) for v in (gain_attn, gain_mlp, segments, positions)])
@@ -854,7 +863,7 @@
     start(add_result)
     grad_up = t_times(h2, dup).astype(BF)
     [grad_up] = wait([add_dh2, add_result], grad_up)
-    dx2, da, gain_two_part = pair_back(here, x2, dy_pair, gain_two, add_dh2.value)
+    dx2, da = pair_back(here, x2, dy_pair, gain_two, add_dh2.value)
     get_da = Transfer(team.one(da, team.gather))
     send_gate = Transfer(team.owners(grad_gate))
     send_up = Transfer(team.owners(grad_up))
@@ -872,7 +881,7 @@
     [grad_qkv] = wait([add_dh1, send_up], grad_qkv)
     send_qkv = Transfer(team.owners(grad_qkv))
     start(add_dh1, add_result, send_qkv)
-    grad_gate = join_columns(send_gate.value, 1, size, *ff_cut)[0]
+    grad_gate, share_gate = join_columns(send_gate.value, [w_gate], size, *ff_cut)
     [grad_gate] = wait([add_dh1, add_result], grad_gate)
     start(add_dh1)
     if whole_heads:
@@ -886,7 +895,8 @@
             grad_out, "fsdp", axis=0, tiled=True, axis_index_groups=team.groups
         )
         grad_out = lax.dynamic_slice_in_dim(grad_out, index * own, own)
-    grad_up = join_columns(send_up.value, 1, size, *ff_cut)[0]
+    grad_up, share_up = join_columns(send_up.value, [w_up], size, *ff_cut)
+    grad_gain_mlp = (share_gate + share_up)[:, 0] / gain_mlp.astype(F32)
     result = own_result(here, x2, add_result.value)
     grad_up, result = wait([add_dh1], grad_up, result)
     start(add_dh1)
@@ -895,22 +905,20 @@
         grad_out = send_out.value
     else:
         wait([add_dh1, send_qkv])
-    grad_tokens, gain_one_part = own_back(here, tokens, dx2, gain_one, add_dh1.value)
-    gains = jnp.stack([gain_one_part, gain_two_part]).reshape(2, count, own).transpose(1, 0, 2)
-    gains = Transfer(team.one(gains, team.everywhere))
-    start(gains)
-    wait([gains])
-    grad_query, grad_key, grad_value = join_columns(send_qkv.value, 3, size, *head_cut)
-    gains = jnp.sum(gains.value, axis=0)
+    grad_tokens = own_back(here, tokens, dx2, gain_one, add_dh1.value)
+    grad_query, grad_key, grad_value, share = join_columns(
+        send_qkv.value, [w_query, w_key, w_value], size, *head_cut
+    )
+    grad_gain_attn = share[:, 0] / gain_attn.astype(F32)
     return (
         result,
         grad_tokens,
-        gains[0],
+        grad_gain_attn,
         grad_query,
         grad_key,
         grad_value,
         grad_out,
-        gains[1],
+        grad_gain_mlp,
         grad_gate,
         grad_up,
         send_down.value,

time: 704 us -> 671 us (0.953)
  waiting for transfers between devices: 319 us -> 259 us
  blocking collectives: 0 us -> 52.5 us
  local copies, waits for them, and re-layouts: 48.3 us -> 36.4 us
  starting transfers between devices: 84.6 us -> 75.9 us
    all_to_all x0 -> x1, blocking collectives: none -> 52.5 us  [everywhere(): return lax.all_to_all(v, 'fsdp', 0, 0, tiled=True)]
    all_to_all x8 -> x6, waiting for transfers between devices: 85.6 us -> 44.5 us  [everywhere(): return lax.all_to_all(v, 'fsdp', 0, 0, tiled=True)]
    ppermute x38, waiting for transfers between devices: 165 us -> 145 us  [flip(): return lambda v: lax.ppermute(v, 'fsdp', pairs)]
    unnamed x146 -> x159, local copies, waits for them, and re-layouts: 40.6 us -> 30.4 us
    all_to_all x8 -> x6, starting transfers between devices: 36.7 us -> 27.9 us  [everywhere(): return lax.all_to_all(v, 'fsdp', 0, 0, tiled=True)]
  transfers between devices with their start and end apart: 54 -> 52, of which waited for: 31 -> 31; matrix products, arithmetic and copies ran while one was open for 15% -> 15% of each run, Pallas kernels for 13% -> 13%
where the time goes in v5:
time: 671 us; the launch traced here: 663 us
  waiting for transfers between devices  259 us (39%)
  Pallas kernels  123 us (18%)
  matrix products  84.4 us (13%)
  starting transfers between devices  75.9 us (11%)
  blocking collectives  52.5 us (8%)
  local copies, waits for them, and re-layouts  36.4 us (5%)
  other arithmetic  16.6 us (2%)
  between operations  15.1 us (2%)
    ppermute x38, waiting for transfers between devices, flip(): return lambda v: lax.ppermute(v, 'fsdp', pairs)  145 us
    all_to_all x1, blocking collectives, everywhere(): return lax.all_to_all(v, 'fsdp', 0, 0, tiled=True)  52.5 us
    dot_general x7, matrix products, t_times(): lax.dot_general(left, right, (((0,), (0,)), ((), ())), preferred_element_...  46.4 us
    all_to_all x6, waiting for transfers between devices, everywhere(): return lax.all_to_all(v, 'fsdp', 0, 0, tiled=True)  44.5 us
    ppermute x38, starting transfers between devices, flip(): return lambda v: lax.ppermute(v, 'fsdp', pairs)  38.2 us
    all_gather x4, waiting for transfers between devices, gather(): lax.all_gather(v, 'fsdp', axis=0, tiled=True, axis_index_groups=self.halves)  38 us
    ppermute x4, waiting for transfers between devices, ahead(): return lambda v: lax.ppermute(v, 'fsdp', pairs)  31.6 us
    unnamed x159, local copies, waits for them, and re-layouts  30.4 us
  transfers between devices with their start and end apart: 52, of which 31 were waited for; matrix products, arithmetic and copies ran while one was open for 15% of the time, Pallas kernels for 13%

profile of v5, /device:TPU:0, one launch (start us, length us, event | category | flops | bytes accessed | tf_op | source)
XLA Modules:
  0.0 663.3 jit_solution(10677766215201294694)
XLA Ops:
  15.2 7.3 %collective-permute-done = bf16[128,2048]{1,0:T(8,128)(2,1)S(1)} collective-permute-done((bf16[128,2048]{1,0:T(8,128)(2,1)}, bf16[128,2048]{1,0:T(8,128)(2,1)S(1)}, u32[]{:S(2)}, u32[]{:S(2)}) %collective-permute-start) | collective-permute-done | bytes 524320 | tf_op jit(solution)/shard_map/ppermute | solution.py:567
  23.7 6.1 all-to-all-start
  34.7 34.4 %collective-permute-done.1 = bf16[128,2048]{1,0:T(8,128)(2,1)S(1)} collective-permute-done((bf16[128,2048]{1,0:T(8,128)(2,1)S(1)}, bf16[128,2048]{1,0:T(8,128)(2,1)S(1)}, u32[]{:S(2)}, u32[]{:S(2)}) %collective-permute-start.1) | collective-permute-done | bytes 524320 | tf_op jit(solution)/shard_map/ppermute | solution.py:567
  97.3 10.5 %shard_map.224 = (bf16[2048,2048]{1,0:T(8,128)(2,1)}, f32[2048,384]{1,0:T(8,128)}) custom-call(bf16[2048,2048]{1,0:T(8,128)(2,1)} %all-gather.5.cloned.1.call-done.x, f32[1,2048]{1,0:T(1,128)} %reshape.214.gain, bf16[2048,384]{1,0:T(8,128)(2,1)} %bitcast.5.w), custom_call_target="tpu_custom_call" | custom-call | flops 67108864 | bytes 1048576 | tf_op jit(solution)/shard_map/pallas_call | solution.py:299
  107.9 15.8 %shard_map.225 = (bf16[2,2048,128]{2,1,0:T(8,128)(2,1)}, bf16[2,2048,128]{2,1,0:T(8,128)(2,1)}, bf16[2048,128]{1,0:T(8,128)(2,1)}, bf16[2048,128]{1,0:T(8,128)(2...) custom-call(s32[32]{0:T(128)} %add.177.offsets, f32[2048,384]{1,0:T(8,128)} %get-tuple-element.279.qkv, ...), custom_call_target="tpu_custom_call" | custom-call | flops 67108864 | bytes 1048576 | tf_op jit(solution)/shard_map/pallas_call | solution.py:260
  133.1 5.9 all-to-all-done.2
  150.2 28.8 %collective-permute-done.5.refs_2_ = bf16[256,2048]{1,0:T(8,128)(2,1)S(1)} collective-permute-done((bf16[256,2048]{1,0:T(8,128)(2,1)S(1)}, bf16[256,2048]{1,0:T(8,128)(2,1)S(1)}, u32[]{:S(2)}, u32[]{:S(2)}) %collective-permute-start.5) | collective-permute-done | bytes 1048608 | tf_op jit(solution)/shard_map/ppermute | solution.py:567
  182.3 13.5 %collective-permute-done.9 = bf16[256,2048]{1,0:T(8,128)(2,1)S(1)} collective-permute-done((bf16[256,2048]{1,0:T(8,128)(2,1)S(1)}, bf16[256,2048]{1,0:T(8,128)(2,1)S(1)}, u32[]{:S(2)}, u32[]{:S(2)}) %collective-permute-start.9) | collective-permute-done | bytes 1048608 | tf_op jit(solution)/shard_map/ppermute | solution.py:572
  200.6 5.2 collective-permute-done.10.refs_2_
  205.8 5.6 collective-permute-done.11.refs_3_
  211.4 5.6 collective-permute-done.12.refs_6_
  222.3 5.1 all-to-all-start.3
  231.2 10.9 %fusion.25.dm = f32[2048,512]{1,0:T(8,128)} fusion(bf16[2048,2048]{1,0:T(8,128)(2,1)} %all-gather.7.cloned.1.call-done, bf16[512,2048]{1,0:T(8,128)(2,1)} %bitcast.11.right), kind=kOutput, calls=%fused_computation.77 | convolution fusion | flops 4294967296 | bytes 14680064 | tf_op jit(solution)/shard_map/dot_general | solution.py:42
  242.1 34.4 %all-to-all-done.3 = bf16[32,64,512]{2,1,0:T(8,128)(2,1)} async-done(((bf16[32,64,512]{2,1,0:T(8,128)(2,1)}), bf16[32,64,512]{2,1,0:T(8,128)(2,1)}, u32[]{:S(2)}, u32[]{:S(2)}) %all-to-all-start.3) | async-done | bytes 2097184 | tf_op jit(solution)/shard_map/all_to_all | solution.py:578
  276.5 19.3 %all-gather.9.cloned.1.call-done.h = bf16[2048,2048]{1,0:T(8,128)(2,1)} async-done(((bf16[256,2048]{1,0:T(8,128)(2,1)}), bf16[2048,2048]{1,0:T(8,128)(2,1)}) %all-gather.9.cloned.1.call-update) | async-done | bytes 8388624 | tf_op jit(solution)/shard_map/all_gather | solution.py:581
  295.8 27.4 %shard_map.230 = (bf16[2048,512]{1,0:T(8,128)(2,1)}, bf16[2048,512]{1,0:T(8,128)(2,1)}, bf16[2048,512]{1,0:T(8,128)(2,1)}, bf16[512,2048]{1,0:T(8,128)(2,1)}, bf...) custom-call(s32[17]{0:T(128)} %pad_add_fusion.1.spots, ...), custom_call_target="tpu_custom_call" | custom-call | flops 67108864 | bytes 1048576 | tf_op jit(solution)/shard_map/pallas_call | solution.py:345
  323.8 6.2 convolution_convert_fusion.11
  339.1 10.1 %convolution_convert_fusion.9 = bf16[2048,512]{1,0:T(8,128)(2,1)} fusion(bf16[2048,2048]{1,0:T(8,128)(2,1)} %all-gather.9.cloned.1.call-done.h, bf16[2048,512]{1,0:T(8,128)(2,1)S(1)} %copy-done.69), kind=kOutput, calls=%fused_computation.9 | convolution fusion | flops 4296015872 | bytes 12582912 | tf_op jit(solution)/shard_map/dot_general | solution.py:46
  349.2 7.2 %shard_map.232 = (bf16[512,2048]{1,0:T(8,128)(2,1)S(1)}, bf16[512,2048]{1,0:T(8,128)(2,1)S(1)}, bf16[512,2048]{1,0:T(8,128)(2,1)S(1)}, bf16[512,2048]{1,0:T(8,128)(2,1)S(1)}) custom-call(s32[17]{0:T(128)S(1)} %copy-done.52, bf16[2048,512]{1,0:T(8,128)(2,1)S(1)} %copy-done.2, bf16[512,2048]{1,0:T(8,128)(2,1)} %bitcast.11.right), custom_call_target="tpu_custom_call" | custom-call | flops 67108864 | bytes 1048576 | tf_op jit(solution)/shard_map/pallas_call | solution.py:365
  368.1 17.4 %collective-permute-done.20 = bf16[256,2048]{1,0:T(8,128)(2,1)S(1)} collective-permute-done((bf16[256,2048]{1,0:T(8,128)(2,1)S(1)}, bf16[256,2048]{1,0:T(8,128)(2,1)S(1)}, u32[]{:S(2)}, u32[]{:S(2)}) %collective-permute-start.20) | collective-permute-done | bytes 1048608 | tf_op jit(solution)/shard_map/ppermute | solution.py:572
  399.3 9.5 %convolution_convert_fusion.8 = bf16[2048,512]{1,0:T(8,128)(2,1)} fusion(bf16[2048,2048]{1,0:T(8,128)(2,1)} %all-gather.9.cloned.1.call-done.h, bf16[2048,512]{1,0:T(8,128)(2,1)S(1)} %copy-done.68), kind=kOutput, calls=%fused_computation.8 | convolution fusion | flops 4296015872 | bytes 12582912 | tf_op jit(solution)/shard_map/dot_general | solution.py:46
  412.0 10.6 %collective-permute-done.27.refs_2_ = bf16[256,2048]{1,0:T(8,128)(2,1)S(1)} collective-permute-done((bf16[256,2048]{1,0:T(8,128)(2,1)S(1)}, bf16[256,2048]{1,0:T(8,128)(2,1)S(1)}, u32[]{:S(2)}, u32[]{:S(2)}) %collective-permute-start.27) | collective-permute-done | bytes 1048608 | tf_op jit(solution)/shard_map/ppermute | solution.py:567
  428.3 52.5 %all_to_all.42.v = bf16[32,64,512]{2,1,0:T(8,128)(2,1)} all-to-all(bf16[32,64,512]{2,1,0:T(8,128)(2,1)} %bitcast.60), channel_id=1, replica_groups=mesh['fsdp'=32] {'fsdp'}, dimensions={0} | all-to-all | bytes 4194304 | tf_op jit(solution)/shard_map/all_to_all | solution.py:578
  480.9 18.7 %all-gather.11.cloned.1.call-done = bf16[2048,2048]{1,0:T(8,128)(2,1)} async-done(((bf16[256,2048]{1,0:T(8,128)(2,1)}), bf16[2048,2048]{1,0:T(8,128)(2,1)}) %all-gather.11.cloned.1.call-update) | async-done | bytes 8388624 | tf_op jit(solution)/shard_map/all_gather | solution.py:581
  514.7 6.5 convolution_convert_fusion.12.dout
  521.3 22.2 %shard_map.237 = (bf16[2048,384]{1,0:T(8,128)(2,1)}, bf16[2048,384]{1,0:T(8,128)(2,1)}) custom-call(s32[32]{0:T(128)} %add.177.offsets, bf16[2,2048,128]{2,1,0:T(8,128)(2,1)} %get-tuple-element.420.qe, bf16[2,2048,128]{2,1,0:T(8,128)(2,1)} %get-tuple-element.421.ke, bf16[2048,128]{1,0:T(8,128)(2,1)} %get-tuple-element.422.vs, ...), custom_call_target="tpu_custom_call" | custom-call | flops 67108864 | bytes 1048576 | tf_op jit(solution)/shard_map/pallas_call | solution.py:276
  549.9 9.1 %convolution_convert_fusion.10 = bf16[2048,384]{1,0:T(8,128)(2,1)} fusion(bf16[2048,2048]{1,0:T(8,128)(2,1)} %get-tuple-element.436, bf16[2048,384]{1,0:T(8,128)(2,1)S(1)} %copy-done.70), kind=kOutput, calls=%fused_computation.10 | convolution fusion | flops 3222011904 | bytes 11534336 | tf_op jit(solution)/shard_map/dot_general | solution.py:46
  582.8 5.2 convolution_convert_fusion.13
  589.8 8.2 %collective-permute-done.35.refs_2_ = bf16[64,2048]{1,0:T(8,128)(2,1)S(1)} collective-permute-done((bf16[64,2048]{1,0:T(8,128)(2,1)S(1)}, bf16[64,2048]{1,0:T(8,128)(2,1)S(1)}, u32[]{:S(2)}, u32[]{:S(2)}) %collective-permute-start.35) | collective-permute-done | bytes 262176 | tf_op jit(solution)/shard_map/ppermute | solution.py:567
  598.0 7.0 %collective-permute-done.36.refs_3_ = bf16[64,2048]{1,0:T(8,128)(2,1)S(1)} collective-permute-done((bf16[64,2048]{1,0:T(8,128)(2,1)S(1)}, bf16[64,2048]{1,0:T(8,128)(2,1)S(1)}, u32[]{:S(2)}, u32[]{:S(2)}) %collective-permute-start.36) | collective-permute-done | bytes 262176 | tf_op jit(solution)/shard_map/ppermute | solution.py:567
  631.3 5.7 collective-permute-done.39.refs_2_
  643.2 5.0 shard_map.247
  (323 shorter events, 211.1 us)
Async XLA Ops:
  7.2 90.1 %all-gather.5.cloned.1.call-start = ((), (), s32[]{:S(2)}) async-start(), calls=%async_computation.7 | async-start | bytes 9437184 | tf_op jit(solution)/shard_map/all_gather | solution.py:581
  23.7 45.4 %all-to-all-start = ((bf16[32,64,384]{2,1,0:T(8,128)(2,1)}), bf16[32,64,384]{2,1,0:T(8,128)(2,1)}, u32[]{:S(2)}, u32[]{:S(2)}) async-start(bf16[32,64,384]{2,1,0:T(8,128)(2,1)} %shard_map.221), calls=%async_computation | async-start | bytes 3145728 | tf_op jit(solution)/shard_map/all_to_all | solution.py:578
  29.9 201.3 %all-gather.7.cloned.1.call-start = ((), (), s32[]{:S(2)}) async-start(), calls=%async_computation.8 | async-start | bytes 9437184 | tf_op jit(solution)/shard_map/all_gather | solution.py:581
  29.9 39.2 %collective-permute-start.1 = (bf16[128,2048]{1,0:T(8,128)(2,1)S(1)}, bf16[128,2048]{1,0:T(8,128)(2,1)S(1)}, u32[]{:S(2)}, u32[]{:S(2)}) collective-permute-start(bf16[128,2048]{1,0:T(8,128)(2,1)S(1)} %copy-done.64), channel_id=1, source_target_pairs={{0,8},{1,9},{2,10},{3,11},{4,12},{5,13},{6,14},{7,15},{8,0},{9,1},... | collective-permute-start | bytes 1572872 | tf_op jit(solution)/shard_map/ppermute | solution.py:567
  77.8 19.4 %collective-permute-start.2 = (bf16[64,2048]{1,0:T(8,128)(2,1)S(1)}, bf16[64,2048]{1,0:T(8,128)(2,1)S(1)}, u32[]{:S(2)}, u32[]{:S(2)}) collective-permute-start(bf16[64,2048]{1,0:T(8,128)(2,1)S(1)} %copy-done.67), channel_id=1, source_target_pairs={{0,16},{1,17},{2,18},{3,19},{4,20},{5,21},{6,22},{7,23},{8,24},{9,... | collective-permute-start | bytes 786440 | tf_op jit(solution)/shard_map/ppermute | solution.py:572
  84.7 54.3 %all-to-all-start.2 = ((bf16[32,64,512]{2,1,0:T(8,128)(2,1)}), bf16[32,64,512]{2,1,0:T(8,128)(2,1)}, u32[]{:S(2)}, u32[]{:S(2)}) async-start(bf16[32,64,512]{2,1,0:T(8,128)(2,1)} %shard_map.222), calls=%async_computation.2 | async-start | bytes 4194304 | tf_op jit(solution)/shard_map/all_to_all | solution.py:578
  88.2 207.6 %all-gather.9.cloned.1.call-start = ((), (), s32[]{:S(2)}) async-start(), calls=%async_computation.9 | async-start | bytes 9437184 | tf_op jit(solution)/shard_map/all_gather | solution.py:581
  144.7 34.3 %collective-permute-start.5 = (bf16[256,2048]{1,0:T(8,128)(2,1)S(1)}, bf16[256,2048]{1,0:T(8,128)(2,1)S(1)}, u32[]{:S(2)}, u32[]{:S(2)}) collective-permute-start(bf16[256,2048]{1,0:T(8,128)(2,1)S(1)} %get-tuple-element.299), channel_id=1, source_target_pairs={{0,4},{1,5},{2,6},{3,7},{4,0},{5,1},{6,2},{7,3},{8,12},{9,13},{10,... | collective-permute-start | bytes 3145736 | tf_op jit(solution)/shard_map/ppermute | solution.py:567
  146.3 32.8 %collective-permute-start.6 = (bf16[256,2048]{1,0:T(8,128)(2,1)S(1)}, bf16[256,2048]{1,0:T(8,128)(2,1)S(1)}, u32[]{:S(2)}, u32[]{:S(2)}) collective-permute-start(bf16[256,2048]{1,0:T(8,128)(2,1)S(1)} %get-tuple-element.301), channel_id=1, source_target_pairs={{0,2},{1,3},{2,0},{3,1},{4,6},{5,7},{6,4},{7,5},{8,10},{9,11},{10,... | collective-permute-start | bytes 3145736 | tf_op jit(solution)/shard_map/ppermute | solution.py:567
  147.7 48.0 %collective-permute-start.9 = (bf16[256,2048]{1,0:T(8,128)(2,1)S(1)}, bf16[256,2048]{1,0:T(8,128)(2,1)S(1)}, u32[]{:S(2)}, u32[]{:S(2)}) collective-permute-start(bf16[256,2048]{1,0:T(8,128)(2,1)S(1)} %copy-done.60), channel_id=1, source_target_pairs={{0,16},{1,17},{2,18},{3,19},{4,20},{5,21},{6,22},{7,23},{8,24},{9,... | collective-permute-start | bytes 3145736 | tf_op jit(solution)/shard_map/ppermute | solution.py:572
  198.5 18.5 %collective-permute-start.12 = (bf16[64,2048]{1,0:T(8,128)(2,1)S(1)}, bf16[64,2048]{1,0:T(8,128)(2,1)S(1)}, u32[]{:S(2)}, u32[]{:S(2)}) collective-permute-start(bf16[64,2048]{1,0:T(8,128)(2,1)S(1)} %get-tuple-element.322), channel_id=1, source_target_pairs={{0,8},{1,9},{2,10},{3,11},{4,12},{5,13},{6,14},{7,15},{8,0},{9,1},... | collective-permute-start | bytes 786440 | tf_op jit(solution)/shard_map/ppermute | solution.py:567
  199.1 21.3 %collective-permute-start.13 = (bf16[64,2048]{1,0:T(8,128)(2,1)S(1)}, bf16[64,2048]{1,0:T(8,128)(2,1)S(1)}, u32[]{:S(2)}, u32[]{:S(2)}) collective-permute-start(bf16[64,2048]{1,0:T(8,128)(2,1)S(1)} %get-tuple-element.324), channel_id=1, source_target_pairs={{0,8},{1,9},{2,10},{3,11},{4,12},{5,13},{6,14},{7,15},{8,0},{9,1},... | collective-permute-start | bytes 786440 | tf_op jit(solution)/shard_map/ppermute | solution.py:567
  222.3 54.2 %all-to-all-start.3 = ((bf16[32,64,512]{2,1,0:T(8,128)(2,1)}), bf16[32,64,512]{2,1,0:T(8,128)(2,1)}, u32[]{:S(2)}, u32[]{:S(2)}) async-start(bf16[32,64,512]{2,1,0:T(8,128)(2,1)} %copy-done.3), calls=%async_computation.3 | async-start | bytes 4194304 | tf_op jit(solution)/shard_map/all_to_all | solution.py:578
  227.5 272.1 %all-gather.11.cloned.1.call-start = ((), (), s32[]{:S(2)}) async-start(), calls=%async_computation.10 | async-start | bytes 9437184 | tf_op jit(solution)/shard_map/all_gather | solution.py:581
  335.1 25.4 %collective-permute-start.16 = (bf16[256,2048]{1,0:T(8,128)(2,1)S(1)}, bf16[256,2048]{1,0:T(8,128)(2,1)S(1)}, u32[]{:S(2)}, u32[]{:S(2)}) collective-permute-start(bf16[256,2048]{1,0:T(8,128)(2,1)S(1)} %get-tuple-element.359), channel_id=1, source_target_pairs={{0,4},{1,5},{2,6},{3,7},{4,0},{5,1},{6,2},{7,3},{8,12},{9,13},{10,... | collective-permute-start | bytes 3145736 | tf_op jit(solution)/shard_map/ppermute | solution.py:567
  335.7 25.0 %collective-permute-start.17 = (bf16[256,2048]{1,0:T(8,128)(2,1)S(1)}, bf16[256,2048]{1,0:T(8,128)(2,1)S(1)}, u32[]{:S(2)}, u32[]{:S(2)}) collective-permute-start(bf16[256,2048]{1,0:T(8,128)(2,1)S(1)} %get-tuple-element.361), channel_id=1, source_target_pairs={{0,2},{1,3},{2,0},{3,1},{4,6},{5,7},{6,4},{7,5},{8,10},{9,11},{10,... | collective-permute-start | bytes 3145736 | tf_op jit(solution)/shard_map/ppermute | solution.py:567
  337.4 48.1 %collective-permute-start.20 = (bf16[256,2048]{1,0:T(8,128)(2,1)S(1)}, bf16[256,2048]{1,0:T(8,128)(2,1)S(1)}, u32[]{:S(2)}, u32[]{:S(2)}) collective-permute-start(bf16[256,2048]{1,0:T(8,128)(2,1)S(1)} %convolution_convert_fusion.11), channel_id=1, source_target_pairs={{0,16},{1,17},{2,18},{3,19},{4,20},{5,21},{6,22},{7,23},{8,24},{9,... | collective-permute-start | bytes 3145736 | tf_op jit(solution)/shard_map/ppermute | solution.py:572
  361.8 23.7 %collective-permute-start.18 = (bf16[128,2048]{1,0:T(8,128)(2,1)S(1)}, bf16[128,2048]{1,0:T(8,128)(2,1)S(1)}, u32[]{:S(2)}, u32[]{:S(2)}) collective-permute-start(bf16[128,2048]{1,0:T(8,128)(2,1)S(1)} %get-tuple-element.375), channel_id=1, source_target_pairs={{0,2},{1,3},{2,0},{3,1},{4,6},{5,7},{6,4},{7,5},{8,10},{9,11},{10,... | collective-permute-start | bytes 1572872 | tf_op jit(solution)/shard_map/ppermute | solution.py:567
  363.5 22.0 %collective-permute-start.19 = (bf16[128,2048]{1,0:T(8,128)(2,1)S(1)}, bf16[128,2048]{1,0:T(8,128)(2,1)S(1)}, u32[]{:S(2)}, u32[]{:S(2)}) collective-permute-start(bf16[128,2048]{1,0:T(8,128)(2,1)S(1)} %get-tuple-element.377), channel_id=1, source_target_pairs={{0,4},{1,5},{2,6},{3,7},{4,0},{5,1},{6,2},{7,3},{8,12},{9,13},{10,... | collective-permute-start | bytes 1572872 | tf_op jit(solution)/shard_map/ppermute | solution.py:567
  387.2 21.6 %collective-permute-start.24 = (bf16[64,2048]{1,0:T(8,128)(2,1)S(1)}, bf16[64,2048]{1,0:T(8,128)(2,1)S(1)}, u32[]{:S(2)}, u32[]{:S(2)}) collective-permute-start(bf16[64,2048]{1,0:T(8,128)(2,1)S(1)} %get-tuple-element.394.refs_5_), channel_id=1, source_target_pairs={{0,8},{1,9},{2,10},{3,11},{4,12},{5,13},{6,14},{7,15},{8,0},{9,1},... | collective-permute-start | bytes 786440 | tf_op jit(solution)/shard_map/ppermute | solution.py:567
  389.2 19.6 %collective-permute-start.25 = (bf16[64,2048]{1,0:T(8,128)(2,1)S(1)}, bf16[64,2048]{1,0:T(8,128)(2,1)S(1)}, u32[]{:S(2)}, u32[]{:S(2)}) collective-permute-start(bf16[64,2048]{1,0:T(8,128)(2,1)S(1)} %get-tuple-element.396), channel_id=1, source_target_pairs={{0,8},{1,9},{2,10},{3,11},{4,12},{5,13},{6,14},{7,15},{8,0},{9,1},... | collective-permute-start | bytes 786440 | tf_op jit(solution)/shard_map/ppermute | solution.py:567
  389.7 22.2 %collective-permute-start.26 = (bf16[64,2048]{1,0:T(8,128)(2,1)S(1)}, bf16[64,2048]{1,0:T(8,128)(2,1)S(1)}, u32[]{:S(2)}, u32[]{:S(2)}) collective-permute-start(bf16[64,2048]{1,0:T(8,128)(2,1)S(1)} %get-tuple-element.398), channel_id=1, source_target_pairs={{0,8},{1,9},{2,10},{3,11},{4,12},{5,13},{6,14},{7,15},{8,0},{9,1},... | collective-permute-start | bytes 786440 | tf_op jit(solution)/shard_map/ppermute | solution.py:567
  397.4 25.2 %collective-permute-start.27 = (bf16[256,2048]{1,0:T(8,128)(2,1)S(1)}, bf16[256,2048]{1,0:T(8,128)(2,1)S(1)}, u32[]{:S(2)}, u32[]{:S(2)}) collective-permute-start(bf16[256,2048]{1,0:T(8,128)(2,1)S(1)} %get-tuple-element.404), channel_id=1, source_target_pairs={{0,4},{1,5},{2,6},{3,7},{4,0},{5,1},{6,2},{7,3},{8,12},{9,13},{10,... | collective-permute-start | bytes 3145736 | tf_op jit(solution)/shard_map/ppermute | solution.py:567
  398.2 25.4 %collective-permute-start.28 = (bf16[256,2048]{1,0:T(8,128)(2,1)S(1)}, bf16[256,2048]{1,0:T(8,128)(2,1)S(1)}, u32[]{:S(2)}, u32[]{:S(2)}) collective-permute-start(bf16[256,2048]{1,0:T(8,128)(2,1)S(1)} %get-tuple-element.406), channel_id=1, source_target_pairs={{0,2},{1,3},{2,0},{3,1},{4,6},{5,7},{6,4},{7,5},{8,10},{9,11},{10,... | collective-permute-start | bytes 3145736 | tf_op jit(solution)/shard_map/ppermute | solution.py:567
  499.5 62.1 %all-to-all-start.5 = ((bf16[32,64,512]{2,1,0:T(8,128)(2,1)}), bf16[32,64,512]{2,1,0:T(8,128)(2,1)}, u32[]{:S(2)}, u32[]{:S(2)}) async-start(bf16[32,64,512]{2,1,0:T(8,128)(2,1)} %bitcast.61), calls=%async_computation.5 | async-start | bytes 4194304 | tf_op jit(solution)/shard_map/all_to_all | solution.py:578
  511.6 37.7 %collective-permute-start.29 = (bf16[128,2048]{1,0:T(8,128)(2,1)S(1)}, bf16[128,2048]{1,0:T(8,128)(2,1)S(1)}, u32[]{:S(2)}, u32[]{:S(2)}) collective-permute-start(bf16[128,2048]{1,0:T(8,128)(2,1)S(1)} %get-tuple-element.432), channel_id=1, source_target_pairs={{0,2},{1,3},{2,0},{3,1},{4,6},{5,7},{6,4},{7,5},{8,10},{9,11},{10,... | collective-permute-start | bytes 1572872 | tf_op jit(solution)/shard_map/ppermute | solution.py:567
  513.3 36.0 %collective-permute-start.30 = (bf16[128,2048]{1,0:T(8,128)(2,1)S(1)}, bf16[128,2048]{1,0:T(8,128)(2,1)S(1)}, u32[]{:S(2)}, u32[]{:S(2)}) collective-permute-start(bf16[128,2048]{1,0:T(8,128)(2,1)S(1)} %get-tuple-element.434), channel_id=1, source_target_pairs={{0,4},{1,5},{2,6},{3,7},{4,0},{5,1},{6,2},{7,3},{8,12},{9,13},{10,... | collective-permute-start | bytes 1572872 | tf_op jit(solution)/shard_map/ppermute | solution.py:567
  561.7 81.5 %all-to-all-start.6 = ((bf16[32,64,384]{2,1,0:T(8,128)(2,1)}), bf16[32,64,384]{2,1,0:T(8,128)(2,1)}, u32[]{:S(2)}, u32[]{:S(2)}) async-start(bf16[32,64,384]{2,1,0:T(8,128)(2,1)} %bitcast.62), calls=%async_computation.6 | async-start | bytes 3145728 | tf_op jit(solution)/shard_map/all_to_all | solution.py:578
  573.8 35.5 %collective-permute-start.33 = (bf16[256,2048]{1,0:T(8,128)(2,1)S(1)}, bf16[256,2048]{1,0:T(8,128)(2,1)S(1)}, u32[]{:S(2)}, u32[]{:S(2)}) collective-permute-start(bf16[256,2048]{1,0:T(8,128)(2,1)S(1)} %get-tuple-element.450), channel_id=1, source_target_pairs={{0,4},{1,5},{2,6},{3,7},{4,0},{5,1},{6,2},{7,3},{8,12},{9,13},{10,... | collective-permute-start | bytes 3145736 | tf_op jit(solution)/shard_map/ppermute | solution.py:567
  575.8 33.6 %collective-permute-start.34 = (bf16[256,2048]{1,0:T(8,128)(2,1)S(1)}, bf16[256,2048]{1,0:T(8,128)(2,1)S(1)}, u32[]{:S(2)}, u32[]{:S(2)}) collective-permute-start(bf16[256,2048]{1,0:T(8,128)(2,1)S(1)} %get-tuple-element.452), channel_id=1, source_target_pairs={{0,2},{1,3},{2,0},{3,1},{4,6},{5,7},{6,4},{7,5},{8,10},{9,11},{10,... | collective-permute-start | bytes 3145736 | tf_op jit(solution)/shard_map/ppermute | solution.py:567
  580.8 17.2 %collective-permute-start.35 = (bf16[64,2048]{1,0:T(8,128)(2,1)S(1)}, bf16[64,2048]{1,0:T(8,128)(2,1)S(1)}, u32[]{:S(2)}, u32[]{:S(2)}) collective-permute-start(bf16[64,2048]{1,0:T(8,128)(2,1)S(1)} %get-tuple-element.458), channel_id=1, source_target_pairs={{0,8},{1,9},{2,10},{3,11},{4,12},{5,13},{6,14},{7,15},{8,0},{9,1},... | collective-permute-start | bytes 786440 | tf_op jit(solution)/shard_map/ppermute | solution.py:567
  582.2 22.8 %collective-permute-start.36 = (bf16[64,2048]{1,0:T(8,128)(2,1)S(1)}, bf16[64,2048]{1,0:T(8,128)(2,1)S(1)}, u32[]{:S(2)}, u32[]{:S(2)}) collective-permute-start(bf16[64,2048]{1,0:T(8,128)(2,1)S(1)} %get-tuple-element.460), channel_id=1, source_target_pairs={{0,8},{1,9},{2,10},{3,11},{4,12},{5,13},{6,14},{7,15},{8,0},{9,1},... | collective-permute-start | bytes 786440 | tf_op jit(solution)/shard_map/ppermute | solution.py:567
  (99 other events, 1000.4 us)
Sparse Core Ops, SparseCore 0:
  23.9 67.9 all-gather.4
  93.7 73.6 all-gather.6
  222.5 73.2 all-gather.8
  428.5 71.0 all-gather.10

commit v6 on v5

--- a/solution.py
+++ b/solution.py
@@ -706,6 +706,10 @@
         values, rest = tied[: len(values)], tied[len(values) :]
         transfer.moves = [(v, move) for v, (_, move) in zip(rest, transfer.moves)]
         return values
+
+    def ready(self, transfer, transfers):
+        made = self.wait(transfers, *[v for v, _ in transfer.moves])
+        transfer.moves = [(v, move) for v, (_, move) in zip(made, transfer.moves)]
 
     def wait(self, transfers, *values):
         tied = list(barrier(self.token, *values, *[g for t in transfers for g in t.got]))
@@ -868,7 +872,7 @@
     send_gate = Transfer(team.owners(grad_gate))
     send_up = Transfer(team.owners(grad_up))
     start(get_da, send_gate)
-    wait([get_da, send_gate])
+    clock.ready(add_result, [get_da, send_gate])
     da = get_da.value
     start(send_up, add_result)
     dout = times_t(da, out_rows).astype(BF)
@@ -898,17 +902,16 @@
     grad_up, share_up = join_columns(send_up.value, [w_up], size, *ff_cut)
     grad_gain_mlp = (share_gate + share_up)[:, 0] / gain_mlp.astype(F32)
     result = own_result(here, x2, add_result.value)
-    grad_up, result = wait([add_dh1], grad_up, result)
+    grad_up, result = wait([add_dh1, send_qkv], grad_up, result)
     start(add_dh1)
+    grads = join_columns(send_qkv.value, [w_query, w_key, w_value], size, *head_cut)
     if whole_heads:
-        wait([add_dh1, send_qkv, send_out])
+        grads = wait([add_dh1, send_out], *grads)
         grad_out = send_out.value
     else:
-        wait([add_dh1, send_qkv])
+        grads = wait([add_dh1], *grads)
+    grad_query, grad_key, grad_value, share = grads
     grad_tokens = own_back(here, tokens, dx2, gain_one, add_dh1.value)
-    grad_query, grad_key, grad_value, share = join_columns(
-        send_qkv.value, [w_query, w_key, w_value], size, *head_cut
-    )
     grad_gain_attn = share[:, 0] / gain_attn.astype(F32)
     return (
         result,

time: 671 us -> 664 us (0.990)
  blocking collectives: 52.5 us -> 0 us
  waiting for transfers between devices: 259 us -> 288 us
  local copies, waits for them, and re-layouts: 36.4 us -> 47.1 us
    all_to_all x1 -> x0, blocking collectives: 52.5 us -> none  [everywhere(): return lax.all_to_all(v, 'fsdp', 0, 0, tiled=True)]
    all_to_all x6 -> x7, waiting for transfers between devices: 44.5 us -> 82.8 us  [everywhere(): return lax.all_to_all(v, 'fsdp', 0, 0, tiled=True)]
    unnamed x159 -> x169, local copies, waits for them, and re-layouts: 30.4 us -> 41.1 us
    ppermute x38, waiting for transfers between devices: 145 us -> 135 us  [flip(): return lambda v: lax.ppermute(v, 'fsdp', pairs)]
    all_to_all x6 -> x7, starting transfers between devices: 27.9 us -> 31.6 us  [everywhere(): return lax.all_to_all(v, 'fsdp', 0, 0, tiled=True)]
  transfers between devices with their start and end apart: 52 -> 53, of which waited for: 31 -> 29; matrix products, arithmetic and copies ran while one was open for 15% -> 16% of each run, Pallas kernels for 13% -> 14%
where the time goes in v6:
time: 664 us; the launch traced here: 656 us
  waiting for transfers between devices  288 us (43%)
  Pallas kernels  125 us (19%)
  matrix products  85.3 us (13%)
  starting transfers between devices  79.4 us (12%)
  local copies, waits for them, and re-layouts  47.1 us (7%)
  other arithmetic  16.6 us (3%)
  between operations  15.1 us (2%)
    ppermute x38, waiting for transfers between devices, flip(): return lambda v: lax.ppermute(v, 'fsdp', pairs)  135 us
    all_to_all x7, waiting for transfers between devices, everywhere(): return lax.all_to_all(v, 'fsdp', 0, 0, tiled=True)  82.8 us
    dot_general x7, matrix products, t_times(): lax.dot_general(left, right, (((0,), (0,)), ((), ())), preferred_element_...  47.1 us
    unnamed x169, local copies, waits for them, and re-layouts  41.1 us
    all_gather x4, waiting for transfers between devices, gather(): lax.all_gather(v, 'fsdp', axis=0, tiled=True, axis_index_groups=self.halves)  38.6 us
    ppermute x38, starting transfers between devices, flip(): return lambda v: lax.ppermute(v, 'fsdp', pairs)  38 us
    all_to_all x7, starting transfers between devices, everywhere(): return lax.all_to_all(v, 'fsdp', 0, 0, tiled=True)  31.6 us
    ppermute x4, waiting for transfers between devices, ahead(): return lambda v: lax.ppermute(v, 'fsdp', pairs)  30.9 us
  transfers between devices with their start and end apart: 53, of which 29 were waited for; matrix products, arithmetic and copies ran while one was open for 16% of the time, Pallas kernels for 14%

profile of v6, /device:TPU:0, one launch (start us, length us, event | category | flops | bytes accessed | tf_op | source)
XLA Modules:
  0.0 655.8 jit_solution(6118445841862895336)
XLA Ops:
  15.2 7.3 %collective-permute-done = bf16[128,2048]{1,0:T(8,128)(2,1)S(1)} collective-permute-done((bf16[128,2048]{1,0:T(8,128)(2,1)}, bf16[128,2048]{1,0:T(8,128)(2,1)S(1)}, u32[]{:S(2)}, u32[]{:S(2)}) %collective-permute-start) | collective-permute-done | bytes 524320 | tf_op jit(solution)/shard_map/ppermute | solution.py:567
  23.7 6.1 all-to-all-start
  34.7 34.4 %collective-permute-done.1 = bf16[128,2048]{1,0:T(8,128)(2,1)S(1)} collective-permute-done((bf16[128,2048]{1,0:T(8,128)(2,1)S(1)}, bf16[128,2048]{1,0:T(8,128)(2,1)S(1)}, u32[]{:S(2)}, u32[]{:S(2)}) %collective-permute-start.1) | collective-permute-done | bytes 524320 | tf_op jit(solution)/shard_map/ppermute | solution.py:567
  72.5 4.7 all-to-all-start.1
  97.4 10.6 %shard_map.224 = (bf16[2048,2048]{1,0:T(8,128)(2,1)}, f32[2048,384]{1,0:T(8,128)}) custom-call(bf16[2048,2048]{1,0:T(8,128)(2,1)} %all-gather.5.cloned.1.call-done.x, f32[1,2048]{1,0:T(1,128)} %reshape.214.gain, bf16[2048,384]{1,0:T(8,128)(2,1)} %bitcast.5.w), custom_call_target="tpu_custom_call" | custom-call | flops 67108864 | bytes 1048576 | tf_op jit(solution)/shard_map/pallas_call | solution.py:299
  107.9 15.8 %shard_map.225 = (bf16[2,2048,128]{2,1,0:T(8,128)(2,1)}, bf16[2,2048,128]{2,1,0:T(8,128)(2,1)}, bf16[2048,128]{1,0:T(8,128)(2,1)}, bf16[2048,128]{1,0:T(8,128)(2...) custom-call(s32[32]{0:T(128)} %add.177.offsets, f32[2048,384]{1,0:T(8,128)} %get-tuple-element.285.qkv, ...), custom_call_target="tpu_custom_call" | custom-call | flops 67108864 | bytes 1048576 | tf_op jit(solution)/shard_map/pallas_call | solution.py:260
  133.2 5.8 all-to-all-done.2
  150.2 28.7 %collective-permute-done.5.refs_2_ = bf16[256,2048]{1,0:T(8,128)(2,1)S(1)} collective-permute-done((bf16[256,2048]{1,0:T(8,128)(2,1)S(1)}, bf16[256,2048]{1,0:T(8,128)(2,1)S(1)}, u32[]{:S(2)}, u32[]{:S(2)}) %collective-permute-start.5) | collective-permute-done | bytes 1048608 | tf_op jit(solution)/shard_map/ppermute | solution.py:567
  182.3 13.5 %collective-permute-done.9 = bf16[256,2048]{1,0:T(8,128)(2,1)S(1)} collective-permute-done((bf16[256,2048]{1,0:T(8,128)(2,1)S(1)}, bf16[256,2048]{1,0:T(8,128)(2,1)S(1)}, u32[]{:S(2)}, u32[]{:S(2)}) %collective-permute-start.9) | collective-permute-done | bytes 1048608 | tf_op jit(solution)/shard_map/ppermute | solution.py:572
  200.6 5.2 collective-permute-done.10.refs_2_
  205.8 5.6 collective-permute-done.11.refs_3_
  211.4 5.6 collective-permute-done.12.refs_6_
  222.4 5.1 all-to-all-start.3
  231.2 10.9 %fusion.25.dm = f32[2048,512]{1,0:T(8,128)} fusion(bf16[2048,2048]{1,0:T(8,128)(2,1)} %all-gather.7.cloned.1.call-done, bf16[512,2048]{1,0:T(8,128)(2,1)} %bitcast.11.right), kind=kOutput, calls=%fused_computation.77 | convolution fusion | flops 4294967296 | bytes 14680064 | tf_op jit(solution)/shard_map/dot_general | solution.py:42
  242.2 34.4 %all-to-all-done.3 = bf16[32,64,512]{2,1,0:T(8,128)(2,1)} async-done(((bf16[32,64,512]{2,1,0:T(8,128)(2,1)}), bf16[32,64,512]{2,1,0:T(8,128)(2,1)}, u32[]{:S(2)}, u32[]{:S(2)}) %all-to-all-start.3) | async-done | bytes 2097184 | tf_op jit(solution)/shard_map/all_to_all | solution.py:578
  276.6 19.3 %all-gather.9.cloned.1.call-done.h = bf16[2048,2048]{1,0:T(8,128)(2,1)} async-done(((bf16[256,2048]{1,0:T(8,128)(2,1)}), bf16[2048,2048]{1,0:T(8,128)(2,1)}) %all-gather.9.cloned.1.call-update) | async-done | bytes 8388624 | tf_op jit(solution)/shard_map/all_gather | solution.py:581
  295.8 27.3 %shard_map.230 = (bf16[2048,512]{1,0:T(8,128)(2,1)}, bf16[2048,512]{1,0:T(8,128)(2,1)}, bf16[2048,512]{1,0:T(8,128)(2,1)}, bf16[512,2048]{1,0:T(8,128)(2,1)}, bf...) custom-call(s32[17]{0:T(128)} %pad_add_fusion.1.spots, ...), custom_call_target="tpu_custom_call" | custom-call | flops 67108864 | bytes 1048576 | tf_op jit(solution)/shard_map/pallas_call | solution.py:345
  323.8 6.2 convolution_convert_fusion.11
  339.1 10.1 %convolution_convert_fusion.9 = bf16[2048,512]{1,0:T(8,128)(2,1)} fusion(bf16[2048,2048]{1,0:T(8,128)(2,1)} %all-gather.9.cloned.1.call-done.h, bf16[2048,512]{1,0:T(8,128)(2,1)S(1)} %copy-done.74), kind=kOutput, calls=%fused_computation.9 | convolution fusion | flops 4296015872 | bytes 12582912 | tf_op jit(solution)/shard_map/dot_general | solution.py:46
  349.2 7.2 %shard_map.232 = (bf16[512,2048]{1,0:T(8,128)(2,1)S(1)}, bf16[512,2048]{1,0:T(8,128)(2,1)S(1)}, bf16[512,2048]{1,0:T(8,128)(2,1)S(1)}, bf16[512,2048]{1,0:T(8,128)(2,1)S(1)}) custom-call(s32[17]{0:T(128)S(1)} %copy-done.57, bf16[2048,512]{1,0:T(8,128)(2,1)S(1)} %copy-done.2, bf16[512,2048]{1,0:T(8,128)(2,1)} %bitcast.11.right), custom_call_target="tpu_custom_call" | custom-call | flops 67108864 | bytes 1048576 | tf_op jit(solution)/shard_map/pallas_call | solution.py:365
  368.2 17.4 %collective-permute-done.20 = bf16[256,2048]{1,0:T(8,128)(2,1)S(1)} collective-permute-done((bf16[256,2048]{1,0:T(8,128)(2,1)S(1)}, bf16[256,2048]{1,0:T(8,128)(2,1)S(1)}, u32[]{:S(2)}, u32[]{:S(2)}) %collective-permute-start.20) | collective-permute-done | bytes 1048608 | tf_op jit(solution)/shard_map/ppermute | solution.py:572
  399.3 9.5 %convolution_convert_fusion.8 = bf16[2048,512]{1,0:T(8,128)(2,1)} fusion(bf16[2048,2048]{1,0:T(8,128)(2,1)} %all-gather.9.cloned.1.call-done.h, bf16[2048,512]{1,0:T(8,128)(2,1)S(1)} %copy-done.73), kind=kOutput, calls=%fused_computation.8 | convolution fusion | flops 4296015872 | bytes 12582912 | tf_op jit(solution)/shard_map/dot_general | solution.py:46
  412.0 10.6 %collective-permute-done.27.refs_2_ = bf16[256,2048]{1,0:T(8,128)(2,1)S(1)} collective-permute-done((bf16[256,2048]{1,0:T(8,128)(2,1)S(1)}, bf16[256,2048]{1,0:T(8,128)(2,1)S(1)}, u32[]{:S(2)}, u32[]{:S(2)}) %collective-permute-start.27) | collective-permute-done | bytes 1048608 | tf_op jit(solution)/shard_map/ppermute | solution.py:567
  442.8 38.5 %all-to-all-done.4.v = bf16[32,64,512]{2,1,0:T(8,128)(2,1)} async-done(((bf16[32,64,512]{2,1,0:T(8,128)(2,1)}), bf16[32,64,512]{2,1,0:T(8,128)(2,1)}, u32[]{:S(2)}, u32[]{:S(2)}) %all-to-all-start.4) | async-done | bytes 2097184 | tf_op jit(solution)/shard_map/all_to_all | solution.py:578
  481.3 19.3 %all-gather.11.cloned.1.call-done = bf16[2048,2048]{1,0:T(8,128)(2,1)} async-done(((bf16[256,2048]{1,0:T(8,128)(2,1)}), bf16[2048,2048]{1,0:T(8,128)(2,1)}) %all-gather.11.cloned.1.call-update) | async-done | bytes 8388624 | tf_op jit(solution)/shard_map/all_gather | solution.py:581
  508.0 6.7 %convolution_convert_fusion.12.dout = bf16[2048,128]{1,0:T(8,128)(2,1)} fusion(bf16[2048,2048]{1,0:T(8,128)(2,1)} %all-gather.11.cloned.1.call-done, bf16[128,2048]{1,0:T(8,128)(2,1)} %bitcast.58), kind=kOutput, calls=%fused_computation.12 | convolution fusion | flops 1074003968 | bytes 9437184 | tf_op jit(solution)/shard_map/dot_general | solution.py:42
  514.7 22.2 %shard_map.238 = (bf16[2048,384]{1,0:T(8,128)(2,1)}, bf16[2048,384]{1,0:T(8,128)(2,1)}) custom-call(s32[32]{0:T(128)} %add.177.offsets, bf16[2,2048,128]{2,1,0:T(8,128)(2,1)} %get-tuple-element.432.qe, bf16[2,2048,128]{2,1,0:T(8,128)(2,1)} %get-tuple-element.433.ke, bf16[2048,128]{1,0:T(8,128)(2,1)} %get-tuple-element.434.vs, ...), custom_call_target="tpu_custom_call" | custom-call | flops 67108864 | bytes 1048576 | tf_op jit(solution)/shard_map/pallas_call | solution.py:276
  543.3 9.1 %convolution_convert_fusion.10 = bf16[2048,384]{1,0:T(8,128)(2,1)} fusion(bf16[2048,2048]{1,0:T(8,128)(2,1)} %get-tuple-element.444, bf16[2048,384]{1,0:T(8,128)(2,1)S(1)} %copy-done.75), kind=kOutput, calls=%fused_computation.10 | convolution fusion | flops 3222011904 | bytes 11534336 | tf_op jit(solution)/shard_map/dot_general | solution.py:46
  576.3 5.9 convolution_convert_fusion.13
  585.5 6.0 collective-permute-done.35.refs_2_
  591.4 7.0 %collective-permute-done.36.refs_3_ = bf16[64,2048]{1,0:T(8,128)(2,1)S(1)} collective-permute-done((bf16[64,2048]{1,0:T(8,128)(2,1)S(1)}, bf16[64,2048]{1,0:T(8,128)(2,1)S(1)}, u32[]{:S(2)}, u32[]{:S(2)}) %collective-permute-start.36) | collective-permute-done | bytes 262176 | tf_op jit(solution)/shard_map/ppermute | solution.py:567
  631.5 5.0 shard_map.246
  (334 shorter events, 219.5 us)
Async XLA Ops:
  7.2 90.2 %all-gather.5.cloned.1.call-start = ((), (), s32[]{:S(2)}) async-start(), calls=%async_computation.7 | async-start | bytes 9437184 | tf_op jit(solution)/shard_map/all_gather | solution.py:581
  23.7 45.4 %all-to-all-start = ((bf16[32,64,384]{2,1,0:T(8,128)(2,1)}), bf16[32,64,384]{2,1,0:T(8,128)(2,1)}, u32[]{:S(2)}, u32[]{:S(2)}) async-start(bf16[32,64,384]{2,1,0:T(8,128)(2,1)} %shard_map.221), calls=%async_computation | async-start | bytes 3145728 | tf_op jit(solution)/shard_map/all_to_all | solution.py:578
  29.9 201.4 %all-gather.7.cloned.1.call-start = ((), (), s32[]{:S(2)}) async-start(), calls=%async_computation.8 | async-start | bytes 9437184 | tf_op jit(solution)/shard_map/all_gather | solution.py:581
  29.9 39.2 %collective-permute-start.1 = (bf16[128,2048]{1,0:T(8,128)(2,1)S(1)}, bf16[128,2048]{1,0:T(8,128)(2,1)S(1)}, u32[]{:S(2)}, u32[]{:S(2)}) collective-permute-start(bf16[128,2048]{1,0:T(8,128)(2,1)S(1)} %copy-done.70), channel_id=1, source_target_pairs={{0,8},{1,9},{2,10},{3,11},{4,12},{5,13},{6,14},{7,15},{8,0},{9,1},... | collective-permute-start | bytes 1572872 | tf_op jit(solution)/shard_map/ppermute | solution.py:567
  77.8 19.5 %collective-permute-start.2 = (bf16[64,2048]{1,0:T(8,128)(2,1)S(1)}, bf16[64,2048]{1,0:T(8,128)(2,1)S(1)}, u32[]{:S(2)}, u32[]{:S(2)}) collective-permute-start(bf16[64,2048]{1,0:T(8,128)(2,1)S(1)} %copy-done.72), channel_id=1, source_target_pairs={{0,16},{1,17},{2,18},{3,19},{4,20},{5,21},{6,22},{7,23},{8,24},{9,... | collective-permute-start | bytes 786440 | tf_op jit(solution)/shard_map/ppermute | solution.py:572
  84.7 54.3 %all-to-all-start.2 = ((bf16[32,64,512]{2,1,0:T(8,128)(2,1)}), bf16[32,64,512]{2,1,0:T(8,128)(2,1)}, u32[]{:S(2)}, u32[]{:S(2)}) async-start(bf16[32,64,512]{2,1,0:T(8,128)(2,1)} %shard_map.222), calls=%async_computation.2 | async-start | bytes 4194304 | tf_op jit(solution)/shard_map/all_to_all | solution.py:578
  88.2 207.7 %all-gather.9.cloned.1.call-start = ((), (), s32[]{:S(2)}) async-start(), calls=%async_computation.9 | async-start | bytes 9437184 | tf_op jit(solution)/shard_map/all_gather | solution.py:581
  144.9 34.1 %collective-permute-start.5 = (bf16[256,2048]{1,0:T(8,128)(2,1)S(1)}, bf16[256,2048]{1,0:T(8,128)(2,1)S(1)}, u32[]{:S(2)}, u32[]{:S(2)}) collective-permute-start(bf16[256,2048]{1,0:T(8,128)(2,1)S(1)} %get-tuple-element.305), channel_id=1, source_target_pairs={{0,4},{1,5},{2,6},{3,7},{4,0},{5,1},{6,2},{7,3},{8,12},{9,13},{10,... | collective-permute-start | bytes 3145736 | tf_op jit(solution)/shard_map/ppermute | solution.py:567
  146.3 32.8 %collective-permute-start.6 = (bf16[256,2048]{1,0:T(8,128)(2,1)S(1)}, bf16[256,2048]{1,0:T(8,128)(2,1)S(1)}, u32[]{:S(2)}, u32[]{:S(2)}) collective-permute-start(bf16[256,2048]{1,0:T(8,128)(2,1)S(1)} %get-tuple-element.307), channel_id=1, source_target_pairs={{0,2},{1,3},{2,0},{3,1},{4,6},{5,7},{6,4},{7,5},{8,10},{9,11},{10,... | collective-permute-start | bytes 3145736 | tf_op jit(solution)/shard_map/ppermute | solution.py:567
  147.8 48.0 %collective-permute-start.9 = (bf16[256,2048]{1,0:T(8,128)(2,1)S(1)}, bf16[256,2048]{1,0:T(8,128)(2,1)S(1)}, u32[]{:S(2)}, u32[]{:S(2)}) collective-permute-start(bf16[256,2048]{1,0:T(8,128)(2,1)S(1)} %copy-done.66), channel_id=1, source_target_pairs={{0,16},{1,17},{2,18},{3,19},{4,20},{5,21},{6,22},{7,23},{8,24},{9,... | collective-permute-start | bytes 3145736 | tf_op jit(solution)/shard_map/ppermute | solution.py:572
  199.2 21.3 %collective-permute-start.13 = (bf16[64,2048]{1,0:T(8,128)(2,1)S(1)}, bf16[64,2048]{1,0:T(8,128)(2,1)S(1)}, u32[]{:S(2)}, u32[]{:S(2)}) collective-permute-start(bf16[64,2048]{1,0:T(8,128)(2,1)S(1)} %get-tuple-element.330), channel_id=1, source_target_pairs={{0,8},{1,9},{2,10},{3,11},{4,12},{5,13},{6,14},{7,15},{8,0},{9,1},... | collective-permute-start | bytes 786440 | tf_op jit(solution)/shard_map/ppermute | solution.py:567
  222.4 54.2 %all-to-all-start.3 = ((bf16[32,64,512]{2,1,0:T(8,128)(2,1)}), bf16[32,64,512]{2,1,0:T(8,128)(2,1)}, u32[]{:S(2)}, u32[]{:S(2)}) async-start(bf16[32,64,512]{2,1,0:T(8,128)(2,1)} %copy-done.3), calls=%async_computation.3 | async-start | bytes 4194304 | tf_op jit(solution)/shard_map/all_to_all | solution.py:578
  227.5 273.1 %all-gather.11.cloned.1.call-start = ((), (), s32[]{:S(2)}) async-start(), calls=%async_computation.10 | async-start | bytes 9437184 | tf_op jit(solution)/shard_map/all_gather | solution.py:581
  335.2 25.4 %collective-permute-start.16 = (bf16[256,2048]{1,0:T(8,128)(2,1)S(1)}, bf16[256,2048]{1,0:T(8,128)(2,1)S(1)}, u32[]{:S(2)}, u32[]{:S(2)}) collective-permute-start(bf16[256,2048]{1,0:T(8,128)(2,1)S(1)} %get-tuple-element.365), channel_id=1, source_target_pairs={{0,4},{1,5},{2,6},{3,7},{4,0},{5,1},{6,2},{7,3},{8,12},{9,13},{10,... | collective-permute-start | bytes 3145736 | tf_op jit(solution)/shard_map/ppermute | solution.py:567
  335.7 25.0 %collective-permute-start.17 = (bf16[256,2048]{1,0:T(8,128)(2,1)S(1)}, bf16[256,2048]{1,0:T(8,128)(2,1)S(1)}, u32[]{:S(2)}, u32[]{:S(2)}) collective-permute-start(bf16[256,2048]{1,0:T(8,128)(2,1)S(1)} %get-tuple-element.367), channel_id=1, source_target_pairs={{0,2},{1,3},{2,0},{3,1},{4,6},{5,7},{6,4},{7,5},{8,10},{9,11},{10,... | collective-permute-start | bytes 3145736 | tf_op jit(solution)/shard_map/ppermute | solution.py:567
  337.4 48.1 %collective-permute-start.20 = (bf16[256,2048]{1,0:T(8,128)(2,1)S(1)}, bf16[256,2048]{1,0:T(8,128)(2,1)S(1)}, u32[]{:S(2)}, u32[]{:S(2)}) collective-permute-start(bf16[256,2048]{1,0:T(8,128)(2,1)S(1)} %convolution_convert_fusion.11), channel_id=1, source_target_pairs={{0,16},{1,17},{2,18},{3,19},{4,20},{5,21},{6,22},{7,23},{8,24},{9,... | collective-permute-start | bytes 3145736 | tf_op jit(solution)/shard_map/ppermute | solution.py:572
  361.8 23.7 %collective-permute-start.18 = (bf16[128,2048]{1,0:T(8,128)(2,1)S(1)}, bf16[128,2048]{1,0:T(8,128)(2,1)S(1)}, u32[]{:S(2)}, u32[]{:S(2)}) collective-permute-start(bf16[128,2048]{1,0:T(8,128)(2,1)S(1)} %get-tuple-element.381), channel_id=1, source_target_pairs={{0,2},{1,3},{2,0},{3,1},{4,6},{5,7},{6,4},{7,5},{8,10},{9,11},{10,... | collective-permute-start | bytes 1572872 | tf_op jit(solution)/shard_map/ppermute | solution.py:567
  363.6 22.0 %collective-permute-start.19 = (bf16[128,2048]{1,0:T(8,128)(2,1)S(1)}, bf16[128,2048]{1,0:T(8,128)(2,1)S(1)}, u32[]{:S(2)}, u32[]{:S(2)}) collective-permute-start(bf16[128,2048]{1,0:T(8,128)(2,1)S(1)} %get-tuple-element.383), channel_id=1, source_target_pairs={{0,4},{1,5},{2,6},{3,7},{4,0},{5,1},{6,2},{7,3},{8,12},{9,13},{10,... | collective-permute-start | bytes 1572872 | tf_op jit(solution)/shard_map/ppermute | solution.py:567
  387.3 21.6 %collective-permute-start.24 = (bf16[64,2048]{1,0:T(8,128)(2,1)S(1)}, bf16[64,2048]{1,0:T(8,128)(2,1)S(1)}, u32[]{:S(2)}, u32[]{:S(2)}) collective-permute-start(bf16[64,2048]{1,0:T(8,128)(2,1)S(1)} %get-tuple-element.400.refs_5_), channel_id=1, source_target_pairs={{0,8},{1,9},{2,10},{3,11},{4,12},{5,13},{6,14},{7,15},{8,0},{9,1},... | collective-permute-start | bytes 786440 | tf_op jit(solution)/shard_map/ppermute | solution.py:567
  389.3 19.6 %collective-permute-start.25 = (bf16[64,2048]{1,0:T(8,128)(2,1)S(1)}, bf16[64,2048]{1,0:T(8,128)(2,1)S(1)}, u32[]{:S(2)}, u32[]{:S(2)}) collective-permute-start(bf16[64,2048]{1,0:T(8,128)(2,1)S(1)} %get-tuple-element.402), channel_id=1, source_target_pairs={{0,8},{1,9},{2,10},{3,11},{4,12},{5,13},{6,14},{7,15},{8,0},{9,1},... | collective-permute-start | bytes 786440 | tf_op jit(solution)/shard_map/ppermute | solution.py:567
  389.8 22.2 %collective-permute-start.26 = (bf16[64,2048]{1,0:T(8,128)(2,1)S(1)}, bf16[64,2048]{1,0:T(8,128)(2,1)S(1)}, u32[]{:S(2)}, u32[]{:S(2)}) collective-permute-start(bf16[64,2048]{1,0:T(8,128)(2,1)S(1)} %get-tuple-element.404), channel_id=1, source_target_pairs={{0,8},{1,9},{2,10},{3,11},{4,12},{5,13},{6,14},{7,15},{8,0},{9,1},... | collective-permute-start | bytes 786440 | tf_op jit(solution)/shard_map/ppermute | solution.py:567
  397.4 25.2 %collective-permute-start.27 = (bf16[256,2048]{1,0:T(8,128)(2,1)S(1)}, bf16[256,2048]{1,0:T(8,128)(2,1)S(1)}, u32[]{:S(2)}, u32[]{:S(2)}) collective-permute-start(bf16[256,2048]{1,0:T(8,128)(2,1)S(1)} %get-tuple-element.410), channel_id=1, source_target_pairs={{0,4},{1,5},{2,6},{3,7},{4,0},{5,1},{6,2},{7,3},{8,12},{9,13},{10,... | collective-permute-start | bytes 3145736 | tf_op jit(solution)/shard_map/ppermute | solution.py:567
  398.2 25.4 %collective-permute-start.28 = (bf16[256,2048]{1,0:T(8,128)(2,1)S(1)}, bf16[256,2048]{1,0:T(8,128)(2,1)S(1)}, u32[]{:S(2)}, u32[]{:S(2)}) collective-permute-start(bf16[256,2048]{1,0:T(8,128)(2,1)S(1)} %get-tuple-element.412), channel_id=1, source_target_pairs={{0,2},{1,3},{2,0},{3,1},{4,6},{5,7},{6,4},{7,5},{8,10},{9,11},{10,... | collective-permute-start | bytes 3145736 | tf_op jit(solution)/shard_map/ppermute | solution.py:567
  428.4 52.9 %all-to-all-start.4 = ((bf16[32,64,512]{2,1,0:T(8,128)(2,1)}), bf16[32,64,512]{2,1,0:T(8,128)(2,1)}, u32[]{:S(2)}, u32[]{:S(2)}) async-start(bf16[32,64,512]{2,1,0:T(8,128)(2,1)} %bitcast.60), calls=%async_computation.4 | async-start | bytes 4194304 | tf_op jit(solution)/shard_map/all_to_all | solution.py:578
  500.6 54.5 %all-to-all-start.5 = ((bf16[32,64,512]{2,1,0:T(8,128)(2,1)}), bf16[32,64,512]{2,1,0:T(8,128)(2,1)}, u32[]{:S(2)}, u32[]{:S(2)}) async-start(bf16[32,64,512]{2,1,0:T(8,128)(2,1)} %bitcast.61), calls=%async_computation.5 | async-start | bytes 4194304 | tf_op jit(solution)/shard_map/all_to_all | solution.py:578
  504.8 37.9 %collective-permute-start.29 = (bf16[128,2048]{1,0:T(8,128)(2,1)}, bf16[128,2048]{1,0:T(8,128)(2,1)S(1)}, u32[]{:S(2)}, u32[]{:S(2)}) collective-permute-start(bf16[128,2048]{1,0:T(8,128)(2,1)} %copy-done.59), channel_id=1, source_target_pairs={{0,2},{1,3},{2,0},{3,1},{4,6},{5,7},{6,4},{7,5},{8,10},{9,11},{10,... | collective-permute-start | bytes 1572872 | tf_op jit(solution)/shard_map/ppermute | solution.py:567
  506.6 36.2 %collective-permute-start.30 = (bf16[128,2048]{1,0:T(8,128)(2,1)}, bf16[128,2048]{1,0:T(8,128)(2,1)S(1)}, u32[]{:S(2)}, u32[]{:S(2)}) collective-permute-start(bf16[128,2048]{1,0:T(8,128)(2,1)} %copy-done.58), channel_id=1, source_target_pairs={{0,4},{1,5},{2,6},{3,7},{4,0},{5,1},{6,2},{7,3},{8,12},{9,13},{10,... | collective-permute-start | bytes 1572872 | tf_op jit(solution)/shard_map/ppermute | solution.py:567
  555.1 65.1 %all-to-all-start.6 = ((bf16[32,64,384]{2,1,0:T(8,128)(2,1)}), bf16[32,64,384]{2,1,0:T(8,128)(2,1)}, u32[]{:S(2)}, u32[]{:S(2)}) async-start(bf16[32,64,384]{2,1,0:T(8,128)(2,1)} %bitcast.62), calls=%async_computation.6 | async-start | bytes 3145728 | tf_op jit(solution)/shard_map/all_to_all | solution.py:578
  567.3 35.5 %collective-permute-start.33 = (bf16[256,2048]{1,0:T(8,128)(2,1)S(1)}, bf16[256,2048]{1,0:T(8,128)(2,1)S(1)}, u32[]{:S(2)}, u32[]{:S(2)}) collective-permute-start(bf16[256,2048]{1,0:T(8,128)(2,1)S(1)} %get-tuple-element.458), channel_id=1, source_target_pairs={{0,4},{1,5},{2,6},{3,7},{4,0},{5,1},{6,2},{7,3},{8,12},{9,13},{10,... | collective-permute-start | bytes 3145736 | tf_op jit(solution)/shard_map/ppermute | solution.py:567
  569.2 33.6 %collective-permute-start.34 = (bf16[256,2048]{1,0:T(8,128)(2,1)S(1)}, bf16[256,2048]{1,0:T(8,128)(2,1)S(1)}, u32[]{:S(2)}, u32[]{:S(2)}) collective-permute-start(bf16[256,2048]{1,0:T(8,128)(2,1)S(1)} %get-tuple-element.460), channel_id=1, source_target_pairs={{0,2},{1,3},{2,0},{3,1},{4,6},{5,7},{6,4},{7,5},{8,10},{9,11},{10,... | collective-permute-start | bytes 3145736 | tf_op jit(solution)/shard_map/ppermute | solution.py:567
  575.7 22.8 %collective-permute-start.36 = (bf16[64,2048]{1,0:T(8,128)(2,1)S(1)}, bf16[64,2048]{1,0:T(8,128)(2,1)S(1)}, u32[]{:S(2)}, u32[]{:S(2)}) collective-permute-start(bf16[64,2048]{1,0:T(8,128)(2,1)S(1)} %get-tuple-element.468), channel_id=1, source_target_pairs={{0,8},{1,9},{2,10},{3,11},{4,12},{5,13},{6,14},{7,15},{8,0},{9,1},... | collective-permute-start | bytes 786440 | tf_op jit(solution)/shard_map/ppermute | solution.py:567
  611.3 25.2 %collective-permute-start.41 = (bf16[64,2048]{1,0:T(8,128)(2,1)}, bf16[64,2048]{1,0:T(8,128)(2,1)}, u32[]{:S(2)}, u32[]{:S(2)}) collective-permute-start(bf16[64,2048]{1,0:T(8,128)(2,1)} %convolution_convert_fusion.13), channel_id=1, source_target_pairs={{0,16},{1,17},{2,18},{3,19},{4,20},{5,21},{6,22},{7,23},{8,24},{9,... | collective-permute-start | bytes 786440 | tf_op jit(solution)/shard_map/ppermute | solution.py:572
  (105 other events, 939.7 us)
Sparse Core Ops, SparseCore 0:
  23.9 67.9 all-gather.4
  93.7 73.3 all-gather.6
  222.5 73.2 all-gather.8
  428.5 72.0 all-gather.10

commit v7 on v6

--- a/solution.py
+++ b/solution.py
@@ -143,10 +143,11 @@
     each_block(size, place)
     shape = (BLOCK, LANES)
     diagonal = lax.broadcasted_iota(jnp.int32, (BLOCK, BLOCK), 0) >= lane_index((BLOCK, BLOCK))
+    lane = lane_index(shape)
     for i in range(SEQ // BLOCK):
         mine = slice(i * BLOCK, (i + 1) * BLOCK)
-        outs = []
-        for head in range(2):
+
+        def one_head(head, carry):
             spare = (1 - head) * HEAD_DIM
             query = qe[head, mine, :]
             scores = []
@@ -161,11 +162,14 @@
                 value = vs[j * BLOCK : (j + 1) * BLOCK, :]
                 value = jnp.where(of_head(head, shape), value, jnp.ones((), BF))
                 total += matmul(probs, value)
-            weight = total[:, spare : spare + 1]
-            outs.append(total / weight)
+            weight = jnp.sum(jnp.where(lane == spare, total, 0.0), axis=1, keepdims=True)
+            before = jnp.where(head == 0, 0.0, out32[mine, :])
+            out32[mine, :] = jnp.where(of_head(head, shape), total / weight, before)
             logsum = top + jnp.log(weight)
             qe[head, mine, :] = query + in_lanes(parts_of(-logsum), spare + HALF, shape)
-        out32[mine, :] = jnp.where(of_head(0, shape), outs[0], outs[1])
+            return carry
+
+        lax.fori_loop(0, 2, one_head, 0)
 
     def send(there, here):
         out[here, :] = out32[there, :].astype(BF)
@@ -269,6 +273,7 @@
         ],
         [IN_SMEM] + [IN_VMEM] * 5,
         [IN_VMEM] * 6,
+        vmem=48,
     )(offsets, qkv, cosine, sine, q_mask, k_mask)
 
 
@@ -852,7 +857,7 @@
 
     add_dh2 = Transfer(team.scatter(sent, kept, True))
     start(add_dh2)
-    send_down = across(team.add, mixed, dy, [16])
+    send_down = across(team.add, mixed, dy, [14, 2])
     wait([add_dh2])
     start(add_dh2, send_down)
     grad_gate = t_times(h2, dgate).astype(BF)
@@ -871,8 +876,8 @@
     get_da = Transfer(team.one(da, team.gather))
     send_gate = Transfer(team.owners(grad_gate))
     send_up = Transfer(team.owners(grad_up))
-    start(get_da, send_gate)
-    clock.ready(add_result, [get_da, send_gate])
+    start(get_da, send_gate, send_down)
+    clock.ready(add_result, [get_da, send_gate, send_down])
     da = get_da.value
     start(send_up, add_result)
     dout = times_t(da, out_rows).astype(BF)

time: 664 us -> 660 us (level)
  local copies, waits for them, and re-layouts: 47.1 us -> 38.5 us
    all_to_all x7, waiting for transfers between devices: 82.8 us -> 44.8 us  [everywhere(): return lax.all_to_all(v, 'fsdp', 0, 0, tiled=True)]
    ppermute x4 -> x5, waiting for transfers between devices: 30.9 us -> 63.2 us  [ahead(): return lambda v: lax.ppermute(v, 'fsdp', pairs)]
    ppermute x38, waiting for transfers between devices: 135 us -> 151 us  [flip(): return lambda v: lax.ppermute(v, 'fsdp', pairs)]
    unnamed x169 -> x185, local copies, waits for them, and re-layouts: 41.1 us -> 35.3 us
  transfers between devices with their start and end apart: 53 -> 54, of which waited for: 29 -> 30; matrix products, arithmetic and copies ran while one was open for 16% -> 15% of each run, Pallas kernels for 14% -> 14%
where the time goes in v7:
time: 660 us; the launch traced here: 652 us
  waiting for transfers between devices  293 us (44%)
  Pallas kernels  127 us (19%)
  starting transfers between devices  82.3 us (12%)
  matrix products  80.3 us (12%)
  local copies, waits for them, and re-layouts  38.5 us (6%)
  other arithmetic  15.6 us (2%)
  between operations  15 us (2%)
    ppermute x38, waiting for transfers between devices, flip(): return lambda v: lax.ppermute(v, 'fsdp', pairs)  151 us
    ppermute x5, waiting for transfers between devices, ahead(): return lambda v: lax.ppermute(v, 'fsdp', pairs)  63.2 us
    all_to_all x7, waiting for transfers between devices, everywhere(): return lax.all_to_all(v, 'fsdp', 0, 0, tiled=True)  44.8 us
    dot_general x7, matrix products, t_times(): lax.dot_general(left, right, (((0,), (0,)), ((), ())), preferred_element_...  42.6 us
    ppermute x38, starting transfers between devices, flip(): return lambda v: lax.ppermute(v, 'fsdp', pairs)  38.6 us
    unnamed x185, local copies, waits for them, and re-layouts  35.3 us
    all_gather x4, waiting for transfers between devices, gather(): lax.all_gather(v, 'fsdp', axis=0, tiled=True, axis_index_groups=self.halves)  33.6 us
    all_to_all x7, starting transfers between devices, everywhere(): return lax.all_to_all(v, 'fsdp', 0, 0, tiled=True)  31.4 us
  transfers between devices with their start and end apart: 54, of which 30 were waited for; matrix products, arithmetic and copies ran while one was open for 15% of the time, Pallas kernels for 14%

profile of v7, /device:TPU:0, one launch (start us, length us, event | category | flops | bytes accessed | tf_op | source)
XLA Modules:
  0.0 652.1 jit_solution(13636835927433747310)
XLA Ops:
  15.2 7.3 %collective-permute-done = bf16[128,2048]{1,0:T(8,128)(2,1)S(1)} collective-permute-done((bf16[128,2048]{1,0:T(8,128)(2,1)}, bf16[128,2048]{1,0:T(8,128)(2,1)S(1)}, u32[]{:S(2)}, u32[]{:S(2)}) %collective-permute-start) | collective-permute-done | bytes 524320 | tf_op jit(solution)/shard_map/ppermute | solution.py:572
  23.7 6.1 all-to-all-start
  34.7 34.4 %collective-permute-done.1 = bf16[128,2048]{1,0:T(8,128)(2,1)S(1)} collective-permute-done((bf16[128,2048]{1,0:T(8,128)(2,1)S(1)}, bf16[128,2048]{1,0:T(8,128)(2,1)S(1)}, u32[]{:S(2)}, u32[]{:S(2)}) %collective-permute-start.1) | collective-permute-done | bytes 524320 | tf_op jit(solution)/shard_map/ppermute | solution.py:572
  95.8 10.5 %shard_map.224 = (bf16[2048,2048]{1,0:T(8,128)(2,1)}, f32[2048,384]{1,0:T(8,128)}) custom-call(bf16[2048,2048]{1,0:T(8,128)(2,1)} %all-gather.5.cloned.1.call-done.x, f32[1,2048]{1,0:T(1,128)} %reshape.214.gain, bf16[2048,384]{1,0:T(8,128)(2,1)} %bitcast.5.w), custom_call_target="tpu_custom_call" | custom-call | flops 67108864 | bytes 1048576 | tf_op jit(solution)/shard_map/pallas_call | solution.py:304
  106.3 18.7 %shard_map.225 = (bf16[2,2048,128]{2,1,0:T(8,128)(2,1)S(1)}, bf16[2,2048,128]{2,1,0:T(8,128)(2,1)S(1)}, bf16[2048,128]{1,0:T(8,128)(2,1)S(1)}, bf16[2048,128]{1,...) custom-call(s32[32]{0:T(128)S(1)} %add.177.offsets, f32[2048,384]{1,0:T(8,128)} %get-tuple-element.287.qkv, ...), custom_call_target="tpu_custom_call" | custom-call | flops 67108864 | bytes 1048576 | tf_op jit(solution)/shard_map/pallas_call | solution.py:264
  150.9 27.6 %collective-permute-done.5.refs_2_ = bf16[256,2048]{1,0:T(8,128)(2,1)S(1)} collective-permute-done((bf16[256,2048]{1,0:T(8,128)(2,1)S(1)}, bf16[256,2048]{1,0:T(8,128)(2,1)S(1)}, u32[]{:S(2)}, u32[]{:S(2)}) %collective-permute-start.5) | collective-permute-done | bytes 1048608 | tf_op jit(solution)/shard_map/ppermute | solution.py:572
  181.8 14.9 %collective-permute-done.9 = bf16[256,2048]{1,0:T(8,128)(2,1)S(1)} collective-permute-done((bf16[256,2048]{1,0:T(8,128)(2,1)S(1)}, bf16[256,2048]{1,0:T(8,128)(2,1)S(1)}, u32[]{:S(2)}, u32[]{:S(2)}) %collective-permute-start.9) | collective-permute-done | bytes 1048608 | tf_op jit(solution)/shard_map/ppermute | solution.py:577
  202.4 5.2 collective-permute-done.10.refs_2_
  207.6 5.6 collective-permute-done.11.refs_3_
  213.2 5.6 collective-permute-done.12.refs_6_
  232.2 10.9 %fusion.25.dm = f32[2048,512]{1,0:T(8,128)} fusion(bf16[2048,2048]{1,0:T(8,128)(2,1)} %all-gather.7.cloned.1.call-done, bf16[512,2048]{1,0:T(8,128)(2,1)S(1)} %bitcast.51), kind=kOutput, calls=%fused_computation.77 | convolution fusion | flops 4294967296 | bytes 14680064 | tf_op jit(solution)/shard_map/dot_general | solution.py:42
  243.1 36.4 %all-to-all-done.3 = bf16[32,64,512]{2,1,0:T(8,128)(2,1)} async-done(((bf16[32,64,512]{2,1,0:T(8,128)(2,1)}), bf16[32,64,512]{2,1,0:T(8,128)(2,1)}, u32[]{:S(2)}, u32[]{:S(2)}) %all-to-all-start.3) | async-done | bytes 2097184 | tf_op jit(solution)/shard_map/all_to_all | solution.py:583
  279.5 19.3 %all-gather.9.cloned.1.call-done.h = bf16[2048,2048]{1,0:T(8,128)(2,1)} async-done(((bf16[256,2048]{1,0:T(8,128)(2,1)}), bf16[2048,2048]{1,0:T(8,128)(2,1)}) %all-gather.9.cloned.1.call-update) | async-done | bytes 8388624 | tf_op jit(solution)/shard_map/all_gather | solution.py:586
  298.7 27.1 %shard_map.230 = (bf16[2048,512]{1,0:T(8,128)(2,1)}, bf16[2048,512]{1,0:T(8,128)(2,1)}, bf16[2048,512]{1,0:T(8,128)(2,1)}, bf16[512,2048]{1,0:T(8,128)(2,1)}, bf...) custom-call(s32[17]{0:T(128)} %pad_add_fusion.1.spots, ...), custom_call_target="tpu_custom_call" | custom-call | flops 67108864 | bytes 1048576 | tf_op jit(solution)/shard_map/pallas_call | solution.py:350
  326.5 6.2 convolution_convert_fusion.11
  341.6 5.7 convolution_convert_fusion.9
  347.3 15.7 %collective-permute-done.16.refs_2_ = bf16[256,2048]{1,0:T(8,128)(2,1)S(1)} collective-permute-done((bf16[256,2048]{1,0:T(8,128)(2,1)S(1)}, bf16[256,2048]{1,0:T(8,128)(2,1)S(1)}, u32[]{:S(2)}, u32[]{:S(2)}) %collective-permute-start.16) | collective-permute-done | bytes 1048608 | tf_op jit(solution)/shard_map/ppermute | solution.py:572
  366.8 6.1 shard_map.232
  373.0 9.4 %collective-permute-done.20 = bf16[224,2048]{1,0:T(8,128)(2,1)S(1)} collective-permute-done((bf16[224,2048]{1,0:T(8,128)(2,1)S(1)}, bf16[224,2048]{1,0:T(8,128)(2,1)S(1)}, u32[]{:S(2)}, u32[]{:S(2)}) %collective-permute-start.20) | collective-permute-done | bytes 917536 | tf_op jit(solution)/shard_map/ppermute | solution.py:577
  396.2 5.7 convolution_convert_fusion.8
  408.8 10.6 %collective-permute-done.27.refs_2_ = bf16[256,2048]{1,0:T(8,128)(2,1)S(1)} collective-permute-done((bf16[256,2048]{1,0:T(8,128)(2,1)S(1)}, bf16[256,2048]{1,0:T(8,128)(2,1)S(1)}, u32[]{:S(2)}, u32[]{:S(2)}) %collective-permute-start.27) | collective-permute-done | bytes 1048608 | tf_op jit(solution)/shard_map/ppermute | solution.py:572
  432.8 7.4 %fusion = f32[256,2048]{1,0:T(8,128)} fusion(bf16[2048,2048]{1,0:T(8,128)(2,1)} %all-gather.7.cloned.1.call-done, bf16[2048,512]{1,0:T(8,128)(2,1)S(1)} %copy-done.2, s32[]{:T(128)S(6)} %select_n.196), kind=kOutput, calls=%fused_computation.23 | convolution fusion | flops 2147483648 | bytes 11534340 | tf_op jit(solution)/shard_map/dot_general | solution.py:46
  444.8 39.0 %collective-permute-done.29 = bf16[32,2048]{1,0:T(8,128)(2,1)S(1)} collective-permute-done((bf16[32,2048]{1,0:T(8,128)(2,1)S(1)}, bf16[32,2048]{1,0:T(8,128)(2,1)S(1)}, u32[]{:S(2)}, u32[]{:S(2)}) %collective-permute-start.29) | collective-permute-done | bytes 131104 | tf_op jit(solution)/shard_map/ppermute | solution.py:577
  483.8 14.3 %all-gather.11.cloned.1.call-done = bf16[2048,2048]{1,0:T(8,128)(2,1)} async-done(((bf16[256,2048]{1,0:T(8,128)(2,1)}), bf16[2048,2048]{1,0:T(8,128)(2,1)}) %all-gather.11.cloned.1.call-update) | async-done | bytes 8388624 | tf_op jit(solution)/shard_map/all_gather | solution.py:586
  505.6 6.7 %convolution_convert_fusion.12.dout = bf16[2048,128]{1,0:T(8,128)(2,1)} fusion(bf16[2048,2048]{1,0:T(8,128)(2,1)} %all-gather.11.cloned.1.call-done, bf16[128,2048]{1,0:T(8,128)(2,1)} %bitcast.58), kind=kOutput, calls=%fused_computation.12 | convolution fusion | flops 1074003968 | bytes 9437184 | tf_op jit(solution)/shard_map/dot_general | solution.py:42
  512.3 22.5 %shard_map.238 = (bf16[2048,384]{1,0:T(8,128)(2,1)}, bf16[2048,384]{1,0:T(8,128)(2,1)}) custom-call(s32[32]{0:T(128)} %copy-done.66, bf16[2,2048,128]{2,1,0:T(8,128)(2,1)} %copy-done.28, bf16[2,2048,128]{2,1,0:T(8,128)(2,1)} %copy-done.29, bf16[2048,128]{1,0:T(8,128)(2,1)} %copy-done.48, f32[2048,128]{1,0:T(8,128)} %copy-done.30, ...), custom_call_target="tpu_custom_call" | custom-call | flops 67108864 | bytes 1048576 | tf_op jit(solution)/shard_map/pallas_call | solution.py:281
  541.2 9.2 %convolution_convert_fusion.10 = bf16[2048,384]{1,0:T(8,128)(2,1)} fusion(bf16[2048,2048]{1,0:T(8,128)(2,1)} %get-tuple-element.447, bf16[2048,384]{1,0:T(8,128)(2,1)S(1)} %copy-done.85), kind=kOutput, calls=%fused_computation.10 | convolution fusion | flops 3222011904 | bytes 11534336 | tf_op jit(solution)/shard_map/dot_general | solution.py:46
  574.1 5.9 convolution_convert_fusion.13
  583.3 6.0 collective-permute-done.36.refs_2_
  589.3 7.0 %collective-permute-done.37.refs_3_ = bf16[64,2048]{1,0:T(8,128)(2,1)S(1)} collective-permute-done((bf16[64,2048]{1,0:T(8,128)(2,1)S(1)}, bf16[64,2048]{1,0:T(8,128)(2,1)S(1)}, u32[]{:S(2)}, u32[]{:S(2)}) %collective-permute-start.37) | collective-permute-done | bytes 262176 | tf_op jit(solution)/shard_map/ppermute | solution.py:572
  611.3 5.2 collective-permute-done.38.refs_2_
  628.1 5.0 shard_map.246
  (353 shorter events, 219.9 us)
Async XLA Ops:
  7.2 88.6 %all-gather.5.cloned.1.call-start = ((), (), s32[]{:S(2)}) async-start(), calls=%async_computation.7 | async-start | bytes 9437184 | tf_op jit(solution)/shard_map/all_gather | solution.py:586
  23.7 45.4 %all-to-all-start = ((bf16[32,64,384]{2,1,0:T(8,128)(2,1)}), bf16[32,64,384]{2,1,0:T(8,128)(2,1)}, u32[]{:S(2)}, u32[]{:S(2)}) async-start(bf16[32,64,384]{2,1,0:T(8,128)(2,1)} %shard_map.221), calls=%async_computation | async-start | bytes 3145728 | tf_op jit(solution)/shard_map/all_to_all | solution.py:583
  29.9 202.3 %all-gather.7.cloned.1.call-start = ((), (), s32[]{:S(2)}) async-start(), calls=%async_computation.8 | async-start | bytes 9437184 | tf_op jit(solution)/shard_map/all_gather | solution.py:586
  29.9 39.2 %collective-permute-start.1 = (bf16[128,2048]{1,0:T(8,128)(2,1)S(1)}, bf16[128,2048]{1,0:T(8,128)(2,1)S(1)}, u32[]{:S(2)}, u32[]{:S(2)}) collective-permute-start(bf16[128,2048]{1,0:T(8,128)(2,1)S(1)} %copy-done.81), channel_id=1, source_target_pairs={{0,8},{1,9},{2,10},{3,11},{4,12},{5,13},{6,14},{7,15},{8,0},{9,1},... | collective-permute-start | bytes 1572872 | tf_op jit(solution)/shard_map/ppermute | solution.py:572
  77.3 18.5 %collective-permute-start.2 = (bf16[64,2048]{1,0:T(8,128)(2,1)S(1)}, bf16[64,2048]{1,0:T(8,128)(2,1)S(1)}, u32[]{:S(2)}, u32[]{:S(2)}) collective-permute-start(bf16[64,2048]{1,0:T(8,128)(2,1)S(1)} %copy-done.82), channel_id=1, source_target_pairs={{0,16},{1,17},{2,18},{3,19},{4,20},{5,21},{6,22},{7,23},{8,24},{9,... | collective-permute-start | bytes 786440 | tf_op jit(solution)/shard_map/ppermute | solution.py:577
  84.1 54.3 %all-to-all-start.2 = ((bf16[32,64,512]{2,1,0:T(8,128)(2,1)}), bf16[32,64,512]{2,1,0:T(8,128)(2,1)}, u32[]{:S(2)}, u32[]{:S(2)}) async-start(bf16[32,64,512]{2,1,0:T(8,128)(2,1)} %shard_map.222), calls=%async_computation.2 | async-start | bytes 4194304 | tf_op jit(solution)/shard_map/all_to_all | solution.py:583
  87.6 211.1 %all-gather.9.cloned.1.call-start = ((), (), s32[]{:S(2)}) async-start(), calls=%async_computation.9 | async-start | bytes 9437184 | tf_op jit(solution)/shard_map/all_gather | solution.py:586
  145.1 33.4 %collective-permute-start.5 = (bf16[256,2048]{1,0:T(8,128)(2,1)S(1)}, bf16[256,2048]{1,0:T(8,128)(2,1)S(1)}, u32[]{:S(2)}, u32[]{:S(2)}) collective-permute-start(bf16[256,2048]{1,0:T(8,128)(2,1)S(1)} %get-tuple-element.307), channel_id=1, source_target_pairs={{0,4},{1,5},{2,6},{3,7},{4,0},{5,1},{6,2},{7,3},{8,12},{9,13},{10,... | collective-permute-start | bytes 3145736 | tf_op jit(solution)/shard_map/ppermute | solution.py:572
  147.0 31.6 %collective-permute-start.6 = (bf16[256,2048]{1,0:T(8,128)(2,1)S(1)}, bf16[256,2048]{1,0:T(8,128)(2,1)S(1)}, u32[]{:S(2)}, u32[]{:S(2)}) collective-permute-start(bf16[256,2048]{1,0:T(8,128)(2,1)S(1)} %get-tuple-element.309), channel_id=1, source_target_pairs={{0,2},{1,3},{2,0},{3,1},{4,6},{5,7},{6,4},{7,5},{8,10},{9,11},{10,... | collective-permute-start | bytes 3145736 | tf_op jit(solution)/shard_map/ppermute | solution.py:572
  148.5 48.2 %collective-permute-start.9 = (bf16[256,2048]{1,0:T(8,128)(2,1)S(1)}, bf16[256,2048]{1,0:T(8,128)(2,1)S(1)}, u32[]{:S(2)}, u32[]{:S(2)}) collective-permute-start(bf16[256,2048]{1,0:T(8,128)(2,1)S(1)} %copy-done.75), channel_id=1, source_target_pairs={{0,16},{1,17},{2,18},{3,19},{4,20},{5,21},{6,22},{7,23},{8,24},{9,... | collective-permute-start | bytes 3145736 | tf_op jit(solution)/shard_map/ppermute | solution.py:577
  200.4 18.5 %collective-permute-start.12 = (bf16[64,2048]{1,0:T(8,128)(2,1)S(1)}, bf16[64,2048]{1,0:T(8,128)(2,1)S(1)}, u32[]{:S(2)}, u32[]{:S(2)}) collective-permute-start(bf16[64,2048]{1,0:T(8,128)(2,1)S(1)} %get-tuple-element.330), channel_id=1, source_target_pairs={{0,8},{1,9},{2,10},{3,11},{4,12},{5,13},{6,14},{7,15},{8,0},{9,1},... | collective-permute-start | bytes 786440 | tf_op jit(solution)/shard_map/ppermute | solution.py:572
  200.8 21.4 %collective-permute-start.13 = (bf16[64,2048]{1,0:T(8,128)(2,1)S(1)}, bf16[64,2048]{1,0:T(8,128)(2,1)S(1)}, u32[]{:S(2)}, u32[]{:S(2)}) collective-permute-start(bf16[64,2048]{1,0:T(8,128)(2,1)S(1)} %get-tuple-element.332), channel_id=1, source_target_pairs={{0,8},{1,9},{2,10},{3,11},{4,12},{5,13},{6,14},{7,15},{8,0},{9,1},... | collective-permute-start | bytes 786440 | tf_op jit(solution)/shard_map/ppermute | solution.py:572
  225.5 54.0 %all-to-all-start.3 = ((bf16[32,64,512]{2,1,0:T(8,128)(2,1)}), bf16[32,64,512]{2,1,0:T(8,128)(2,1)}, u32[]{:S(2)}, u32[]{:S(2)}) async-start(bf16[32,64,512]{2,1,0:T(8,128)(2,1)} %shard_map.223), calls=%async_computation.3 | async-start | bytes 4194304 | tf_op jit(solution)/shard_map/all_to_all | solution.py:583
  230.4 267.6 %all-gather.11.cloned.1.call-start = ((), (), s32[]{:S(2)}) async-start(), calls=%async_computation.10 | async-start | bytes 9437184 | tf_op jit(solution)/shard_map/all_gather | solution.py:586
  337.6 25.4 %collective-permute-start.16 = (bf16[256,2048]{1,0:T(8,128)(2,1)S(1)}, bf16[256,2048]{1,0:T(8,128)(2,1)S(1)}, u32[]{:S(2)}, u32[]{:S(2)}) collective-permute-start(bf16[256,2048]{1,0:T(8,128)(2,1)S(1)} %get-tuple-element.367), channel_id=1, source_target_pairs={{0,4},{1,5},{2,6},{3,7},{4,0},{5,1},{6,2},{7,3},{8,12},{9,13},{10,... | collective-permute-start | bytes 3145736 | tf_op jit(solution)/shard_map/ppermute | solution.py:572
  338.2 25.0 %collective-permute-start.17 = (bf16[256,2048]{1,0:T(8,128)(2,1)S(1)}, bf16[256,2048]{1,0:T(8,128)(2,1)S(1)}, u32[]{:S(2)}, u32[]{:S(2)}) collective-permute-start(bf16[256,2048]{1,0:T(8,128)(2,1)S(1)} %get-tuple-element.369), channel_id=1, source_target_pairs={{0,2},{1,3},{2,0},{3,1},{4,6},{5,7},{6,4},{7,5},{8,10},{9,11},{10,... | collective-permute-start | bytes 3145736 | tf_op jit(solution)/shard_map/ppermute | solution.py:572
  339.9 42.5 %collective-permute-start.20 = (bf16[224,2048]{1,0:T(8,128)(2,1)S(1)}, bf16[224,2048]{1,0:T(8,128)(2,1)S(1)}, u32[]{:S(2)}, u32[]{:S(2)}) collective-permute-start(bf16[224,2048]{1,0:T(8,128)(2,1)S(1)} %slice.68), channel_id=1, source_target_pairs={{0,16},{1,17},{2,18},{3,19},{4,20},{5,21},{6,22},{7,23},{8,24},{9,... | collective-permute-start | bytes 2752520 | tf_op jit(solution)/shard_map/ppermute | solution.py:577
  364.3 18.1 %collective-permute-start.18 = (bf16[128,2048]{1,0:T(8,128)(2,1)S(1)}, bf16[128,2048]{1,0:T(8,128)(2,1)S(1)}, u32[]{:S(2)}, u32[]{:S(2)}) collective-permute-start(bf16[128,2048]{1,0:T(8,128)(2,1)S(1)} %get-tuple-element.383), channel_id=1, source_target_pairs={{0,2},{1,3},{2,0},{3,1},{4,6},{5,7},{6,4},{7,5},{8,10},{9,11},{10,... | collective-permute-start | bytes 1572872 | tf_op jit(solution)/shard_map/ppermute | solution.py:572
  386.1 18.4 %collective-permute-start.25 = (bf16[64,2048]{1,0:T(8,128)(2,1)S(1)}, bf16[64,2048]{1,0:T(8,128)(2,1)S(1)}, u32[]{:S(2)}, u32[]{:S(2)}) collective-permute-start(bf16[64,2048]{1,0:T(8,128)(2,1)S(1)} %get-tuple-element.403), channel_id=1, source_target_pairs={{0,8},{1,9},{2,10},{3,11},{4,12},{5,13},{6,14},{7,15},{8,0},{9,1},... | collective-permute-start | bytes 786440 | tf_op jit(solution)/shard_map/ppermute | solution.py:572
  386.6 22.2 %collective-permute-start.26 = (bf16[64,2048]{1,0:T(8,128)(2,1)S(1)}, bf16[64,2048]{1,0:T(8,128)(2,1)S(1)}, u32[]{:S(2)}, u32[]{:S(2)}) collective-permute-start(bf16[64,2048]{1,0:T(8,128)(2,1)S(1)} %get-tuple-element.405), channel_id=1, source_target_pairs={{0,8},{1,9},{2,10},{3,11},{4,12},{5,13},{6,14},{7,15},{8,0},{9,1},... | collective-permute-start | bytes 786440 | tf_op jit(solution)/shard_map/ppermute | solution.py:572
  394.3 25.2 %collective-permute-start.27 = (bf16[256,2048]{1,0:T(8,128)(2,1)S(1)}, bf16[256,2048]{1,0:T(8,128)(2,1)S(1)}, u32[]{:S(2)}, u32[]{:S(2)}) collective-permute-start(bf16[256,2048]{1,0:T(8,128)(2,1)S(1)} %get-tuple-element.411), channel_id=1, source_target_pairs={{0,4},{1,5},{2,6},{3,7},{4,0},{5,1},{6,2},{7,3},{8,12},{9,13},{10,... | collective-permute-start | bytes 3145736 | tf_op jit(solution)/shard_map/ppermute | solution.py:572
  395.1 25.4 %collective-permute-start.28 = (bf16[256,2048]{1,0:T(8,128)(2,1)S(1)}, bf16[256,2048]{1,0:T(8,128)(2,1)S(1)}, u32[]{:S(2)}, u32[]{:S(2)}) collective-permute-start(bf16[256,2048]{1,0:T(8,128)(2,1)S(1)} %get-tuple-element.413), channel_id=1, source_target_pairs={{0,2},{1,3},{2,0},{3,1},{4,6},{5,7},{6,4},{7,5},{8,10},{9,11},{10,... | collective-permute-start | bytes 3145736 | tf_op jit(solution)/shard_map/ppermute | solution.py:572
  425.3 58.4 %all-to-all-start.4 = ((bf16[32,64,512]{2,1,0:T(8,128)(2,1)}), bf16[32,64,512]{2,1,0:T(8,128)(2,1)}, u32[]{:S(2)}, u32[]{:S(2)}) async-start(bf16[32,64,512]{2,1,0:T(8,128)(2,1)} %bitcast.60), calls=%async_computation.4 | async-start | bytes 4194304 | tf_op jit(solution)/shard_map/all_to_all | solution.py:583
  430.1 53.6 %collective-permute-start.29 = (bf16[32,2048]{1,0:T(8,128)(2,1)S(1)}, bf16[32,2048]{1,0:T(8,128)(2,1)S(1)}, u32[]{:S(2)}, u32[]{:S(2)}) collective-permute-start(bf16[32,2048]{1,0:T(8,128)(2,1)S(1)} %slice.69), channel_id=1, source_target_pairs={{0,16},{1,17},{2,18},{3,19},{4,20},{5,21},{6,22},{7,23},{8,24},{9,... | collective-permute-start | bytes 393224 | tf_op jit(solution)/shard_map/ppermute | solution.py:577
  498.0 55.0 %all-to-all-start.5 = ((bf16[32,64,512]{2,1,0:T(8,128)(2,1)}), bf16[32,64,512]{2,1,0:T(8,128)(2,1)S(1)}, u32[]{:S(2)}, u32[]{:S(2)}) async-start(bf16[32,64,512]{2,1,0:T(8,128)(2,1)} %bitcast.61), calls=%async_computation.5 | async-start | bytes 4194304 | tf_op jit(solution)/shard_map/all_to_all | solution.py:583
  502.3 38.3 %collective-permute-start.30 = (bf16[128,2048]{1,0:T(8,128)(2,1)}, bf16[128,2048]{1,0:T(8,128)(2,1)S(1)}, u32[]{:S(2)}, u32[]{:S(2)}) collective-permute-start(bf16[128,2048]{1,0:T(8,128)(2,1)} %copy-done.69), channel_id=1, source_target_pairs={{0,2},{1,3},{2,0},{3,1},{4,6},{5,7},{6,4},{7,5},{8,10},{9,11},{10,... | collective-permute-start | bytes 1572872 | tf_op jit(solution)/shard_map/ppermute | solution.py:572
  504.1 36.5 %collective-permute-start.31 = (bf16[128,2048]{1,0:T(8,128)(2,1)}, bf16[128,2048]{1,0:T(8,128)(2,1)S(1)}, u32[]{:S(2)}, u32[]{:S(2)}) collective-permute-start(bf16[128,2048]{1,0:T(8,128)(2,1)} %copy-done.68), channel_id=1, source_target_pairs={{0,4},{1,5},{2,6},{3,7},{4,0},{5,1},{6,2},{7,3},{8,12},{9,13},{10,... | collective-permute-start | bytes 1572872 | tf_op jit(solution)/shard_map/ppermute | solution.py:572
  553.1 65.0 %all-to-all-start.6 = ((bf16[32,64,384]{2,1,0:T(8,128)(2,1)}), bf16[32,64,384]{2,1,0:T(8,128)(2,1)}, u32[]{:S(2)}, u32[]{:S(2)}) async-start(bf16[32,64,384]{2,1,0:T(8,128)(2,1)} %bitcast.62), calls=%async_computation.6 | async-start | bytes 3145728 | tf_op jit(solution)/shard_map/all_to_all | solution.py:583
  565.1 35.5 %collective-permute-start.34 = (bf16[256,2048]{1,0:T(8,128)(2,1)S(1)}, bf16[256,2048]{1,0:T(8,128)(2,1)S(1)}, u32[]{:S(2)}, u32[]{:S(2)}) collective-permute-start(bf16[256,2048]{1,0:T(8,128)(2,1)S(1)} %get-tuple-element.461), channel_id=1, source_target_pairs={{0,4},{1,5},{2,6},{3,7},{4,0},{5,1},{6,2},{7,3},{8,12},{9,13},{10,... | collective-permute-start | bytes 3145736 | tf_op jit(solution)/shard_map/ppermute | solution.py:572
  567.1 33.6 %collective-permute-start.35 = (bf16[256,2048]{1,0:T(8,128)(2,1)S(1)}, bf16[256,2048]{1,0:T(8,128)(2,1)S(1)}, u32[]{:S(2)}, u32[]{:S(2)}) collective-permute-start(bf16[256,2048]{1,0:T(8,128)(2,1)S(1)} %get-tuple-element.463), channel_id=1, source_target_pairs={{0,2},{1,3},{2,0},{3,1},{4,6},{5,7},{6,4},{7,5},{8,10},{9,11},{10,... | collective-permute-start | bytes 3145736 | tf_op jit(solution)/shard_map/ppermute | solution.py:572
  573.5 22.8 %collective-permute-start.37 = (bf16[64,2048]{1,0:T(8,128)(2,1)S(1)}, bf16[64,2048]{1,0:T(8,128)(2,1)S(1)}, u32[]{:S(2)}, u32[]{:S(2)}) collective-permute-start(bf16[64,2048]{1,0:T(8,128)(2,1)S(1)} %get-tuple-element.471), channel_id=1, source_target_pairs={{0,8},{1,9},{2,10},{3,11},{4,12},{5,13},{6,14},{7,15},{8,0},{9,1},... | collective-permute-start | bytes 786440 | tf_op jit(solution)/shard_map/ppermute | solution.py:572
  607.6 25.5 %collective-permute-start.42 = (bf16[64,2048]{1,0:T(8,128)(2,1)}, bf16[64,2048]{1,0:T(8,128)(2,1)}, u32[]{:S(2)}, u32[]{:S(2)}) collective-permute-start(bf16[64,2048]{1,0:T(8,128)(2,1)} %convolution_convert_fusion.13), channel_id=1, source_target_pairs={{0,16},{1,17},{2,18},{3,19},{4,20},{5,21},{6,22},{7,23},{8,24},{9,... | collective-permute-start | bytes 786440 | tf_op jit(solution)/shard_map/ppermute | solution.py:577
  (114 other events, 1021.6 us)
Sparse Core Ops, SparseCore 0:
  23.9 67.9 all-gather.4
  93.7 71.9 all-gather.6
  225.6 73.1 all-gather.8
  425.5 72.5 all-gather.10
